TPU v7x, 512 devices: a whole 4x4x16 slice. The times are simulated.
512 devices in a mesh: seq: 64 (over z, y), head: 8 (over x, core).
Axes of the slice: x: 4, y: 4, z: 16, core: 2. Of those that a mesh axis runs over, the one named last changes fastest.
Arguments:
- grad_full: bfloat16 [65536, 8192], P('seq', 'head'), may hold values from -6 to 6
- keep: int32 [512, 16], P('seq'), may hold values from 0 to 127, as said below
- router_score: float32 [8192], P('seq'), may hold values from 0.2 to 1
- x_in: bfloat16 [8192, 8192], P('seq', 'head'), may hold values from -6 to 6
- z_in: bfloat16 [8192, 8192], P('seq', 'head'), may hold values from -6 to 6
- b_in: bfloat16 [8192, 128], P('seq'), may hold values from -4 to 4
- c_in: bfloat16 [8192, 128], P('seq'), may hold values from -4 to 4
- dt_raw: float32 [8192, 64], P('seq', 'head'), may hold values from -3 to 3
- dt_bias: float32 [64], P('head'), may hold values from -2.8 to -2.2
- a_log: float32 [64], P('head')
- d_skip: float32 [64], P('head'), may hold values from 0.5 to 1.5
- norm_gain: float32 [8192], P('head'), may hold values from 0.5 to 1.5
- state_in: float32 [64, 128, 128], P('head'), may hold values from -12 to 12
Outputs:
- grad_x: bfloat16 [8192, 8192], P('seq', 'head')
- grad_z: bfloat16 [8192, 8192], P('seq', 'head')
- grad_b: float32 [8192, 128], P('seq')
- grad_c: float32 [8192, 128], P('seq')
- grad_dt: float32 [8192, 64], P('seq', 'head')
- grad_router: float32 [8192], P('seq')
- grad_gain: float32 [8192], P('head')
- grad_alog: float32 [64], P('head')
- grad_skip: float32 [64], P('head')
Inputs may be any that keep to these rules, and one draw needn't show every extreme that they name: `keep`: each row lists 16 different positions of its routing block in increasing order.
All inputs are finite; a program needn't handle non-finite values.
Results may differ from a plain program's by a relative error of at most 0.002.
Values sent between devices are 32-bit elements; how exact they have to be, the bound alone decides.
No kernel may reach another device: no remote copies, remote signals or barrier semaphores. Data moves between devices by JAX's collectives and lax.ppermute only.
A program may use at most 128 MiB of HBM per device.

v0:
```python
import jax
import jax.numpy as jnp
from jax import lax
from jax.sharding import PartitionSpec as P

EPS = 1e-05
HIGH = lax.Precision.HIGHEST


def entering_2(part, axis, combine, identity, reverse):
    count = lax.axis_size(axis)
    place = lax.axis_index(axis)
    ahead = count - 1 - place if reverse else place
    gathered = jax.tree.map(lambda a: lax.all_gather(a, axis), part)
    state = jax.tree.map(lambda a, e: jnp.zeros_like(a) + jnp.asarray(e, a.dtype), part, identity)

    def one(lap, state):
        source = count - 1 - lap if reverse else lap
        return combine(
            state, jax.tree.map(lambda a: lax.dynamic_index_in_dim(a, source, 0, False), gathered)
        )

    return lax.fori_loop(0, ahead, one, state)


def step_logs(raw, bias, alog):
    step = jax.nn.softplus(raw + bias[None, :])
    rate = -jnp.exp(alog)
    logs = jnp.cumsum(step * rate[None, :], axis=0)
    return (step, logs)


def leaving_part(x_rows, b_rows, raw, bias, alog):
    step, logs = step_logs(raw, bias, alog)
    tail = jnp.exp(logs[-1][None, :] - logs) * step
    scaled_rows = tail[:, :, None] * x_rows
    own = jnp.einsum("thp,tn->hpn", scaled_rows, b_rows, precision=HIGH)
    return (jnp.exp(logs[-1]), own)


def output_part(x_rows, b_rows, c_rows, raw, bias, alog, skip, entering):
    step, logs = step_logs(raw, bias, alog)
    count = step.shape[0]
    lower = (jnp.arange(count)[:, None] >= jnp.arange(count)[None, :])[:, :, None]
    diff = logs[:, None, :] - logs[None, :, :]
    weights = jnp.where(lower, jnp.exp(jnp.where(lower, diff, 0.0)), 0.0)
    scores = jnp.dot(c_rows, b_rows.T, precision=HIGH)
    mixed = weights * scores[:, :, None] * step[None, :, :]
    inner = jnp.einsum("tsh,shp->thp", mixed, x_rows, precision=HIGH)
    carried = (
        jnp.einsum("hpn,tn->thp", entering, c_rows, precision=HIGH) * jnp.exp(logs)[:, :, None]
    )
    return inner + carried + skip[None, :, None] * x_rows


def forward_join(earlier, later):
    return (earlier[0] * later[0], later[0][:, None, None] * earlier[1] + later[1])


def backward_join(earlier, later):
    return (earlier[0] * later[0], later[1] + later[0][:, None, None] * earlier[1])


def shards(
    grad_full,
    keep,
    router_score,
    x_in,
    z_in,
    b_in,
    c_in,
    dt_raw,
    dt_bias,
    a_log,
    d_skip,
    norm_gain,
    state_in,
):
    count = x_in.shape[0]
    heads = dt_raw.shape[1]
    width = x_in.shape[1]
    per_head = width // heads
    total_width = width * lax.axis_size("head")
    block_len = grad_full.shape[0] // keep.shape[0]
    rows = (jnp.arange(keep.shape[0], dtype=jnp.int32)[:, None] * block_len + keep).reshape(-1)
    upstream = jnp.take(grad_full, rows, axis=0).astype(jnp.float32)
    x_rows = x_in.astype(jnp.float32).reshape(count, heads, per_head)
    z_rows = z_in.astype(jnp.float32)
    b_rows = b_in.astype(jnp.float32)
    c_rows = c_in.astype(jnp.float32)
    (decay, own_state), leave_back = jax.vjp(leaving_part, x_rows, b_rows, dt_raw, dt_bias, a_log)
    empty_state = jnp.zeros_like(state_in)
    prior = entering_2(
        (decay, own_state), "seq", forward_join, (jnp.ones_like(decay), empty_state), False
    )
    entering = prior[1] + prior[0][:, None, None] * state_in
    y_rows, out_back = jax.vjp(
        output_part, x_rows, b_rows, c_rows, dt_raw, dt_bias, a_log, d_skip, entering
    )
    y_all = y_rows.reshape(count, width)
    sig = jax.nn.sigmoid(z_rows)
    gate = z_rows * sig
    gated = y_all * gate
    squares = lax.psum(jnp.sum(gated * gated, axis=1), "head")
    rstd = lax.rsqrt(squares / total_width + EPS)[:, None]
    normed = gated * rstd
    scaled = upstream * router_score[:, None]
    weighted = scaled * norm_gain[None, :]
    router_grad, projection = lax.psum(
        (
            jnp.sum(upstream * normed * norm_gain[None, :], axis=1),
            jnp.sum(weighted * gated, axis=1),
        ),
        "head",
    )
    grad_gated = rstd * weighted - gated * rstd * rstd * rstd * (projection / total_width)[:, None]
    grad_z = (grad_gated * y_all * sig * (1.0 + z_rows * (1.0 - sig))).astype(jnp.bfloat16)
    grad_y = (grad_gated * gate).reshape(count, heads, per_head)
    gain_part = jnp.sum(scaled * normed, axis=0)
    gx1, gb1, gc1, graw1, _, galog1, gskip1, own_grad = out_back(grad_y)
    later = entering_2(
        (decay, own_grad), "seq", backward_join, (jnp.ones_like(decay), empty_state), True
    )
    decay_grad = jnp.sum(later[1] * entering, axis=(1, 2))
    gx2, gb2, graw2, _, galog2 = leave_back((decay_grad, later[1]))
    grad_b, grad_c = lax.psum((gb1 + gb2, gc1), "head")
    grad_gain, grad_alog, grad_skip = lax.psum((gain_part, galog1 + galog2, gskip1), "seq")
    grad_x = (gx1 + gx2).reshape(count, width).astype(jnp.bfloat16)
    return (
        grad_x,
        grad_z,
        grad_b,
        grad_c,
        graw1 + graw2,
        router_grad,
        grad_gain,
        grad_alog,
        grad_skip,
    )


def solution(mesh):
    in_specs = (
        P("seq", "head"),
        P("seq", None),
        P("seq"),
        P("seq", "head"),
        P("seq", "head"),
        P("seq", None),
        P("seq", None),
        P("seq", "head"),
        P("head"),
        P("head"),
        P("head"),
        P("head"),
        P("head", None, None),
    )
    out_specs = (
        P("seq", "head"),
        P("seq", "head"),
        P("seq", None),
        P("seq", None),
        P("seq", "head"),
        P("seq"),
        P("head"),
        P("head"),
        P("head"),
    )
    return jax.shard_map(shards, mesh=mesh, in_specs=in_specs, out_specs=out_specs, check_vma=False)
```

profile of v0, /device:TPU:8, one launch (start us, length us, event | category | flops | bytes accessed | tf_op | source)
XLA Modules:
  0.0 1084.7 jit_solution(5528619131554867958)
XLA Ops:
  11.6 2.0 fusion.29
  17.5 84.4 %all-gather.2 = f32[64,1,8]{2,1,0:T(1,128)} all-gather(f32[1,1,8]{2,1,0:T(1,128)S(1)} %get-tuple-element.216), channel_id=1, replica_groups=mesh['seq'=64,'head'=8] {'seq'}, dimensions={0}, use_global_device_ids=true | all-gather | bytes 2080 | tf_op jit(solution)/shard_map/all_gather | solution.py:14
  102.5 1.6 fusion.73
  104.0 207.3 %all-gather.6.cloned.1.call-done = f32[512,128,128]{2,1,0:T(8,128)} async-done(((f32[8,128,128]{2,1,0:T(8,128)}), f32[512,128,128]{2,1,0:T(8,128)}) %all-gather.6.cloned.1.call-update) | async-done | bytes 33554448 | tf_op jit(solution)/shard_map/all_gather | solution.py:14
  311.9 2.4 while.26
  317.5 2.9 fusion.3
  321.6 2.4 multiply_reduce_fusion.6
  324.0 14.7 %psum.56 = f32[128]{0:T(128)} all-reduce(f32[128]{0:T(128)} %get-tuple-element.205), channel_id=1, replica_groups=mesh['seq'=64,'head'=8] {'head'}, use_global_device_ids=true, to_apply=%region_4.6 | all-reduce | flops 128 | bytes 1024 | tf_op jit(solution)/shard_map/psum | solution.py:104
  339.9 2.0 fusion.13
  342.0 13.0 %all-reduce.3 = (f32[128]{0:T(128)}, f32[128]{0:T(128)}) all-reduce(f32[128]{0:T(128)} %get-tuple-element.162, f32[128]{0:T(128)} %get-tuple-element.161), channel_id=1, replica_groups=mesh['seq'=64,'head'=8] {'head'}, use_global_device_ids=true, to_apply=%region_6.8 | all-reduce | flops 256 | bytes 2048 | tf_op jit(solution)/shard_map/psum | solution.py:109
  355.7 3.2 multiply_reduce_fusion
  360.1 1.9 fusion.26
  363.9 2.5 fusion.31
  368.5 2.1 convolution_bitcast_fusion.5
  370.6 1.6 convolution_add_fusion
  372.1 422.0 %all-gather.8.cloned.1.call-done = f32[512,128,128]{2,1,0:T(8,128)} async-done(((f32[8,128,128]{2,1,0:T(8,128)}), f32[512,128,128]{2,1,0:T(8,128)}) %all-gather.8.cloned.1.call-update) | async-done | bytes 33554448 | tf_op jit(solution)/shard_map/all_gather | solution.py:14
  794.2 117.6 %while.27 = (s32[]{:T(128)}, f32[8,128,128]{2,1,0:T(8,128)S(1)}, s32[]{:T(128)}, f32[64,8,128,128]{3,2,1,0:T(8,128)}, f32[64,8]{1,0:T(8,128)}, /*index=5*/s32[]{:T(128)}, s32[]{:T(128)}, s32[]{:T(128)}, s32[]{:T(128)}) while((s32[]{:T(128)}, f32[8,128,128]{2,1,0:T(8,128)S(1)}, s32[]{:T(128)}, f32[64,8,128,128]{3,2,1,0:T(8,128)}, ...), condition=%wide.region_8.10_spmd, body=%wide.region_7.9_spmd.sunk | while | flops 262150 | bytes 1573115 | solution.py:23
  913.0 2.0 convolution_bitcast_fusion.6
  915.0 2.8 multiply_reduce_fusion.2
  917.9 1.6 convolution_add_fusion.1
  919.5 2.0 fusion.4
  931.0 144.2 %all-reduce.2 = (f32[1024]{0:T(1024)}, f32[8]{0:T(128)}, f32[8]{0:T(128)}) all-reduce(f32[1024]{0:T(1024)} %get-tuple-element.163, f32[8]{0:T(128)S(1)} %add_multiply_fusion, f32[8]{0:T(128)} %bitcast_reduce_fusion), channel_id=1, replica_groups=mesh['seq'=64,'head'=8] {'seq'}, use_global_device_ids=true, to_apply=%region_24.26 | all-reduce | flops 1040 | bytes 8320 | tf_op jit(solution)/shard_map/psum | solution.py:127
  1075.2 1.5 copy.127
  1076.7 1.5 copy.128
  (202 shorter events, 149.8 us)
Async XLA Ops:
  7.2 9.4 copy-start
  7.2 304.2 %all-gather.6.cloned.1.call-start = ((), (), s32[]{:S(2)}) async-start(), calls=%async_computation | async-start | bytes 34078720 | tf_op jit(solution)/shard_map/all_gather | solution.py:14
  8.0 2.4 copy-start.5
  9.7 0.7 copy-start.6
  10.5 300.8 %copy-start.4 = (f32[128,8]{0,1:T(8,128)}, f32[128,8]{0,1:T(8,128)S(1)}, u32[]{:S(2)}) copy-start(f32[128,8]{0,1:T(8,128)S(1)} %copy.71) | copy-start | bytes 12292
  11.6 782.5 %copy-start.1 = (f32[128,1024]{0,1:T(8,128)}, f32[128,1024]{0,1:T(8,128)S(1)}, u32[]{:S(2)}) copy-start(f32[128,1024]{0,1:T(8,128)S(1)} %copy.72) | copy-start | bytes 1572868
  13.6 780.5 %all-gather.8.cloned.1.call-start = ((), (), s32[]{:S(2)}) async-start(), calls=%async_computation.1 | async-start | bytes 34078720 | tf_op jit(solution)/shard_map/all_gather | solution.py:14
  315.5 0.8 copy-start.2
  317.4 2.9 copy-start.3
  339.3 0.6 copy-start.7
  362.1 713.1 %all-reduce.7.cloned.1.call-start = ((), (), s32[]{:S(2)}) async-start(), calls=%async_computation.2 | async-start | bytes 262144 | tf_op jit(solution)/shard_map/psum | solution.py:126
Sparse Core Ops, SparseCore 0:
  13.8 297.5 all-gather.5
  362.2 431.9 all-gather.7
  928.9 66.3 all-reduce.6
where the time goes:
time: 1090 us; the launch traced here: 1080 us
  waiting for transfers between devices  629 us (58%)
  blocking collectives  256 us (23%)
  other arithmetic  100 us (9%)
  local copies, waits for them, and re-layouts  59.1 us (5%)
  matrix products  24 us (2%)
  between operations  13.9 us (1%)
    all_gather x2, waiting for transfers between devices, entering_2(): gathered = jax.tree.map(lambda a: lax.all_gather(a, axis), part)  629 us
    psum x1, blocking collectives, shards(): lax.psum((gain_part, galog1 + galog2, gskip1), 'seq')  144 us
    all_gather x1, blocking collectives, entering_2(): gathered = jax.tree.map(lambda a: lax.all_gather(a, axis), part)  84.4 us
    add x62, other arithmetic, backward_join(): later[1] + later[0][:, None, None] * earlier[1]  73.4 us
    mul x62, local copies, waits for them, and re-layouts, backward_join(): later[0][:, None, None] * earlier[1]  42.6 us
  transfers between devices with their start and end apart: 3, of which 2 were waited for; matrix products, arithmetic and copies ran while one was open for 2% of the time, Pallas kernels for 0%

commit v1 on v0

v1 whole, which is shorter than its diff:
```python
import functools

import jax
import jax.numpy as jnp
import numpy as np
from jax import lax
from jax.experimental import pallas as pl
from jax.experimental.pallas import tpu as pltpu
from jax.sharding import Mesh
from jax.sharding import PartitionSpec as P

EPS = 1e-05
GROUP = 4
CHUNK = 128
HP = 2
PC = 128
NS = 128
WIDE = HP * PC
F32 = jnp.float32
BF16 = jnp.bfloat16
NN = ((1,), (0,))
NT = ((1,), (1,))

X_B, X_C, X_S, ROWS_X = CHUNK, CHUNK + CHUNK // 2, 2 * CHUNK, 2 * CHUNK + 8
ROWS_Y = CHUNK + 8
HOME_S, HOME_B, HOME_C = CHUNK, CHUNK + 8, CHUNK + 8 + CHUNK // 2
ROWS_HOME = 2 * CHUNK + 8

VMEM = pl.BlockSpec(memory_space=pltpu.VMEM)
SMEM = pl.BlockSpec(memory_space=pltpu.SMEM)
ANY = pl.BlockSpec(memory_space=pl.ANY)
LIMIT = 24 * 2**20
FULL = 56 * 2**20


def mm(a, b, dims=NN):
    return lax.dot_general(a, b, (dims, ((), ())), preferred_element_type=F32)


def split(a):
    high = a.astype(BF16)
    return high, (a - high.astype(F32)).astype(BF16)


def mm_left(a, exact, dims=NN):
    high, low = split(a)
    return mm(high, exact, dims) + mm(low, exact, dims)


def mm_right(exact, b, dims=NN):
    high, low = split(b)
    return mm(exact, high, dims) + mm(exact, low, dims)


def mm_both(a, b, dims=NN):
    ah, al = split(a)
    bh, bl = split(b)
    return mm(ah, bh, dims) + (mm(ah, bl, dims) + mm(al, bh, dims))


def iota(shape, dim):
    return lax.broadcasted_iota(jnp.int32, shape, dim)


def softplus(v):
    return jnp.maximum(v, 0.0) + jnp.log1p(jnp.exp(-jnp.abs(v)))


def sigmoid(v):
    return 1.0 / (1.0 + jnp.exp(-v))


def own_heads():
    return lax.axis_index("y") * HP


def two_rows(x, row):
    odd = iota((GROUP * HP, PC), 0) % HP == 1
    at = slice(X_S + row, X_S + row + 1)
    return jnp.where(odd, x[0, at, PC:], x[0, at, :PC])


def halves(ref, k, at, count=CHUNK):
    return jnp.concatenate([ref[k, at : at + count // 2, :PC], ref[k, at : at + count // 2, PC:]], axis=0)


def token_rows(x):
    raw = jnp.concatenate(
        [x[k, X_S : X_S + 1, h * PC : (h + 1) * PC] for k in range(GROUP) for h in range(HP)], axis=0
    )
    raw = raw + two_rows(x, 1)
    step = softplus(raw)
    rate = -jnp.exp(two_rows(x, 2))
    la = step * rate
    upper = (iota((CHUNK, CHUNK), 0) <= iota((CHUNK, CHUNK), 1)).astype(F32)
    logs = jnp.dot(la, upper, precision=lax.Precision.HIGHEST, preferred_element_type=F32)
    return raw, step, rate, la, logs, logs[:, CHUNK - 1 :]


def columns(*rows):
    count = sum(r.shape[0] for r in rows)
    return jnp.concatenate(rows + (jnp.zeros((CHUNK - count, CHUNK), F32),), axis=0).T


def rows_of(cols):
    pad = jnp.zeros((CHUNK, CHUNK - len(cols)), F32)
    return jnp.concatenate(list(cols) + [pad], axis=1).T[: len(cols)]


def pair(a, b, rows):
    return jnp.concatenate(
        [jnp.broadcast_to(a, (rows, PC)), jnp.broadcast_to(b, (rows, PC))], axis=1
    )


def lanes_of(values):
    return [pair(values[k * HP : k * HP + 1], values[k * HP + 1 : k * HP + 2], 1) for k in range(GROUP)]


def pair_cols(cols, k, at=0):
    c = at + k * HP
    return pair(cols[:, c : c + 1], cols[:, c + 1 : c + 2], CHUNK)


def head_sums(a):
    return [jnp.sum(a[:, h * PC : (h + 1) * PC], axis=1, keepdims=True) for h in range(HP)]


def pack_body(x_hbm, b_hbm, c_hbm, dt_hbm, bias_hbm, alog_hbm, skip_hbm, xs, x, b, c, dt_t, bias, alog, skip, sem):
    copies = [
        pltpu.make_async_copy(src, dst, sem.at[i])
        for i, (src, dst) in enumerate(
            [(x_hbm, x), (b_hbm, b), (c_hbm, c), (dt_hbm, dt_t), (bias_hbm, bias), (alog_hbm, alog), (skip_hbm, skip)]
        )
    ]
    for copy in copies:
        copy.start()
    for copy in copies:
        copy.wait()
    half = CHUNK // 2
    odd = iota((1, WIDE), 1) >= PC
    for q in range(GROUP):
        xs[q, :CHUNK, :] = x[:, q * WIDE : (q + 1) * WIDE].astype(F32)
        for at, ref in ((X_B, b), (X_C, c)):
            xs[q, at : at + half, :PC] = ref[:half].astype(F32)
            xs[q, at : at + half, PC:] = ref[half:].astype(F32)
        row = q * HP
        tile = [jnp.concatenate([dt_t[row : row + 1, :], dt_t[row + 1 : row + 2, :]], axis=1)]
        tile += [jnp.where(odd, ref[row + 1], ref[row]) for ref in (bias, alog, skip)]
        tile += [jnp.zeros((4, WIDE), F32)]
        xs[q, X_S:, :] = jnp.concatenate(tile, axis=0)


def upstream_body(block_len, after, grad_full, keep, out):
    blocks, kept = keep.shape
    for i in range(blocks):
        pick = (iota((kept, block_len), 1) == keep[i : i + 1, :].T).astype(BF16)
        out[i * kept : (i + 1) * kept, :] = mm(pick, grad_full[i * block_len : (i + 1) * block_len, :])


def to_slices(out, at, state, rows):
    for lap in range(NS // rows):
        for h in range(HP):
            out[lap, at + h * rows : at + (h + 1) * rows, :] = state[
                lap * rows : (lap + 1) * rows, h * PC : (h + 1) * PC
            ]


def from_slices(ref, rows):
    return jnp.concatenate(
        [ref[:, h * rows : (h + 1) * rows, :].reshape(NS, PC) for h in range(HP)], axis=1
    )


def group_log(total):
    out = total[:HP]
    for k in range(1, GROUP):
        out = out + total[k * HP : (k + 1) * HP]
    return out


def own_state_body(rows, x, part, send):
    _, step, _, _, logs, total = token_rows(x)
    cols = columns(jnp.exp(total - logs) * step)
    decay = lanes_of(jnp.exp(total))
    state = jnp.zeros((NS, WIDE), F32)
    for k in range(GROUP):
        b_t = halves(x, k, X_B).T.astype(BF16)
        state = decay[k] * state + mm_right(b_t, x[k, :CHUNK, :] * pair_cols(cols, k))
        part[k] = state
    to_slices(send, 0, state, rows)
    whole = jnp.exp(group_log(total))
    extra = jnp.where(iota((8, PC), 0) == 0, whole[:1], whole[1:])
    for lap in range(NS // rows):
        send[lap, HP * rows :, :] = extra


def scan_body(rows, got, first, out, decay):
    state = [first[h * rows : (h + 1) * rows, :] for h in range(HP)]
    for lap in range(got.shape[0]):
        for h in range(HP):
            at = slice(h * rows, (h + 1) * rows)
            out[lap, at, :] = state[h]
            state[h] = got[lap, HP * rows + h : HP * rows + h + 1, :] * state[h] + got[lap, at, :]
        decay[lap] = got[lap, HP * rows :, :]


def scan_back_body(rows, got, decay, out, done):
    laps = got.shape[0]
    wide = HP * rows
    state = [jnp.zeros((rows, PC), F32) for _ in range(HP)]
    cross = [jnp.zeros((rows, PC), F32) for _ in range(HP)]
    total = jnp.zeros((8, PC), F32)
    for lap in reversed(range(laps)):
        for h in range(HP):
            at = slice(h * rows, (h + 1) * rows)
            out[lap, at, :] = state[h]
            cross[h] = cross[h] + state[h] * got[lap, wide + h * rows : wide + (h + 1) * rows, :]
            state[h] = decay[lap, h : h + 1, :] * state[h] + got[lap, at, :]
        total = total + got[lap, 2 * wide :, :]
    done[...] = total
    row = iota((8, PC), 0)
    extra = jnp.zeros((8, PC), F32)
    for h in range(HP):
        extra = extra + jnp.where(row == h, jnp.sum(cross[h], axis=0, keepdims=True), 0.0)
    for lap in range(laps):
        out[lap, wide:, :] = extra


def first_body(rows, after, state_in, out, flat):
    base = own_heads()
    for h in range(HP):
        flat[...] = state_in[base + h].T
        out[h * rows : (h + 1) * rows, :] = flat[
            pl.ds(pl.multiple_of(lax.axis_index("z") * rows, rows), rows), :
        ]


def group_states(part, enter, total):
    out, log = [enter], jnp.zeros((HP, 1), F32)
    for k in range(GROUP):
        log = log + total[k * HP : (k + 1) * HP]
        out.append(part[k] + pair(jnp.exp(log[:1]), jnp.exp(log[1:]), 1) * enter)
    return out


def rest_logs(total):
    out, log = [None] * GROUP, jnp.zeros((HP, 1), F32)
    for k in reversed(range(GROUP)):
        out[k] = log
        log = log + total[k * HP : (k + 1) * HP]
    return jnp.concatenate(out, axis=0)


def decays(logs, cols, k, h, lower):
    r = k * HP + h
    diff = cols[:, r : r + 1] - logs[r : r + 1]
    return jnp.where(lower, jnp.exp(jnp.where(lower, diff, 0.0)), 0.0)


def output_body(rows, x, part, got, y_out):
    _, step, _, _, logs, total = token_rows(x)
    cols = columns(logs, jnp.exp(logs))
    lower = iota((CHUNK, CHUNK), 0) >= iota((CHUNK, CHUNK), 1)
    states = group_states(part, from_slices(got, rows), total)
    d = x[0, X_S + 3 : X_S + 4, :]
    for k in range(GROUP):
        b = halves(x, k, X_B).astype(BF16)
        c = halves(x, k, X_C).astype(BF16)
        xk = x[k, :CHUNK, :]
        scores = mm(c, b, NT)
        inner = []
        for h in range(HP):
            r = k * HP + h
            mixed = decays(logs, cols, k, h, lower) * scores * step[r : r + 1]
            inner.append(mm_left(mixed, xk[:, h * PC : (h + 1) * PC].astype(BF16)))
        carried = mm_right(c, states[k]) * pair_cols(cols, k, GROUP * HP)
        y_out[k] = jnp.concatenate(inner, axis=1) + carried + d * xk


def norm_body(y, z, up, gain, stats):
    squares = jnp.zeros((CHUNK, 1), F32)
    crosses = jnp.zeros((CHUNK, 1), F32)
    for q in range(GROUP):
        at = slice(q * WIDE, (q + 1) * WIDE)
        zq = z[:, at].astype(F32)
        gated = y[q] * zq * sigmoid(zq)
        squares = squares + jnp.sum(gated * gated, axis=1, keepdims=True)
        crosses = crosses + jnp.sum(up[:, at] * gated * gain[:, at], axis=1, keepdims=True)
    both = rows_of([squares, crosses])
    tile = jnp.concatenate([both, jnp.zeros((6, CHUNK), F32)], axis=0)
    stats[...] = jnp.broadcast_to(tile[None], stats.shape)


def norm_back_body(total_width, stats, y, z, up, gain, router, gz, gy, router_grad):
    sums = stats[0, :2, :]
    for q in range(1, stats.shape[0]):
        sums = sums + stats[q, :2, :]
    rstd = lax.rsqrt(sums[:1] / total_width + EPS)
    cross = sums[1:]
    router_grad[...] = rstd * cross
    cols = columns(rstd * router[...], rstd * rstd * rstd * (router[...] * cross / total_width))
    for q in range(GROUP):
        at = slice(q * WIDE, (q + 1) * WIDE)
        zq = z[:, at].astype(F32)
        sig = sigmoid(zq)
        gate = zq * sig
        gated = y[q] * gate
        scaled = cols[:, :1] * up[:, at]
        gg = scaled * gain[:, at] - gated * cols[:, 1:2]
        gz[:, at] = (gg * y[q] * sig * (1.0 + zq * (1.0 - sig))).astype(BF16)
        gy[q, :CHUNK, :] = gg * gate
        gy[q, CHUNK:, :] = jnp.broadcast_to(jnp.sum(scaled * gated, axis=0, keepdims=True), (8, WIDE))


def sum_body(got, out):
    total = got[0]
    for q in range(1, got.shape[0]):
        total = total + got[q]
    out[...] = jnp.broadcast_to(total[None], out.shape)


def tangent_body(rows, after, x, part, got, out):
    _, step, _, _, logs, total = token_rows(x)
    rest = rest_logs(total)
    cols = columns(jnp.exp(total - logs + rest) * step * logs)
    near = lanes_of(jnp.exp(rest) * total)
    states = group_states(part, from_slices(got, rows), total)
    tangent = jnp.zeros((NS, WIDE), F32)
    for k in range(GROUP):
        b_t = halves(x, k, X_B).T.astype(BF16)
        scaled = x[k, :CHUNK, :] * pair_cols(cols, k)
        tangent = tangent + near[k] * states[k + 1] - mm_right(b_t, scaled)
    to_slices(out, 0, tangent, rows)


def output_back_body(rows, x, gy_in, y_in, part, got, tangent, gx_out, db_out, dc_out, send, small):
    raw, step, rate, la, logs, total = token_rows(x)
    cols = columns(logs, jnp.exp(logs), jnp.exp(total - logs), step)
    n = GROUP * HP
    lower = iota((CHUNK, CHUNK), 0) >= iota((CHUNK, CHUNK), 1)
    upper = iota((CHUNK, CHUNK), 0) <= iota((CHUNK, CHUNK), 1)
    states = group_states(part, from_slices(got, rows), total)
    d = x[0, X_S + 3 : X_S + 4, :]
    decay = lanes_of(jnp.exp(total))
    gain_part = jnp.zeros((1, WIDE), F32)
    skip_part = jnp.zeros((1, WIDE), F32)
    dots, xv, ends = [None] * n, [None] * n, [None] * n
    own = jnp.zeros((NS, WIDE), F32)
    for k in reversed(range(GROUP)):
        b = halves(x, k, X_B).astype(BF16)
        c32 = halves(x, k, X_C)
        c = c32.astype(BF16)
        xk, y, gy = x[k, :CHUNK, :], y_in[k], gy_in[k, :CHUNK, :]
        gain_part = gain_part + gy_in[k, CHUNK : CHUNK + 1, :]
        skip_part = skip_part + jnp.sum(gy * xk, axis=0, keepdims=True)
        dots[k * HP : (k + 1) * HP] = head_sums(gy * (y - d * xk))
        scores_t = mm(b, c, NT)
        dscores = jnp.zeros((CHUNK, CHUNK), F32)
        inner = []
        for h in range(HP):
            r = k * HP + h
            sl = slice(h * PC, (h + 1) * PC)
            gh, gl = split(gy[:, sl])
            xh = xk[:, sl].astype(BF16)
            dmixed = mm(gh, xh, NT) + mm(gl, xh, NT)
            dscores = dscores + decays(logs, cols, k, h, lower) * dmixed * step[r : r + 1]
            diff = logs[r : r + 1] - cols[:, r : r + 1]
            mixed_t = jnp.where(upper, jnp.exp(jnp.where(upper, diff, 0.0)), 0.0) * scores_t
            mh, ml = split(mixed_t)
            inner.append(mm(mh, gh) + (mm(mh, gl) + mm(ml, gh)))
        tail = pair_cols(cols, k, 2 * n)
        stepc = pair_cols(cols, k, 3 * n)
        oh, ol = split(own)
        v = jnp.concatenate(inner, axis=1) + tail * (mm(b, oh) + mm(b, ol))
        gx_out[k] = stepc * v + d * gy
        xv[k * HP : (k + 1) * HP] = head_sums(xk * v)
        ends[k * HP : (k + 1) * HP] = [
            jnp.sum(e, axis=0, keepdims=True) for e in head_sums(own * states[k + 1])
        ]
        sh, sl = split(tail * stepc * xk)
        db_out[k] = mm_left(dscores.T, c) + (mm(sh, oh, NT) + (mm(sh, ol, NT) + mm(sl, oh, NT)))
        eg = pair_cols(cols, k, n) * gy
        dc_out[k] = mm_left(dscores, b) + mm_both(eg, states[k], NT)
        own = decay[k] * own + mm_right(c32.T.astype(BF16), eg)
    xv = rows_of(xv)
    after = (iota((CHUNK, CHUNK), 0) >= iota((CHUNK, CHUNK), 1)).astype(F32)
    dla = jnp.dot(rows_of(dots) - step * xv, after, precision=lax.Precision.HIGHEST, preferred_element_type=F32)
    dla = dla + jnp.concatenate(ends, axis=0)
    small[:n] = dla
    small[n:] = xv
    to_slices(send, 0, own, rows)
    send[:, HP * rows : 2 * HP * rows, :] = tangent[...]
    decayed = dla * la
    odd = iota((n, 1), 0) % HP
    extra = jnp.concatenate(
        [gain_part[:, :PC], gain_part[:, PC:], skip_part[:, :PC], skip_part[:, PC:]]
        + [jnp.sum(jnp.where(odd == h, decayed, 0.0), axis=0, keepdims=True) for h in range(HP)]
        + [jnp.zeros((2, PC), F32)], axis=0,
    )
    for lap in range(NS // rows):
        send[lap, 2 * HP * rows :, :] = extra


def input_back_body(rows, x, gx_in, part, got, late, done, small, db_in, dc_in, home):
    raw, step, rate, la, logs, total = token_rows(x)
    n = GROUP * HP
    rest = rest_logs(total)
    cols = columns(jnp.exp(total - logs + rest), step)
    states = group_states(part, from_slices(got, rows), total)
    reach = lanes_of(jnp.exp(rest))
    grad = from_slices(late, rows)
    gh, gl = split(grad)
    ends, xv = [], []
    half = CHUNK // 2
    for k in range(GROUP):
        b = halves(x, k, X_B).astype(BF16)
        xk = x[k, :CHUNK, :]
        tail = pair_cols(cols, k)
        stepc = pair_cols(cols, k, n)
        v = tail * (mm(b, gh) + mm(b, gl))
        home[k, :CHUNK, :] = gx_in[k] + stepc * v
        sh, sl = split(tail * stepc * xk)
        db = db_in[k] + (mm(sh, gh, NT) + (mm(sh, gl, NT) + mm(sl, gh, NT)))
        for at, grad_map in ((HOME_B, db), (HOME_C, dc_in[k])):
            home[k, at : at + half, :PC] = grad_map[:half]
            home[k, at : at + half, PC:] = grad_map[half:]
        xv += head_sums(xk * v)
        ends += [jnp.sum(e, axis=0, keepdims=True) for e in head_sums(reach[k] * grad * states[k + 1])]
    xv = rows_of(xv)
    after = (iota((CHUNK, CHUNK), 0) >= iota((CHUNK, CHUNK), 1)).astype(F32)
    dla = jnp.dot(-step * xv, after, precision=lax.Precision.HIGHEST, preferred_element_type=F32)
    dla = small[:n] + dla + jnp.concatenate(ends, axis=0)
    ddt = (dla * rate + small[n:] + xv) * sigmoid(raw)
    alog_rows = done[4:6, :]
    for lap in range(late.shape[0]):
        alog_rows = alog_rows + late[lap, HP * rows : HP * rows + HP, :]
    shared = jnp.concatenate(
        [jnp.concatenate([done[i : i + 1, :], done[i + 1 : i + 2, :]], axis=1) for i in (0, 2)]
        + [jnp.concatenate([alog_rows[:1], alog_rows[1:]], axis=1), jnp.zeros((4, WIDE), F32)], axis=0,
    )
    for k in range(GROUP):
        own = jnp.concatenate([ddt[k * HP : k * HP + 1], ddt[k * HP + 1 : k * HP + 2]], axis=1)
        home[k, HOME_S:HOME_B, :] = jnp.concatenate([own, shared], axis=0)


def summed(block, lo, hi):
    got = block[0, lo:hi, :]
    for q in range(1, GROUP):
        got = got + block[q, lo:hi, :]
    return got


def home_body(block, gx, ddt, gain, alog, skip, send):
    lane = iota((1, GROUP * HP), 1)
    a = jnp.zeros((1, GROUP * HP), F32)
    s = jnp.zeros((1, GROUP * HP), F32)
    for q in range(GROUP):
        gx[:, q * WIDE : (q + 1) * WIDE] = block[q, :CHUNK, :].astype(BF16)
        gain[:, q * WIDE : (q + 1) * WIDE] = block[q, HOME_S + 1 : HOME_S + 2, :]
        for h in range(HP):
            sl = slice(h * PC, (h + 1) * PC)
            ddt[q * HP + h : q * HP + h + 1, :] = block[q, HOME_S : HOME_S + 1, sl]
            here = lane == q * HP + h
            s = s + jnp.where(here, jnp.sum(block[q, HOME_S + 2 : HOME_S + 3, sl], axis=1, keepdims=True), 0.0)
            a = a + jnp.where(here, jnp.sum(block[q, HOME_S + 3 : HOME_S + 4, sl], axis=1, keepdims=True), 0.0)
    alog[...] = a
    skip[...] = s
    ranks = send.shape[0]
    rows = CHUNK // ranks
    for i, at in enumerate((HOME_B, HOME_C)):
        got = summed(block, at, at + CHUNK // 2)
        both = jnp.concatenate([got[:, :PC], got[:, PC:]], axis=0)
        for j in range(ranks):
            send[j, i * rows : (i + 1) * rows, :] = both[j * rows : (j + 1) * rows]


def maps_body(got, db, dc):
    ranks = got.shape[0]
    rows = CHUNK // ranks
    for i in range(ranks):
        db[i * rows : (i + 1) * rows, :] = got[i, :rows, :]
        dc[i * rows : (i + 1) * rows, :] = got[i, rows:, :]


def call(body, ins, outs, scratch=(), limit=LIMIT):
    out = pl.pallas_call(
        body,
        in_specs=ins,
        out_specs=[VMEM] * len(outs),
        out_shape=[jax.ShapeDtypeStruct(s, t) for s, t in outs],
        scratch_shapes=scratch,
        compiler_params=pltpu.CompilerParams(vmem_limit_bytes=limit),
    )
    return out


def swap(a, axis):
    return lax.all_to_all(a, axis, 0, 0, tiled=True)


def shards(
    grad_full, keep, router_score, x_in, z_in, b_in, c_in, dt_raw, dt_bias, a_log, d_skip, norm_gain, state_in,
):
    laps = lax.axis_size("z")
    ranks = lax.axis_size("head")
    heads = dt_raw.shape[1]
    width = x_in.shape[1]
    total_width = width * ranks
    block_len = grad_full.shape[0] // keep.shape[0]
    big = ((GROUP, CHUNK, WIDE), F32)
    states = ((GROUP, NS, WIDE), F32)
    rows = NS // laps
    wide = HP * rows
    bind = functools.partial
    dma = pltpu.SemaphoreType.DMA

    router = router_score.reshape(1, CHUNK)
    gain = norm_gain.reshape(1, width)
    (xs,) = call(
        pack_body, [ANY] * 7, [((GROUP, ROWS_X, WIDE), F32)],
        [
            pltpu.VMEM((CHUNK, width), BF16), pltpu.VMEM((CHUNK, NS), BF16), pltpu.VMEM((CHUNK, NS), BF16),
            pltpu.VMEM((heads, CHUNK), F32), pltpu.SMEM((heads,), F32), pltpu.SMEM((heads,), F32),
            pltpu.SMEM((heads,), F32), dma((7,)),
        ], FULL,
    )(x_in, b_in, c_in, dt_raw.T, dt_bias, a_log, d_skip)
    x = swap(xs, "y")
    (up,) = call(bind(upstream_body, block_len), [ANY] + [VMEM] * 2, [((CHUNK, width), F32)])(xs, grad_full, keep)
    (first,) = call(bind(first_body, rows), [ANY, VMEM], [((wide, PC), F32)], [pltpu.VMEM((NS, PC), F32)])(
        xs, state_in
    )

    part, send = call(bind(own_state_body, rows), [VMEM], [states, ((laps, wide + 8, PC), F32)])(x)
    got = swap(send, "z")
    send, decay = call(bind(scan_body, rows), [VMEM] * 2, [((laps, wide, PC), F32), ((laps, 8, PC), F32)])(got, first)
    enter = swap(send, "z")

    (y,) = call(bind(output_body, rows), [VMEM] * 3, [big])(x, part, enter)
    y_home = swap(y, "y")
    (stats,) = call(norm_body, [VMEM] * 4, [((ranks, 8, CHUNK), F32)])(y_home, z_in, up, gain)
    (tangent,) = call(bind(tangent_body, rows), [ANY] + [VMEM] * 3, [((laps, wide, PC), F32)])(stats, x, part, enter)
    stats = swap(stats, "head")
    grad_z, gy, router_grad = call(
        bind(norm_back_body, total_width), [VMEM] * 6,
        [((CHUNK, width), BF16), ((GROUP, ROWS_Y, WIDE), F32), ((1, CHUNK), F32)],
    )(stats, y_home, z_in, up, gain, router)
    gx, db, dc, send, small = call(
        bind(output_back_body, rows), [VMEM] * 6,
        [
            big, ((GROUP, CHUNK, NS), F32), ((GROUP, CHUNK, NS), F32), ((laps, 2 * wide + 8, PC), F32),
            ((2 * GROUP * HP, CHUNK), F32),
        ],
    )(x, swap(gy, "y"), y, part, enter, tangent)
    got = swap(send, "z")
    send, done = call(bind(scan_back_body, rows), [VMEM] * 2, [((laps, wide + 8, PC), F32), ((8, PC), F32)])(got, decay)
    late = swap(send, "z")

    (home,) = call(bind(input_back_body, rows), [VMEM] * 9, [((GROUP, ROWS_HOME, WIDE), F32)])(
        x, gx, part, enter, late, done, small, db, dc
    )
    piece = ((ranks, 2 * CHUNK // ranks, NS), F32)
    grad_x, ddt, grad_gain, grad_alog, grad_skip, send = call(
        home_body, [VMEM],
        [
            ((CHUNK, width), BF16), ((heads, CHUNK), F32), ((1, width), F32), ((1, heads), F32),
            ((1, heads), F32), piece,
        ],
    )(swap(home, "y"))
    (send,) = call(sum_body, [VMEM], [piece])(swap(send, "head"))
    grad_b, grad_c = call(maps_body, [VMEM], [((CHUNK, NS), F32)] * 2)(swap(send, "head"))
    return (
        grad_x,
        grad_z,
        grad_b,
        grad_c,
        ddt.T,
        router_grad.reshape(CHUNK),
        grad_gain.reshape(width),
        grad_alog.reshape(heads),
        grad_skip.reshape(heads),
    )


def solution(mesh):
    count, heads = mesh.devices.shape
    inner = Mesh(mesh.devices.reshape(count // GROUP, GROUP, heads), ("z", "y", "head"))
    seq = ("z", "y")
    in_specs = (
        P(seq, "head"),
        P(seq, None),
        P(seq),
        P(seq, "head"),
        P(seq, "head"),
        P(seq, None),
        P(seq, None),
        P(seq, "head"),
        P("head"),
        P("head"),
        P("head"),
        P("head"),
        P("head", None, None),
    )
    out_specs = (
        P(seq, "head"),
        P(seq, "head"),
        P(seq, None),
        P(seq, None),
        P(seq, "head"),
        P(seq),
        P("head"),
        P("head"),
        P("head"),
    )
    return jax.shard_map(shards, mesh=inner, in_specs=in_specs, out_specs=out_specs, check_vma=False)
```

time: 1090 us -> 199 us (0.18)
  the two profiles are of different devices: /device:TPU:8 before, /device:TPU:1 now
where the time goes in v1:
time: 199 us; the launch traced here: 197 us
  blocking collectives  125 us (63%)
  starting transfers between devices  26.2 us (13%)
  waiting for transfers between devices  24 us (12%)
  Pallas kernels  15.3 us (8%)
  local copies, waits for them, and re-layouts  5.91 us (3%)
    all_to_all x8, blocking collectives, swap(): return lax.all_to_all(a, axis, 0, 0, tiled=True)  125 us
    all_to_all x3, starting transfers between devices, swap(): return lax.all_to_all(a, axis, 0, 0, tiled=True)  26.2 us
    all_to_all x3, waiting for transfers between devices, swap(): return lax.all_to_all(a, axis, 0, 0, tiled=True)  24 us
    unnamed x28, local copies, waits for them, and re-layouts  5.91 us
  transfers between devices with their start and end apart: 3, of which 3 were waited for; matrix products, arithmetic and copies ran while one was open for 0% of the time, Pallas kernels for 1%

profile of v1, /device:TPU:1, one launch (start us, length us, event | category | flops | bytes accessed | tf_op | source)
XLA Modules:
  0.0 197.1 jit_solution(9492869586596274156)
XLA Ops:
  0.6 2.1 %shard_map.196.after = f32[4,264,256]{2,1,0:T(8,128)} custom-call(bf16[128,1024]{1,0:T(8,128)(2,1)} %x_hbm.1, bf16[128,128]{1,0:T(8,128)(2,1)} %b_hbm.1, bf16[128,128]{1,0:T(8,128)(2,1)} %c_hbm.1, f32[8,128]{1,0:T(8,128)} %bitcast.11, f32[8]{0:T(128)} %bias_hbm.1, f32[8]{0:T(128)} %alog_hbm.1, f32[8]{0:T(128)} %skip_hbm.1), custom_call_target="tpu_custom_call" | custom-call | tf_op jit(solution)/shard_map/pallas_call | solution.py:520
  2.8 15.1 %all_to_all.55.x = f32[4,264,256]{2,1,0:T(8,128)S(1)} all-to-all(f32[4,264,256]{2,1,0:T(8,128)} %shard_map.196.after), channel_id=1, replica_groups=mesh['z'=16,'y'=4,'head'=8] {'y'}, dimensions={0} | all-to-all | bytes 2162688 | tf_op jit(solution)/shard_map/all_to_all | solution.py:499
  19.4 19.3 %all-to-all-start.1 = ((f32[16,24,128]{2,1,0:T(8,128)}), f32[16,24,128]{2,1,0:T(8,128)S(1)}, u32[]{:S(2)}, u32[]{:S(2)}) async-start(f32[16,24,128]{2,1,0:T(8,128)} %copy-done.8), calls=%async_computation.1 | async-start | bytes 393216 | tf_op jit(solution)/shard_map/all_to_all | solution.py:499
  38.9 12.2 %all-to-all-done.1.got = f32[16,24,128]{2,1,0:T(8,128)S(1)} async-done(((f32[16,24,128]{2,1,0:T(8,128)}), f32[16,24,128]{2,1,0:T(8,128)S(1)}, u32[]{:S(2)}, u32[]{:S(2)}) %all-to-all-start.1) | async-done | bytes 196640 | tf_op jit(solution)/shard_map/all_to_all | solution.py:499
  51.1 18.8 %all_to_all.56.got = f32[16,16,128]{2,1,0:T(8,128)S(1)} all-to-all(f32[16,16,128]{2,1,0:T(8,128)S(1)} %get-tuple-element.33), channel_id=1, replica_groups=mesh['z'=16,'y'=4,'head'=8] {'z'}, dimensions={0} | all-to-all | bytes 262144 | tf_op jit(solution)/shard_map/all_to_all | solution.py:499
  69.9 2.1 %shard_map.200.y_in = f32[4,128,256]{2,1,0:T(8,128)} custom-call(f32[4,264,256]{2,1,0:T(8,128)S(1)} %all_to_all.55.x, f32[4,128,256]{2,1,0:T(8,128)S(1)} %get-tuple-element.31.part, f32[16,16,128]{2,1,0:T(8,128)S(1)} %all_to_all.56.got), custom_call_target="tpu_custom_call" | custom-call | tf_op jit(solution)/shard_map/pallas_call | solution.py:539
  72.0 3.5 %all-to-all-start.3 = ((f32[4,128,256]{2,1,0:T(8,128)}), f32[4,128,256]{2,1,0:T(8,128)S(1)}, u32[]{:S(2)}, u32[]{:S(2)}) async-start(f32[4,128,256]{2,1,0:T(8,128)} %shard_map.200.y_in), calls=%async_computation.3 | async-start | bytes 1048576 | tf_op jit(solution)/shard_map/all_to_all | solution.py:499
  75.5 1.6 copy-done.4
  77.1 0.9 shard_map.201.up
  78.8 3.6 %all-to-all-done.3.y = f32[4,128,256]{2,1,0:T(8,128)S(1)} async-done(((f32[4,128,256]{2,1,0:T(8,128)}), f32[4,128,256]{2,1,0:T(8,128)S(1)}, u32[]{:S(2)}, u32[]{:S(2)}) %all-to-all-start.3) | async-done | bytes 524320 | tf_op jit(solution)/shard_map/all_to_all | solution.py:499
  82.4 1.0 copy-done.2
  83.5 0.9 copy-done.5
  84.7 14.2 %all_to_all.57.stats = f32[8,8,128]{2,1,0:T(8,128)S(1)} all-to-all(f32[8,8,128]{2,1,0:T(8,128)S(1)} %shard_map.202.after), channel_id=1, replica_groups=mesh['z'=16,'y'=4,'head'=8] {'head'}, dimensions={0} | all-to-all | bytes 65536 | tf_op jit(solution)/shard_map/all_to_all | solution.py:499
  98.9 1.2 shard_map.203
  100.9 3.5 %all-to-all-start.5 = ((f32[4,136,256]{2,1,0:T(8,128)}), f32[4,136,256]{2,1,0:T(8,128)S(1)}, u32[]{:S(2)}, u32[]{:S(2)}) async-start(f32[4,136,256]{2,1,0:T(8,128)} %copy-done.6), calls=%async_computation.5 | async-start | bytes 1114112 | tf_op jit(solution)/shard_map/all_to_all | solution.py:499
  104.4 0.9 shard_map.204.tangent
  105.3 8.2 %all-to-all-done.5.gy_in = f32[4,136,256]{2,1,0:T(8,128)S(1)} async-done(((f32[4,136,256]{2,1,0:T(8,128)}), f32[4,136,256]{2,1,0:T(8,128)S(1)}, u32[]{:S(2)}, u32[]{:S(2)}) %all-to-all-start.5) | async-done | bytes 557088 | tf_op jit(solution)/shard_map/all_to_all | solution.py:499
  113.5 3.9 %shard_map.205 = (f32[4,128,256]{2,1,0:T(8,128)S(1)}, f32[4,128,128]{2,1,0:T(8,128)S(1)}, f32[4,128,128]{2,1,0:T(8,128)S(1)}, f32[16,40,128]{2,1,0:T(8,128)S(1)}, f32[16,128]{1,0:T(8,128)S(1)}) custom-call(f32[4,264,256]{2,1,0:T(8,128)S(1)} %all_to_all.55.x, f32[4,136,256]{2,1,0:T(8,128)S(1)} %all-to-all-done.5.gy_in, f32[4,128,256]{2,1,0:T(8,128)} %shard_map.200.y_in, ...), custom_call_target="tpu_custom_call" | custom-call | tf_op jit(solution)/shard_map/pallas_call | solution.py:548
  117.4 17.3 %all_to_all.58.got = f32[16,40,128]{2,1,0:T(8,128)S(1)} all-to-all(f32[16,40,128]{2,1,0:T(8,128)S(1)} %get-tuple-element.36), channel_id=1, replica_groups=mesh['z'=16,'y'=4,'head'=8] {'z'}, dimensions={0} | all-to-all | bytes 655360 | tf_op jit(solution)/shard_map/all_to_all | solution.py:499
  134.7 24.5 %all_to_all.59.late = f32[16,24,128]{2,1,0:T(8,128)S(1)} all-to-all(f32[16,24,128]{2,1,0:T(8,128)S(1)} %get-tuple-element.38), channel_id=1, replica_groups=mesh['z'=16,'y'=4,'head'=8] {'z'}, dimensions={0} | all-to-all | bytes 393216 | tf_op jit(solution)/shard_map/all_to_all | solution.py:499
  159.3 1.4 shard_map.207
  160.7 12.4 %all_to_all.60.block = f32[4,264,256]{2,1,0:T(8,128)S(1)} all-to-all(f32[4,264,256]{2,1,0:T(8,128)S(1)} %shard_map.207), channel_id=1, replica_groups=mesh['z'=16,'y'=4,'head'=8] {'y'}, dimensions={0} | all-to-all | bytes 2162688 | tf_op jit(solution)/shard_map/all_to_all | solution.py:499
  173.8 14.1 %all_to_all.61.got = f32[8,32,128]{2,1,0:T(8,128)S(1)} all-to-all(f32[8,32,128]{2,1,0:T(8,128)S(1)} %get-tuple-element.45), channel_id=1, replica_groups=mesh['z'=16,'y'=4,'head'=8] {'head'}, dimensions={0} | all-to-all | bytes 262144 | tf_op jit(solution)/shard_map/all_to_all | solution.py:499
  187.9 8.5 %all_to_all.62.got = f32[8,32,128]{2,1,0:T(8,128)S(1)} all-to-all(f32[8,32,128]{2,1,0:T(8,128)S(1)} %shard_map.209), channel_id=1, replica_groups=mesh['z'=16,'y'=4,'head'=8] {'head'}, dimensions={0} | all-to-all | bytes 262144 | tf_op jit(solution)/shard_map/all_to_all | solution.py:499
  (33 shorter events, 5.2 us)
Async XLA Ops:
  2.8 36.0 %copy-start.7 = (f32[8,128,128]{2,1,0:T(8,128)S(1)}, f32[8,128,128]{2,1,0:T(8,128)}, u32[]{:S(2)}) copy-start(f32[8,128,128]{2,1,0:T(8,128)} %state_in.1) | copy-start | bytes 1572868
  17.9 20.9 %copy-start = (f32[4,264,256]{2,1,0:T(8,128)S(1)}, f32[4,264,256]{2,1,0:T(8,128)}, u32[]{:S(2)}) copy-start(f32[4,264,256]{2,1,0:T(8,128)} %shard_map.196.after) | copy-start | bytes 3244036
  18.8 0.7 copy-start.8
  19.4 31.6 %all-to-all-start.1 = ((f32[16,24,128]{2,1,0:T(8,128)}), f32[16,24,128]{2,1,0:T(8,128)S(1)}, u32[]{:S(2)}, u32[]{:S(2)}) async-start(f32[16,24,128]{2,1,0:T(8,128)} %copy-done.8), calls=%async_computation.1 | async-start | bytes 393216 | tf_op jit(solution)/shard_map/all_to_all | solution.py:499
  51.1 20.9 %copy-start.9 = (f32[16,8,128]{2,1,0:T(8,128)}, f32[16,8,128]{2,1,0:T(8,128)S(1)}, u32[]{:S(2)}) copy-start(f32[16,8,128]{2,1,0:T(8,128)S(1)} %get-tuple-element.37.decay) | copy-start | bytes 196612
  69.9 5.6 %copy-start.12 = (s32[8,16]{1,0:T(8,128)S(1)}, s32[8,16]{1,0:T(8,128)}, u32[]{:S(2)}) copy-start(s32[8,16]{1,0:T(8,128)} %keep.1) | copy-start | bytes 1540
  72.0 10.4 %all-to-all-start.3 = ((f32[4,128,256]{2,1,0:T(8,128)}), f32[4,128,256]{2,1,0:T(8,128)S(1)}, u32[]{:S(2)}, u32[]{:S(2)}) async-start(f32[4,128,256]{2,1,0:T(8,128)} %shard_map.200.y_in), calls=%async_computation.3 | async-start | bytes 1048576 | tf_op jit(solution)/shard_map/all_to_all | solution.py:499
  75.5 1.6 copy-start.4
  77.1 5.3 %copy-start.11 = (f32[1024]{0:T(1024)S(1)}, f32[1024]{0:T(1024)}, u32[]{:S(2)}) copy-start(f32[1024]{0:T(1024)} %param.24) | copy-start | bytes 12292
  78.0 0.8 copy-start.1
  78.8 20.1 %copy-start.13 = (f32[128]{0:T(128)S(1)}, f32[128]{0:T(128)}, u32[]{:S(2)}) copy-start(f32[128]{0:T(128)} %param.15) | copy-start | bytes 1540
  82.4 1.0 copy-start.2
  83.4 0.9 copy-start.5
  84.4 14.5 %copy-start.3 = (f32[128,1024]{1,0:T(8,128)S(1)}, f32[128,1024]{1,0:T(8,128)}, u32[]{:S(2)}) copy-start(f32[128,1024]{1,0:T(8,128)} %copy-done.1) | copy-start | bytes 1572868
  100.1 0.8 copy-start.6
  100.9 12.6 %all-to-all-start.5 = ((f32[4,136,256]{2,1,0:T(8,128)}), f32[4,136,256]{2,1,0:T(8,128)S(1)}, u32[]{:S(2)}, u32[]{:S(2)}) async-start(f32[4,136,256]{2,1,0:T(8,128)} %copy-done.6), calls=%async_computation.5 | async-start | bytes 1114112 | tf_op jit(solution)/shard_map/all_to_all | solution.py:499
  105.3 29.4 %copy-start.10 = (f32[16,8,128]{2,1,0:T(8,128)S(1)}, f32[16,8,128]{2,1,0:T(8,128)}, u32[]{:S(2)}) copy-start(f32[16,8,128]{2,1,0:T(8,128)} %copy-done.9) | copy-start | bytes 196612

commit v2 on v1

--- a/solution.py
+++ b/solution.py
@@ -151,25 +151,19 @@
         xs[q, X_S:, :] = jnp.concatenate(tile, axis=0)
 
 
-def upstream_body(block_len, after, grad_full, keep, out):
-    blocks, kept = keep.shape
-    for i in range(blocks):
-        pick = (iota((kept, block_len), 1) == keep[i : i + 1, :].T).astype(BF16)
-        out[i * kept : (i + 1) * kept, :] = mm(pick, grad_full[i * block_len : (i + 1) * block_len, :])
-
-
-def to_slices(out, at, state, rows):
-    for lap in range(NS // rows):
+def to_slices(out, at, state):
+    rows = NS // out.shape[0]
+    for n in range(NS):
+        tile = slice((at + n % rows) * PC, (at + n % rows + 1) * PC)
+        out[n // rows, :, tile] = jnp.concatenate([state[n : n + 1, :PC], state[n : n + 1, PC:]], axis=0)
+
+
+def from_slices(ref, out):
+    rows = NS // ref.shape[0]
+    for n in range(NS):
+        tile = slice(n % rows * PC, (n % rows + 1) * PC)
         for h in range(HP):
-            out[lap, at + h * rows : at + (h + 1) * rows, :] = state[
-                lap * rows : (lap + 1) * rows, h * PC : (h + 1) * PC
-            ]
-
-
-def from_slices(ref, rows):
-    return jnp.concatenate(
-        [ref[:, h * rows : (h + 1) * rows, :].reshape(NS, PC) for h in range(HP)], axis=1
-    )
+            out[n : n + 1, h * PC : (h + 1) * PC] = ref[n // rows, h : h + 1, tile]
 
 
 def group_log(total):
@@ -179,7 +173,7 @@
     return out
 
 
-def own_state_body(rows, x, part, send):
+def own_state_body(block_len, x, grad_full, keep, part, send, up):
     _, step, _, _, logs, total = token_rows(x)
     cols = columns(jnp.exp(total - logs) * step)
     decay = lanes_of(jnp.exp(total))
@@ -188,52 +182,54 @@
         b_t = halves(x, k, X_B).T.astype(BF16)
         state = decay[k] * state + mm_right(b_t, x[k, :CHUNK, :] * pair_cols(cols, k))
         part[k] = state
-    to_slices(send, 0, state, rows)
-    whole = jnp.exp(group_log(total))
-    extra = jnp.where(iota((8, PC), 0) == 0, whole[:1], whole[1:])
-    for lap in range(NS // rows):
-        send[lap, HP * rows :, :] = extra
-
-
-def scan_body(rows, got, first, out, decay):
-    state = [first[h * rows : (h + 1) * rows, :] for h in range(HP)]
-    for lap in range(got.shape[0]):
-        for h in range(HP):
-            at = slice(h * rows, (h + 1) * rows)
-            out[lap, at, :] = state[h]
-            state[h] = got[lap, HP * rows + h : HP * rows + h + 1, :] * state[h] + got[lap, at, :]
-        decay[lap] = got[lap, HP * rows :, :]
-
-
-def scan_back_body(rows, got, decay, out, done):
-    laps = got.shape[0]
-    wide = HP * rows
-    state = [jnp.zeros((rows, PC), F32) for _ in range(HP)]
-    cross = [jnp.zeros((rows, PC), F32) for _ in range(HP)]
-    total = jnp.zeros((8, PC), F32)
-    for lap in reversed(range(laps)):
-        for h in range(HP):
-            at = slice(h * rows, (h + 1) * rows)
-            out[lap, at, :] = state[h]
-            cross[h] = cross[h] + state[h] * got[lap, wide + h * rows : wide + (h + 1) * rows, :]
-            state[h] = decay[lap, h : h + 1, :] * state[h] + got[lap, at, :]
-        total = total + got[lap, 2 * wide :, :]
-    done[...] = total
-    row = iota((8, PC), 0)
-    extra = jnp.zeros((8, PC), F32)
-    for h in range(HP):
-        extra = extra + jnp.where(row == h, jnp.sum(cross[h], axis=0, keepdims=True), 0.0)
-    for lap in range(laps):
-        out[lap, wide:, :] = extra
-
-
-def first_body(rows, after, state_in, out, flat):
+    to_slices(send, 0, state)
+    whole = jnp.broadcast_to(jnp.exp(group_log(total)), (HP, PC))
+    for lap in range(send.shape[0]):
+        send[lap, :, send.shape[2] - PC :] = whole
+    blocks, kept = keep.shape
+    for i in range(blocks):
+        pick = (iota((kept, block_len), 1) == keep[i : i + 1, :].T).astype(BF16)
+        up[i * kept : (i + 1) * kept, :] = mm(pick, grad_full[i * block_len : (i + 1) * block_len, :])
+
+
+def spread(row, count):
+    return jnp.concatenate([row] * count, axis=1)
+
+
+def scan_body(got, state_in, out, decay, flat, first):
+    laps, _, lanes = out.shape
+    rows = lanes // PC
     base = own_heads()
     for h in range(HP):
         flat[...] = state_in[base + h].T
-        out[h * rows : (h + 1) * rows, :] = flat[
-            pl.ds(pl.multiple_of(lax.axis_index("z") * rows, rows), rows), :
-        ]
+        for j in range(rows):
+            first[h : h + 1, j * PC : (j + 1) * PC] = flat[pl.ds(lax.axis_index("z") * rows + j, 1), :]
+    state = first[...]
+    for lap in range(laps):
+        out[lap] = state
+        factor = got[lap, :, lanes:]
+        decay[lap] = factor
+        state = spread(factor, rows) * state + got[lap, :, :lanes]
+
+
+def scan_back_body(got, decay, out, done):
+    laps = got.shape[0]
+    lanes = out.shape[2] - PC
+    rows = lanes // PC
+    state = jnp.zeros((HP, lanes), F32)
+    cross = jnp.zeros((HP, lanes), F32)
+    total = jnp.zeros((HP, 3 * PC), F32)
+    for lap in reversed(range(laps)):
+        out[lap, :, :lanes] = state
+        cross = cross + state * got[lap, :, lanes : 2 * lanes]
+        state = spread(decay[lap], rows) * state + got[lap, :, :lanes]
+        total = total + got[lap, :, 2 * lanes :]
+    done[...] = total
+    extra = cross[:, :PC]
+    for j in range(1, rows):
+        extra = extra + cross[:, j * PC : (j + 1) * PC]
+    for lap in range(laps):
+        out[lap, :, lanes:] = extra
 
 
 def group_states(part, enter, total):
@@ -258,11 +254,12 @@
     return jnp.where(lower, jnp.exp(jnp.where(lower, diff, 0.0)), 0.0)
 
 
-def output_body(rows, x, part, got, y_out):
+def output_body(x, part, got, y_out, enter):
+    from_slices(got, enter)
     _, step, _, _, logs, total = token_rows(x)
     cols = columns(logs, jnp.exp(logs))
     lower = iota((CHUNK, CHUNK), 0) >= iota((CHUNK, CHUNK), 1)
-    states = group_states(part, from_slices(got, rows), total)
+    states = group_states(part, enter[...], total)
     d = x[0, X_S + 3 : X_S + 4, :]
     for k in range(GROUP):
         b = halves(x, k, X_B).astype(BF16)
@@ -320,33 +317,24 @@
     out[...] = jnp.broadcast_to(total[None], out.shape)
 
 
-def tangent_body(rows, after, x, part, got, out):
-    _, step, _, _, logs, total = token_rows(x)
+def output_back_body(x, gy_in, y_in, part, enter, gx_out, db_out, dc_out, send, small):
+    raw, step, rate, la, logs, total = token_rows(x)
     rest = rest_logs(total)
-    cols = columns(jnp.exp(total - logs + rest) * step * logs)
+    cols = columns(
+        logs, jnp.exp(logs), jnp.exp(total - logs), step, jnp.exp(total - logs + rest) * step * logs
+    )
     near = lanes_of(jnp.exp(rest) * total)
-    states = group_states(part, from_slices(got, rows), total)
-    tangent = jnp.zeros((NS, WIDE), F32)
-    for k in range(GROUP):
-        b_t = halves(x, k, X_B).T.astype(BF16)
-        scaled = x[k, :CHUNK, :] * pair_cols(cols, k)
-        tangent = tangent + near[k] * states[k + 1] - mm_right(b_t, scaled)
-    to_slices(out, 0, tangent, rows)
-
-
-def output_back_body(rows, x, gy_in, y_in, part, got, tangent, gx_out, db_out, dc_out, send, small):
-    raw, step, rate, la, logs, total = token_rows(x)
-    cols = columns(logs, jnp.exp(logs), jnp.exp(total - logs), step)
     n = GROUP * HP
     lower = iota((CHUNK, CHUNK), 0) >= iota((CHUNK, CHUNK), 1)
     upper = iota((CHUNK, CHUNK), 0) <= iota((CHUNK, CHUNK), 1)
-    states = group_states(part, from_slices(got, rows), total)
+    states = group_states(part, enter[...], total)
     d = x[0, X_S + 3 : X_S + 4, :]
     decay = lanes_of(jnp.exp(total))
     gain_part = jnp.zeros((1, WIDE), F32)
     skip_part = jnp.zeros((1, WIDE), F32)
     dots, xv, ends = [None] * n, [None] * n, [None] * n
     own = jnp.zeros((NS, WIDE), F32)
+    tangent = jnp.zeros((NS, WIDE), F32)
     for k in reversed(range(GROUP)):
         b = halves(x, k, X_B).astype(BF16)
         c32 = halves(x, k, X_C)
@@ -380,6 +368,8 @@
         ]
         sh, sl = split(tail * stepc * xk)
         db_out[k] = mm_left(dscores.T, c) + (mm(sh, oh, NT) + (mm(sh, ol, NT) + mm(sl, oh, NT)))
+        b_t = halves(x, k, X_B).T.astype(BF16)
+        tangent = tangent + near[k] * states[k + 1] - mm_right(b_t, xk * pair_cols(cols, k, 4 * n))
         eg = pair_cols(cols, k, n) * gy
         dc_out[k] = mm_left(dscores, b) + mm_both(eg, states[k], NT)
         own = decay[k] * own + mm_right(c32.T.astype(BF16), eg)
@@ -389,27 +379,33 @@
     dla = dla + jnp.concatenate(ends, axis=0)
     small[:n] = dla
     small[n:] = xv
-    to_slices(send, 0, own, rows)
-    send[:, HP * rows : 2 * HP * rows, :] = tangent[...]
+    laps = send.shape[0]
+    rows = NS // laps
+    to_slices(send, 0, own)
+    to_slices(send, rows, tangent)
     decayed = dla * la
     odd = iota((n, 1), 0) % HP
     extra = jnp.concatenate(
-        [gain_part[:, :PC], gain_part[:, PC:], skip_part[:, :PC], skip_part[:, PC:]]
-        + [jnp.sum(jnp.where(odd == h, decayed, 0.0), axis=0, keepdims=True) for h in range(HP)]
-        + [jnp.zeros((2, PC), F32)], axis=0,
-    )
-    for lap in range(NS // rows):
-        send[lap, 2 * HP * rows :, :] = extra
-
-
-def input_back_body(rows, x, gx_in, part, got, late, done, small, db_in, dc_in, home):
+        [jnp.concatenate([a[:, :PC], a[:, PC:]], axis=0) for a in (gain_part, skip_part)]
+        + [
+            jnp.concatenate(
+                [jnp.sum(jnp.where(odd == h, decayed, 0.0), axis=0, keepdims=True) for h in range(HP)], axis=0
+            )
+        ], axis=1,
+    )
+    for lap in range(laps):
+        send[lap, :, 2 * rows * PC :] = extra
+
+
+def input_back_body(x, gx_in, part, enter, late, done, small, db_in, dc_in, home, grad_out):
+    from_slices(late, grad_out)
     raw, step, rate, la, logs, total = token_rows(x)
     n = GROUP * HP
     rest = rest_logs(total)
     cols = columns(jnp.exp(total - logs + rest), step)
-    states = group_states(part, from_slices(got, rows), total)
+    states = group_states(part, enter[...], total)
     reach = lanes_of(jnp.exp(rest))
-    grad = from_slices(late, rows)
+    grad = grad_out[...]
     gh, gl = split(grad)
     ends, xv = [], []
     half = CHUNK // 2
@@ -432,12 +428,13 @@
     dla = jnp.dot(-step * xv, after, precision=lax.Precision.HIGHEST, preferred_element_type=F32)
     dla = small[:n] + dla + jnp.concatenate(ends, axis=0)
     ddt = (dla * rate + small[n:] + xv) * sigmoid(raw)
-    alog_rows = done[4:6, :]
+    alog_rows = done[:, 2 * PC :]
+    lanes = late.shape[2] - PC
     for lap in range(late.shape[0]):
-        alog_rows = alog_rows + late[lap, HP * rows : HP * rows + HP, :]
+        alog_rows = alog_rows + late[lap, :, lanes:]
     shared = jnp.concatenate(
-        [jnp.concatenate([done[i : i + 1, :], done[i + 1 : i + 2, :]], axis=1) for i in (0, 2)]
-        + [jnp.concatenate([alog_rows[:1], alog_rows[1:]], axis=1), jnp.zeros((4, WIDE), F32)], axis=0,
+        [jnp.concatenate([a[:1], a[1:]], axis=1) for a in (done[:, :PC], done[:, PC : 2 * PC], alog_rows)]
+        + [jnp.zeros((4, WIDE), F32)], axis=0,
     )
     for k in range(GROUP):
         own = jnp.concatenate([ddt[k * HP : k * HP + 1], ddt[k * HP + 1 : k * HP + 2]], axis=1)
@@ -510,8 +507,7 @@
     block_len = grad_full.shape[0] // keep.shape[0]
     big = ((GROUP, CHUNK, WIDE), F32)
     states = ((GROUP, NS, WIDE), F32)
-    rows = NS // laps
-    wide = HP * rows
+    lanes = NS // laps * PC
     bind = functools.partial
     dma = pltpu.SemaphoreType.DMA
 
@@ -526,39 +522,36 @@
         ], FULL,
     )(x_in, b_in, c_in, dt_raw.T, dt_bias, a_log, d_skip)
     x = swap(xs, "y")
-    (up,) = call(bind(upstream_body, block_len), [ANY] + [VMEM] * 2, [((CHUNK, width), F32)])(xs, grad_full, keep)
-    (first,) = call(bind(first_body, rows), [ANY, VMEM], [((wide, PC), F32)], [pltpu.VMEM((NS, PC), F32)])(
-        xs, state_in
-    )
-
-    part, send = call(bind(own_state_body, rows), [VMEM], [states, ((laps, wide + 8, PC), F32)])(x)
-    got = swap(send, "z")
-    send, decay = call(bind(scan_body, rows), [VMEM] * 2, [((laps, wide, PC), F32), ((laps, 8, PC), F32)])(got, first)
-    enter = swap(send, "z")
-
-    (y,) = call(bind(output_body, rows), [VMEM] * 3, [big])(x, part, enter)
+    part, send, up = call(
+        bind(own_state_body, block_len), [VMEM] * 3,
+        [states, ((laps, HP, lanes + PC), F32), ((CHUNK, width), F32)],
+    )(x, grad_full, keep)
+    send, decay = call(
+        scan_body, [VMEM] * 2, [((laps, HP, lanes), F32), ((laps, HP, PC), F32)],
+        [pltpu.VMEM((NS, PC), F32), pltpu.VMEM((HP, lanes), F32)],
+    )(swap(send, "z"), state_in)
+
+    y, enter = call(output_body, [VMEM] * 3, [big, ((NS, WIDE), F32)])(x, part, swap(send, "z"))
     y_home = swap(y, "y")
     (stats,) = call(norm_body, [VMEM] * 4, [((ranks, 8, CHUNK), F32)])(y_home, z_in, up, gain)
-    (tangent,) = call(bind(tangent_body, rows), [ANY] + [VMEM] * 3, [((laps, wide, PC), F32)])(stats, x, part, enter)
-    stats = swap(stats, "head")
     grad_z, gy, router_grad = call(
         bind(norm_back_body, total_width), [VMEM] * 6,
         [((CHUNK, width), BF16), ((GROUP, ROWS_Y, WIDE), F32), ((1, CHUNK), F32)],
-    )(stats, y_home, z_in, up, gain, router)
+    )(swap(stats, "head"), y_home, z_in, up, gain, router)
     gx, db, dc, send, small = call(
-        bind(output_back_body, rows), [VMEM] * 6,
+        output_back_body, [VMEM] * 5,
         [
-            big, ((GROUP, CHUNK, NS), F32), ((GROUP, CHUNK, NS), F32), ((laps, 2 * wide + 8, PC), F32),
+            big, ((GROUP, CHUNK, NS), F32), ((GROUP, CHUNK, NS), F32), ((laps, HP, 2 * lanes + 3 * PC), F32),
             ((2 * GROUP * HP, CHUNK), F32),
         ],
-    )(x, swap(gy, "y"), y, part, enter, tangent)
-    got = swap(send, "z")
-    send, done = call(bind(scan_back_body, rows), [VMEM] * 2, [((laps, wide + 8, PC), F32), ((8, PC), F32)])(got, decay)
-    late = swap(send, "z")
-
-    (home,) = call(bind(input_back_body, rows), [VMEM] * 9, [((GROUP, ROWS_HOME, WIDE), F32)])(
-        x, gx, part, enter, late, done, small, db, dc
-    )
+    )(x, swap(gy, "y"), y, part, enter)
+    send, done = call(scan_back_body, [VMEM] * 2, [((laps, HP, lanes + PC), F32), ((HP, 3 * PC), F32)])(
+        swap(send, "z"), decay
+    )
+
+    (home,) = call(
+        input_back_body, [VMEM] * 9, [((GROUP, ROWS_HOME, WIDE), F32)], [pltpu.VMEM((NS, WIDE), F32)]
+    )(x, gx, part, enter, swap(send, "z"), done, small, db, dc)
     piece = ((ranks, 2 * CHUNK // ranks, NS), F32)
     grad_x, ddt, grad_gain, grad_alog, grad_skip, send = call(
         home_body, [VMEM],

time: 199 us -> 188 us (0.945)
  blocking collectives: 125 us -> 174 us
  starting transfers between devices: 26.2 us -> 0 us
  waiting for transfers between devices: 24 us -> 0 us
  local copies, waits for them, and re-layouts: 5.91 us -> 0.03 us
  Pallas kernels: 15.3 us -> 13 us
    all_to_all x8 -> x11, blocking collectives: 125 us -> 174 us  [swap(): return lax.all_to_all(a, axis, 0, 0, tiled=True)]
    all_to_all x3 -> x0, starting transfers between devices: 26.2 us -> none  [swap(): return lax.all_to_all(a, axis, 0, 0, tiled=True)]
    all_to_all x3 -> x0, waiting for transfers between devices: 24 us -> none  [swap(): return lax.all_to_all(a, axis, 0, 0, tiled=True)]
    unnamed x28 -> x12, local copies, waits for them, and re-layouts: 5.91 us -> 0.03 us
    pallas_call x9 -> x6, Pallas kernels: 10.2 us -> 7.96 us  [the longest x1 3.22 us: shards(): call(output_back_body, [VMEM] * 5, [big, ((GROUP, CHUNK, NS), F32), ((GRO...]
  transfers between devices with their start and end apart: 3 -> 0, of which waited for: 3 -> 0; matrix products, arithmetic and copies ran while one was open for 0% -> 0% of each run, Pallas kernels for 1% -> 0%
where the time goes in v2:
time: 188 us
  blocking collectives  174 us (93%)
  Pallas kernels  13 us (7%)
    all_to_all x11, blocking collectives, swap(): return lax.all_to_all(a, axis, 0, 0, tiled=True)  174 us

profile of v2, /device:TPU:1, one launch (start us, length us, event | category | flops | bytes accessed | tf_op | source)
XLA Modules:
  0.0 187.8 jit_solution(17805938444935887053)
XLA Ops:
  0.6 2.1 %shard_map.196 = f32[4,264,256]{2,1,0:T(8,128)} custom-call(bf16[128,1024]{1,0:T(8,128)(2,1)} %x_hbm.1, bf16[128,128]{1,0:T(8,128)(2,1)} %b_hbm.1, bf16[128,128]{1,0:T(8,128)(2,1)} %c_hbm.1, f32[8,128]{1,0:T(8,128)} %bitcast.11, f32[8]{0:T(128)} %bias_hbm.1, f32[8]{0:T(128)} %alog_hbm.1, f32[8]{0:T(128)} %skip_hbm.1), custom_call_target="tpu_custom_call" | custom-call | tf_op jit(solution)/shard_map/pallas_call | solution.py:516
  2.8 0.0 copy-start
  2.8 0.0 copy-start.4
  2.8 15.1 %all_to_all.55.x = f32[4,264,256]{2,1,0:T(8,128)S(1)} all-to-all(f32[4,264,256]{2,1,0:T(8,128)} %shard_map.196), channel_id=1, replica_groups=mesh['z'=16,'y'=4,'head'=8] {'y'}, dimensions={0} | all-to-all | bytes 2162688 | tf_op jit(solution)/shard_map/all_to_all | solution.py:496
  17.9 1.7 shard_map.197
  19.6 31.2 %all_to_all.56.got = f32[16,2,1152]{2,1,0:T(2,128)S(1)} all-to-all(f32[16,2,1152]{2,1,0:T(2,128)S(1)} %get-tuple-element.35), channel_id=1, replica_groups=mesh['z'=16,'y'=4,'head'=8] {'z'}, dimensions={0} | all-to-all | bytes 294912 | tf_op jit(solution)/shard_map/all_to_all | solution.py:496
  50.8 0.2 shard_map.198
  51.0 16.8 %all_to_all.57.got = f32[16,2,1024]{2,1,0:T(2,128)S(1)} all-to-all(f32[16,2,1024]{2,1,0:T(2,128)S(1)} %get-tuple-element.36), channel_id=1, replica_groups=mesh['z'=16,'y'=4,'head'=8] {'z'}, dimensions={0} | all-to-all | bytes 262144 | tf_op jit(solution)/shard_map/all_to_all | solution.py:496
  67.7 1.3 shard_map.199
  69.1 9.5 %all_to_all.58.y = f32[4,128,256]{2,1,0:T(8,128)S(1)} all-to-all(f32[4,128,256]{2,1,0:T(8,128)S(1)} %get-tuple-element.37.y_in), channel_id=1, replica_groups=mesh['z'=16,'y'=4,'head'=8] {'y'}, dimensions={0} | all-to-all | bytes 1048576 | tf_op jit(solution)/shard_map/all_to_all | solution.py:496
  78.6 0.3 shard_map.200
  78.9 14.2 %all_to_all.59.stats = f32[8,8,128]{2,1,0:T(8,128)S(1)} all-to-all(f32[8,8,128]{2,1,0:T(8,128)S(1)} %shard_map.200), channel_id=1, replica_groups=mesh['z'=16,'y'=4,'head'=8] {'head'}, dimensions={0} | all-to-all | bytes 65536 | tf_op jit(solution)/shard_map/all_to_all | solution.py:496
  93.1 1.2 shard_map.201
  94.3 11.5 %all_to_all.60.gy_in = f32[4,136,256]{2,1,0:T(8,128)S(1)} all-to-all(f32[4,136,256]{2,1,0:T(8,128)S(1)} %get-tuple-element.39), channel_id=1, replica_groups=mesh['z'=16,'y'=4,'head'=8] {'y'}, dimensions={0} | all-to-all | bytes 1114112 | tf_op jit(solution)/shard_map/all_to_all | solution.py:496
  105.8 3.2 %shard_map.202 = (f32[4,128,256]{2,1,0:T(8,128)S(1)}, f32[4,128,128]{2,1,0:T(8,128)S(1)}, f32[4,128,128]{2,1,0:T(8,128)S(1)}, f32[16,2,2432]{2,1,0:T(2,128)S(1)}, f32[16,128]{1,0:T(8,128)S(1)}) custom-call(f32[4,264,256]{2,1,0:T(8,128)S(1)} %all_to_all.55.x, f32[4,136,256]{2,1,0:T(8,128)S(1)} %all_to_all.60.gy_in, ...), custom_call_target="tpu_custom_call" | custom-call | tf_op jit(solution)/shard_map/pallas_call | solution.py:541
  109.0 16.8 %all_to_all.61.got = f32[16,2,2432]{2,1,0:T(2,128)S(1)} all-to-all(f32[16,2,2432]{2,1,0:T(2,128)S(1)} %get-tuple-element.42), channel_id=1, replica_groups=mesh['z'=16,'y'=4,'head'=8] {'z'}, dimensions={0} | all-to-all | bytes 622592 | tf_op jit(solution)/shard_map/all_to_all | solution.py:496
  125.8 0.1 shard_map.203
  126.0 24.0 %all_to_all.62.late = f32[16,2,1152]{2,1,0:T(2,128)S(1)} all-to-all(f32[16,2,1152]{2,1,0:T(2,128)S(1)} %get-tuple-element.44), channel_id=1, replica_groups=mesh['z'=16,'y'=4,'head'=8] {'z'}, dimensions={0} | all-to-all | bytes 294912 | tf_op jit(solution)/shard_map/all_to_all | solution.py:496
  150.0 1.4 shard_map.204
  151.4 13.9 %all_to_all.63.block = f32[4,264,256]{2,1,0:T(8,128)S(1)} all-to-all(f32[4,264,256]{2,1,0:T(8,128)S(1)} %shard_map.204), channel_id=1, replica_groups=mesh['z'=16,'y'=4,'head'=8] {'y'}, dimensions={0} | all-to-all | bytes 2162688 | tf_op jit(solution)/shard_map/all_to_all | solution.py:496
  165.4 0.8 shard_map.205
  166.1 12.5 %all_to_all.64.got = f32[8,32,128]{2,1,0:T(8,128)S(1)} all-to-all(f32[8,32,128]{2,1,0:T(8,128)S(1)} %get-tuple-element.51), channel_id=1, replica_groups=mesh['z'=16,'y'=4,'head'=8] {'head'}, dimensions={0} | all-to-all | bytes 262144 | tf_op jit(solution)/shard_map/all_to_all | solution.py:496
  178.7 8.5 %all_to_all.65.got = f32[8,32,128]{2,1,0:T(8,128)S(1)} all-to-all(f32[8,32,128]{2,1,0:T(8,128)S(1)} %shard_map.206), channel_id=1, replica_groups=mesh['z'=16,'y'=4,'head'=8] {'head'}, dimensions={0} | all-to-all | bytes 262144 | tf_op jit(solution)/shard_map/all_to_all | solution.py:496
  187.2 0.7 shard_map.207
  (11 shorter events, 0.0 us)
Async XLA Ops:
  2.8 15.1 %copy-start = (bf16[1024,1024]{1,0:T(8,128)(2,1)S(1)}, bf16[1024,1024]{1,0:T(8,128)(2,1)}, u32[]{:S(2)}) copy-start(bf16[1024,1024]{1,0:T(8,128)(2,1)} %grad_full.1) | copy-start | bytes 6291460
  2.8 15.1 %copy-start.4 = (s32[8,16]{1,0:T(8,128)S(1)}, s32[8,16]{1,0:T(8,128)}, u32[]{:S(2)}) copy-start(s32[8,16]{1,0:T(8,128)} %keep.1) | copy-start | bytes 1540
  17.9 32.9 %copy-start.2 = (f32[8,128,128]{2,1,0:T(8,128)S(1)}, f32[8,128,128]{2,1,0:T(8,128)}, u32[]{:S(2)}) copy-start(f32[8,128,128]{2,1,0:T(8,128)} %state_in.1) | copy-start | bytes 1572868
  67.7 10.8 %copy-start.1 = (bf16[128,1024]{1,0:T(8,128)(2,1)S(1)}, bf16[128,1024]{1,0:T(8,128)(2,1)}, u32[]{:S(2)}) copy-start(bf16[128,1024]{1,0:T(8,128)(2,1)} %z.3) | copy-start | bytes 786436
  67.7 10.8 %copy-start.3 = (f32[1024]{0:T(1024)S(1)}, f32[1024]{0:T(1024)}, u32[]{:S(2)}) copy-start(f32[1024]{0:T(1024)} %param.24) | copy-start | bytes 12292
  69.0 24.1 %copy-start.5 = (f32[128]{0:T(128)S(1)}, f32[128]{0:T(128)}, u32[]{:S(2)}) copy-start(f32[128]{0:T(128)} %param.15) | copy-start | bytes 1540

commit v3 on v2

v3 whole, which is shorter than its diff:
```python
import functools

import jax
import jax.numpy as jnp
import numpy as np
from jax import lax
from jax.experimental import pallas as pl
from jax.experimental.pallas import tpu as pltpu
from jax.sharding import Mesh
from jax.sharding import PartitionSpec as P

EPS = 1e-05
GROUP = 4
CHUNK = 128
HP = 2
PC = 128
NS = 128
WIDE = HP * PC
F32 = jnp.float32
BF16 = jnp.bfloat16
NN = ((1,), (0,))
NT = ((1,), (1,))

HD = GROUP * HP
ROWS_S = NS + 8
ROWS_G = 2 * NS + 8

VMEM = pl.BlockSpec(memory_space=pltpu.VMEM)
SMEM = pl.BlockSpec(memory_space=pltpu.SMEM)
ANY = pl.BlockSpec(memory_space=pl.ANY)
LIMIT = 24 * 2**20
FULL = 56 * 2**20


def mm(a, b, dims=NN):
    return lax.dot_general(a, b, (dims, ((), ())), preferred_element_type=F32)


def split(a):
    high = a.astype(BF16)
    return high, (a - high.astype(F32)).astype(BF16)


def mm_left(a, exact, dims=NN):
    high, low = split(a)
    return mm(high, exact, dims) + mm(low, exact, dims)


def mm_right(exact, b, dims=NN):
    high, low = split(b)
    return mm(exact, high, dims) + mm(exact, low, dims)


def mm_both(a, b, dims=NN):
    ah, al = split(a)
    bh, bl = split(b)
    return mm(ah, bh, dims) + (mm(ah, bl, dims) + mm(al, bh, dims))


def iota(shape, dim):
    return lax.broadcasted_iota(jnp.int32, shape, dim)


def softplus(v):
    return jnp.maximum(v, 0.0) + jnp.log1p(jnp.exp(-jnp.abs(v)))


def sigmoid(v):
    return 1.0 / (1.0 + jnp.exp(-v))


def own_heads():
    return lax.axis_index("y") * HP


def head_col(ref):
    row = iota((HD, 1), 0)
    out = jnp.zeros((HD, 1), F32)
    for h in range(HD):
        out = jnp.where(row == h, ref[h], out)
    return out


T_RAW, T_STEP, T_LA, T_LOGS, T_RATE, T_SKIP, ROWS_T = (HD * i for i in range(7))


def table(tok, at):
    return tok[at : at + HD, :]


def last(rows):
    return rows[:, CHUNK - 1 :]


def columns(*rows):
    count = sum(r.shape[0] for r in rows)
    return jnp.concatenate(rows + (jnp.zeros((CHUNK - count, CHUNK), F32),), axis=0).T


def rows_of(cols):
    pad = jnp.zeros((CHUNK, CHUNK - len(cols)), F32)
    return jnp.concatenate(list(cols) + [pad], axis=1).T[: len(cols)]


def pair(a, b, rows):
    return jnp.concatenate(
        [jnp.broadcast_to(a, (rows, PC)), jnp.broadcast_to(b, (rows, PC))], axis=1
    )


def lanes_of(values):
    return [pair(values[q * HP : q * HP + 1], values[q * HP + 1 : q * HP + 2], 1) for q in range(GROUP)]


def pair_cols(cols, q, at=0):
    c = at + q * HP
    return pair(cols[:, c : c + 1], cols[:, c + 1 : c + 2], CHUNK)


def head_sums(a):
    return [jnp.sum(a[:, h * PC : (h + 1) * PC], axis=1, keepdims=True) for h in range(HP)]


def two(row):
    return jnp.concatenate([row[:, :PC], row[:, PC:]], axis=0)


def one(rows):
    return jnp.concatenate([rows[:1], rows[1:]], axis=1)


def lanes(q):
    return slice(q * WIDE, (q + 1) * WIDE)


def own_state_body(
    x_hbm, b_hbm, dt_hbm, bias_hbm, alog_hbm, skip_hbm, send, tok, x, b, dt_t, bias, alog, skip, sem
):
    copies = [
        pltpu.make_async_copy(src, dst, sem.at[i])
        for i, (src, dst) in enumerate(
            [(dt_hbm, dt_t), (bias_hbm, bias), (alog_hbm, alog), (skip_hbm, skip), (b_hbm, b), (x_hbm, x)]
        )
    ]
    for copy in copies:
        copy.start()
    for copy in copies:
        copy.wait()
    raw = dt_t[...] + head_col(bias)
    step = softplus(raw)
    rate = -jnp.exp(head_col(alog))
    la = step * rate
    upper = (iota((CHUNK, CHUNK), 0) <= iota((CHUNK, CHUNK), 1)).astype(F32)
    logs = jnp.dot(la, upper, precision=lax.Precision.HIGHEST, preferred_element_type=F32)
    for at, value in (
        (T_RAW, raw), (T_STEP, step), (T_LA, la), (T_LOGS, logs), (T_RATE, rate), (T_SKIP, head_col(skip))
    ):
        tok[at : at + HD, :] = jnp.broadcast_to(value, (HD, CHUNK))
    cols = columns(jnp.exp(last(logs) - logs) * step)
    decay = lanes_of(jnp.exp(last(logs)))
    b_t = b[...].astype(F32).T.astype(BF16)
    for q in range(GROUP):
        send[q, :NS, :] = mm_right(b_t, x[:, lanes(q)].astype(F32) * pair_cols(cols, q))
        send[q, NS:, :] = jnp.broadcast_to(decay[q], (8, WIDE))


def to_slices(out, at, state):
    rows = NS // out.shape[0]
    for n in range(NS):
        tile = slice((at + n % rows) * PC, (at + n % rows + 1) * PC)
        out[n // rows, :, tile] = jnp.concatenate([state[n : n + 1, :PC], state[n : n + 1, PC:]], axis=0)


def from_slices(ref, out):
    rows = NS // ref.shape[0]
    for n in range(NS):
        tile = slice(n % rows * PC, (n % rows + 1) * PC)
        for h in range(HP):
            out[n : n + 1, h * PC : (h + 1) * PC] = ref[n // rows, h : h + 1, tile]


def group_state_body(block_len, got, grad_full, keep, part, send, up):
    state = got[0, :NS, :]
    whole = got[0, NS : NS + 1, :]
    part[0] = state
    for k in range(1, GROUP):
        decay = got[k, NS : NS + 1, :]
        state = decay * state + got[k, :NS, :]
        whole = whole * decay
        part[k] = state
    to_slices(send, 0, state)
    for lap in range(send.shape[0]):
        send[lap, :, send.shape[2] - PC :] = two(whole)
    blocks, kept = keep.shape
    for i in range(blocks):
        pick = (iota((kept, block_len), 1) == keep[i : i + 1, :].T).astype(BF16)
        up[i * kept : (i + 1) * kept, :] = mm(pick, grad_full[i * block_len : (i + 1) * block_len, :])


def spread(row, count):
    return jnp.concatenate([row] * count, axis=1)


def scan_body(got, state_in, out, decay, flat, first):
    laps, _, lanes = out.shape
    rows = lanes // PC
    base = own_heads()
    for h in range(HP):
        flat[...] = state_in[base + h].T
        for j in range(rows):
            first[h : h + 1, j * PC : (j + 1) * PC] = flat[pl.ds(lax.axis_index("z") * rows + j, 1), :]
    state = first[...]
    for lap in range(laps):
        out[lap] = state
        factor = got[lap, :, lanes:]
        decay[lap] = factor
        state = spread(factor, rows) * state + got[lap, :, :lanes]


def scan_back_body(got, decay, out, done):
    laps = got.shape[0]
    lanes = out.shape[2] - PC
    rows = lanes // PC
    state = jnp.zeros((HP, lanes), F32)
    cross = jnp.zeros((HP, lanes), F32)
    total = jnp.zeros((HP, 3 * PC), F32)
    for lap in reversed(range(laps)):
        out[lap, :, :lanes] = state
        cross = cross + state * got[lap, :, lanes : 2 * lanes]
        state = spread(decay[lap], rows) * state + got[lap, :, :lanes]
        total = total + got[lap, :, 2 * lanes :]
    done[...] = total
    extra = cross[:, :PC]
    for j in range(1, rows):
        extra = extra + cross[:, j * PC : (j + 1) * PC]
    for lap in range(laps):
        out[lap, :, lanes:] = extra


def enter_body(got, own, part, send, flat):
    from_slices(got, flat)
    state = flat[...]
    send[0] = state
    reach = own[0, NS : NS + 1, :]
    for k in range(1, GROUP):
        send[k] = part[k - 1] + reach * state
        reach = reach * own[k, NS : NS + 1, :]


def decays(logs, cols, r, lower):
    diff = cols[:, r : r + 1] - logs[r : r + 1]
    return jnp.where(lower, jnp.exp(jnp.where(lower, diff, 0.0)), 0.0)


def output_body(x, b, c, z, up, gain, tok, enter, y_out, stats):
    logs, step = table(tok, T_LOGS), table(tok, T_STEP)
    cols = columns(logs, jnp.exp(logs))
    lower = iota((CHUNK, CHUNK), 0) >= iota((CHUNK, CHUNK), 1)
    d = lanes_of(last(table(tok, T_SKIP)))
    scores = mm(c[...], b[...], NT)
    squares = jnp.zeros((CHUNK, 1), F32)
    crosses = jnp.zeros((CHUNK, 1), F32)
    for q in range(GROUP):
        inner = []
        for h in range(HP):
            r = q * HP + h
            mixed = decays(logs, cols, r, lower) * scores * step[r : r + 1]
            inner.append(mm_left(mixed, x[:, r * PC : (r + 1) * PC]))
        carried = mm_right(c[...], enter[q]) * pair_cols(cols, q, HD)
        y = jnp.concatenate(inner, axis=1) + carried + d[q] * x[:, lanes(q)].astype(F32)
        y_out[:, lanes(q)] = y
        zq = z[:, lanes(q)].astype(F32)
        gated = y * zq * sigmoid(zq)
        squares = squares + jnp.sum(gated * gated, axis=1, keepdims=True)
        crosses = crosses + jnp.sum(up[:, lanes(q)] * gated * gain[:, lanes(q)], axis=1, keepdims=True)
    tile = jnp.concatenate([rows_of([squares, crosses]), jnp.zeros((6, CHUNK), F32)], axis=0)
    stats[...] = jnp.broadcast_to(tile[None], stats.shape)


def output_back_body(
    total_width, stats, x, b, c, z, up, gain, router, tok, enter, own, y_in,
    gz, gx_out, send, small, maps, router_grad,
):
    sums = stats[0, :2, :]
    for i in range(1, stats.shape[0]):
        sums = sums + stats[i, :2, :]
    rstd = lax.rsqrt(sums[:1] / total_width + EPS)
    cross = sums[1:]
    router_grad[...] = rstd * cross
    logs, step, la = table(tok, T_LOGS), table(tok, T_STEP), table(tok, T_LA)
    total = last(logs)
    tail = jnp.exp(total - logs)
    cols = columns(
        logs, jnp.exp(logs), step, tail * step * logs,
        rstd * router[...], rstd * rstd * rstd * (router[...] * cross / total_width),
    )
    at_a = 4 * HD
    lower = iota((CHUNK, CHUNK), 0) >= iota((CHUNK, CHUNK), 1)
    upper = iota((CHUNK, CHUNK), 0) <= iota((CHUNK, CHUNK), 1)
    d = lanes_of(last(table(tok, T_SKIP)))
    decay = lanes_of(jnp.exp(total))
    near = lanes_of(total)
    scores_t = mm(b[...], c[...], NT)
    b_t = b[...].astype(F32).T.astype(BF16)
    c_t = c[...].astype(F32).T.astype(BF16)
    dscores = jnp.zeros((CHUNK, CHUNK), F32)
    dc = jnp.zeros((CHUNK, NS), F32)
    dots, xv, shared = [], [], []
    for q in range(GROUP):
        xb = x[:, lanes(q)]
        xq, zq, u, y = xb.astype(F32), z[:, lanes(q)].astype(F32), up[:, lanes(q)], y_in[:, lanes(q)]
        sig = sigmoid(zq)
        gate = zq * sig
        gated = y * gate
        scaled = cols[:, at_a : at_a + 1] * u
        gg = scaled * gain[:, lanes(q)] - gated * cols[:, at_a + 1 : at_a + 2]
        gz[:, lanes(q)] = (gg * y * sig * (1.0 + zq * (1.0 - sig))).astype(BF16)
        gy = gg * gate
        shared.append(
            [jnp.sum(scaled * gated, axis=0, keepdims=True), jnp.sum(gy * xq, axis=0, keepdims=True)]
        )
        dots += head_sums(gy * (y - d[q] * xq))
        gh, gl = split(gy)
        inner = []
        for h in range(HP):
            r = q * HP + h
            sl = slice(h * PC, (h + 1) * PC)
            dmixed = mm(gh[:, sl], xb[:, sl], NT) + mm(gl[:, sl], xb[:, sl], NT)
            dscores = dscores + decays(logs, cols, r, lower) * dmixed * step[r : r + 1]
            diff = logs[r : r + 1] - cols[:, r : r + 1]
            mixed_t = jnp.where(upper, jnp.exp(jnp.where(upper, diff, 0.0)), 0.0) * scores_t
            mh, ml = split(mixed_t)
            inner.append(mm(mh, gh[:, sl]) + (mm(mh, gl[:, sl]) + mm(ml, gh[:, sl])))
        v = jnp.concatenate(inner, axis=1)
        gx_out[:, lanes(q)] = pair_cols(cols, q, 2 * HD) * v + d[q] * gy
        xv += head_sums(xq * v)
        eg = pair_cols(cols, q, HD) * gy
        dc = dc + mm_both(eg, enter[q], NT)
        send[q, :NS, :] = mm_right(c_t, eg)
        leaving = decay[q] * enter[q] + own[q, :NS, :]
        send[q, NS : 2 * NS, :] = near[q] * leaving - mm_right(b_t, xq * pair_cols(cols, q, 3 * HD))
    maps[0] = mm_left(dscores.T, c[...])
    maps[1] = dc + mm_left(dscores, b[...])
    xv = rows_of(xv)
    after = (iota((CHUNK, CHUNK), 0) >= iota((CHUNK, CHUNK), 1)).astype(F32)
    dla = jnp.dot(rows_of(dots) - step * xv, after, precision=lax.Precision.HIGHEST, preferred_element_type=F32)
    small[:HD] = dla
    small[HD:] = xv
    decayed = dla * la
    for q in range(GROUP):
        rows = shared[q] + [one(decayed[q * HP : (q + 1) * HP]), jnp.zeros((5, WIDE), F32)]
        send[q, 2 * NS :, :] = jnp.concatenate(rows, axis=0)


def group_back_body(got, own, back, send):
    grad = got[GROUP - 1, :NS, :]
    tangent = got[GROUP - 1, NS : 2 * NS, :]
    reach = own[GROUP - 1, NS : NS + 1, :]
    back[GROUP - 1] = jnp.zeros((NS, WIDE), F32)
    extra = got[GROUP - 1, 2 * NS : 2 * NS + 3, :]
    cross = jnp.zeros((1, WIDE), F32)
    for k in reversed(range(GROUP - 1)):
        q = got[k, NS : 2 * NS, :]
        back[k] = grad
        cross = cross + jnp.sum(grad * q, axis=0, keepdims=True)
        tangent = tangent + reach * q
        extra = extra + got[k, 2 * NS : 2 * NS + 3, :]
        decay = own[k, NS : NS + 1, :]
        reach = reach * decay
        grad = decay * grad + got[k, :NS, :]
    laps = send.shape[0]
    rows = NS // laps
    to_slices(send, 0, grad)
    to_slices(send, rows, tangent)
    tail = jnp.concatenate([two(extra[:1]), two(extra[1:2]), two(extra[2:] + cross)], axis=1)
    for lap in range(laps):
        send[lap, :, 2 * rows * PC :] = tail


def leave_body(late, done, back, own, send, flat):
    from_slices(late, flat)
    grad = flat[...]
    alog = done[:, 2 * PC :]
    at = late.shape[2] - PC
    for lap in range(late.shape[0]):
        alog = alog + late[lap, :, at:]
    extra = jnp.concatenate(
        [one(done[:, :PC]), one(done[:, PC : 2 * PC]), one(alog), jnp.zeros((5, WIDE), F32)], axis=0
    )
    reach = jnp.ones((1, WIDE), F32)
    for k in reversed(range(GROUP)):
        send[k, :NS, :] = back[k] + reach * grad
        send[k, NS:, :] = extra
        reach = reach * own[k, NS : NS + 1, :]


def input_back_body(x, b, tok, gx_in, small, maps, enter, own, late, gx, ddt, gain, alog, skip, send):
    raw, step, rate = table(tok, T_RAW), table(tok, T_STEP), table(tok, T_RATE)
    logs = table(tok, T_LOGS)
    total = last(logs)
    cols = columns(jnp.exp(total - logs), step)
    decay = lanes_of(jnp.exp(total))
    db = maps[0]
    ends, xv = [], []
    lane = iota((1, HD), 1)
    a = jnp.zeros((1, HD), F32)
    s = jnp.zeros((1, HD), F32)
    for q in range(GROUP):
        grad = late[q, :NS, :]
        xq = x[:, lanes(q)].astype(F32)
        tail = pair_cols(cols, q)
        stepc = pair_cols(cols, q, HD)
        gh, gl = split(grad)
        v = tail * (mm(b[...], gh) + mm(b[...], gl))
        gx[:, lanes(q)] = (gx_in[:, lanes(q)] + stepc * v).astype(BF16)
        sh, sl = split(tail * stepc * xq)
        db = db + (mm(sh, gh, NT) + (mm(sh, gl, NT) + mm(sl, gh, NT)))
        xv += head_sums(xq * v)
        leaving = decay[q] * enter[q] + own[q, :NS, :]
        ends += [jnp.sum(e, axis=0, keepdims=True) for e in head_sums(grad * leaving)]
        gain[:, lanes(q)] = late[q, NS : NS + 1, :]
        for h in range(HP):
            here = lane == q * HP + h
            sl = slice(h * PC, (h + 1) * PC)
            s = s + jnp.where(here, jnp.sum(late[q, NS + 1 : NS + 2, sl], axis=1, keepdims=True), 0.0)
            a = a + jnp.where(here, jnp.sum(late[q, NS + 2 : NS + 3, sl], axis=1, keepdims=True), 0.0)
    alog[...] = a
    skip[...] = s
    xv = rows_of(xv)
    after = (iota((CHUNK, CHUNK), 0) >= iota((CHUNK, CHUNK), 1)).astype(F32)
    dla = jnp.dot(-step * xv, after, precision=lax.Precision.HIGHEST, preferred_element_type=F32)
    dla = small[:HD] + dla + jnp.concatenate(ends, axis=0)
    ddt[...] = (dla * rate + small[HD:] + xv) * sigmoid(raw)
    ranks = send.shape[0]
    rows = CHUNK // ranks
    for j in range(ranks):
        send[j, :rows, :] = db[j * rows : (j + 1) * rows]
        send[j, rows:, :] = maps[1, j * rows : (j + 1) * rows, :]


def sum_body(got, out):
    total = got[0]
    for q in range(1, got.shape[0]):
        total = total + got[q]
    out[...] = jnp.broadcast_to(total[None], out.shape)


def maps_body(got, db, dc):
    ranks = got.shape[0]
    rows = CHUNK // ranks
    for i in range(ranks):
        db[i * rows : (i + 1) * rows, :] = got[i, :rows, :]
        dc[i * rows : (i + 1) * rows, :] = got[i, rows:, :]


def call(body, ins, outs, scratch=(), limit=LIMIT):
    out = pl.pallas_call(
        body,
        in_specs=ins,
        out_specs=[VMEM] * len(outs),
        out_shape=[jax.ShapeDtypeStruct(s, t) for s, t in outs],
        scratch_shapes=scratch,
        compiler_params=pltpu.CompilerParams(vmem_limit_bytes=limit),
    )
    return out


def swap(a, axis):
    return lax.all_to_all(a, axis, 0, 0, tiled=True)


def shards(
    grad_full, keep, router_score, x_in, z_in, b_in, c_in, dt_raw, dt_bias, a_log, d_skip, norm_gain, state_in,
):
    laps = lax.axis_size("z")
    ranks = lax.axis_size("head")
    heads = dt_raw.shape[1]
    width = x_in.shape[1]
    total_width = width * ranks
    block_len = grad_full.shape[0] // keep.shape[0]
    states = ((GROUP, NS, WIDE), F32)
    slab = ((CHUNK, width), F32)
    tile = NS // laps * PC
    bind = functools.partial
    dma = pltpu.SemaphoreType.DMA
    router = router_score.reshape(1, CHUNK)
    gain = norm_gain.reshape(1, width)
    flat = pltpu.VMEM((NS, WIDE), F32)

    own, tok = call(
        own_state_body, [ANY] * 6, [((GROUP, ROWS_S, WIDE), F32), ((ROWS_T, CHUNK), F32)],
        [
            pltpu.VMEM((CHUNK, width), BF16), pltpu.VMEM((CHUNK, NS), BF16), pltpu.VMEM((heads, CHUNK), F32),
            pltpu.SMEM((heads,), F32), pltpu.SMEM((heads,), F32), pltpu.SMEM((heads,), F32), dma((6,)),
        ], FULL,
    )(x_in, b_in, dt_raw.T, dt_bias, a_log, d_skip)
    group = swap(own, "y")
    part, send, up = call(
        bind(group_state_body, block_len), [VMEM] * 3, [states, ((laps, HP, tile + PC), F32), slab]
    )(group, grad_full, keep)
    send, decay = call(
        scan_body, [VMEM] * 2, [((laps, HP, tile), F32), ((laps, HP, PC), F32)],
        [pltpu.VMEM((NS, PC), F32), pltpu.VMEM((HP, tile), F32)],
    )(swap(send, "z"), state_in)
    (enter,) = call(enter_body, [VMEM] * 3, [states], [flat])(swap(send, "z"), group, part)
    enter = swap(enter, "y")

    y, stats = call(output_body, [VMEM] * 8, [slab, ((ranks, 8, CHUNK), F32)])(
        x_in, b_in, c_in, z_in, up, gain, tok, enter
    )
    grad_z, gx, send, small, maps, router_grad = call(
        bind(output_back_body, total_width), [VMEM] * 12,
        [
            ((CHUNK, width), BF16), slab, ((GROUP, ROWS_G, WIDE), F32), ((2 * HD, CHUNK), F32),
            ((2, CHUNK, NS), F32), ((1, CHUNK), F32),
        ],
    )(swap(stats, "head"), x_in, b_in, c_in, z_in, up, gain, router, tok, enter, own, y)
    back, send = call(group_back_body, [VMEM] * 2, [states, ((laps, HP, 2 * tile + 3 * PC), F32)])(
        swap(send, "y"), group
    )
    send, done = call(scan_back_body, [VMEM] * 2, [((laps, HP, tile + PC), F32), ((HP, 3 * PC), F32)])(
        swap(send, "z"), decay
    )
    (late,) = call(leave_body, [VMEM] * 4, [((GROUP, ROWS_S, WIDE), F32)], [flat])(
        swap(send, "z"), done, back, group
    )
    piece = ((ranks, 2 * CHUNK // ranks, NS), F32)
    grad_x, ddt, grad_gain, grad_alog, grad_skip, send = call(
        input_back_body, [VMEM] * 9,
        [
            ((CHUNK, width), BF16), ((heads, CHUNK), F32), ((1, width), F32), ((1, heads), F32),
            ((1, heads), F32), piece,
        ],
    )(x_in, b_in, tok, gx, small, maps, enter, own, swap(late, "y"))
    (send,) = call(sum_body, [VMEM], [piece])(swap(send, "head"))
    grad_b, grad_c = call(maps_body, [VMEM], [((CHUNK, NS), F32)] * 2)(swap(send, "head"))
    return (
        grad_x,
        grad_z,
        grad_b,
        grad_c,
        ddt.T,
        router_grad.reshape(CHUNK),
        grad_gain.reshape(width),
        grad_alog.reshape(heads),
        grad_skip.reshape(heads),
    )


def solution(mesh):
    count, heads = mesh.devices.shape
    inner = Mesh(mesh.devices.reshape(count // GROUP, GROUP, heads), ("z", "y", "head"))
    seq = ("z", "y")
    in_specs = (
        P(seq, "head"),
        P(seq, None),
        P(seq),
        P(seq, "head"),
        P(seq, "head"),
        P(seq, None),
        P(seq, None),
        P(seq, "head"),
        P("head"),
        P("head"),
        P("head"),
        P("head"),
        P("head", None, None),
    )
    out_specs = (
        P(seq, "head"),
        P(seq, "head"),
        P(seq, None),
        P(seq, None),
        P(seq, "head"),
        P(seq),
        P("head"),
        P("head"),
        P("head"),
    )
    return jax.shard_map(shards, mesh=inner, in_specs=in_specs, out_specs=out_specs, check_vma=False)
```

time: 188 us -> 184 us (0.979)
  blocking collectives: 174 us -> 170 us
  Pallas kernels: 13 us -> 11 us
    all_to_all x11, blocking collectives: 174 us -> 170 us  [swap(): return lax.all_to_all(a, axis, 0, 0, tiled=True)]
    pallas_call x10, Pallas kernels: 12.4 us -> 10.3 us  [the longest x1 2.88 us: shards(): call(bind(output_back_body, total_width), [VMEM] * 12, [((CHUNK, width),...]
where the time goes in v3:
time: 184 us; the launch traced here: 183 us
  blocking collectives  170 us (92%)
  Pallas kernels  11 us (6%)
    all_to_all x11, blocking collectives, swap(): return lax.all_to_all(a, axis, 0, 0, tiled=True)  170 us

profile of v3, /device:TPU:1, one launch (start us, length us, event | category | flops | bytes accessed | tf_op | source)
XLA Modules:
  0.0 183.2 jit_solution(8643578921290226324)
XLA Ops:
  0.7 2.8 %shard_map.196 = (f32[4,136,256]{2,1,0:T(8,128)}, f32[48,128]{1,0:T(8,128)}) custom-call(bf16[128,1024]{1,0:T(8,128)(2,1)} %x.5, bf16[128,128]{1,0:T(8,128)(2,1)} %b.5, f32[8,128]{1,0:T(8,128)} %bitcast.11, f32[8]{0:T(128)} %bias_hbm.1, f32[8]{0:T(128)} %alog_hbm.1, f32[8]{0:T(128)} %skip_hbm.1), custom_call_target="tpu_custom_call" | custom-call | tf_op jit(solution)/shard_map/pallas_call | solution.py:490
  3.5 12.1 %all_to_all.55.got.own = f32[4,136,256]{2,1,0:T(8,128)S(1)} all-to-all(f32[4,136,256]{2,1,0:T(8,128)} %get-tuple-element.37.own), channel_id=1, replica_groups=mesh['z'=16,'y'=4,'head'=8] {'y'}, dimensions={0} | all-to-all | bytes 1114112 | tf_op jit(solution)/shard_map/all_to_all | solution.py:469
  15.6 1.6 copy-done.2
  17.2 0.9 shard_map.197
  18.1 28.4 %all_to_all.56.got = f32[16,2,1152]{2,1,0:T(2,128)S(1)} all-to-all(f32[16,2,1152]{2,1,0:T(2,128)S(1)} %get-tuple-element.39), channel_id=1, replica_groups=mesh['z'=16,'y'=4,'head'=8] {'z'}, dimensions={0} | all-to-all | bytes 294912 | tf_op jit(solution)/shard_map/all_to_all | solution.py:469
  46.5 0.2 shard_map.198
  46.7 16.8 %all_to_all.57.got = f32[16,2,1024]{2,1,0:T(2,128)S(1)} all-to-all(f32[16,2,1024]{2,1,0:T(2,128)S(1)} %get-tuple-element.40), channel_id=1, replica_groups=mesh['z'=16,'y'=4,'head'=8] {'z'}, dimensions={0} | all-to-all | bytes 262144 | tf_op jit(solution)/shard_map/all_to_all | solution.py:469
  63.5 0.0 copy-start.8
  63.5 0.1 shard_map.199
  63.6 9.7 %all_to_all.58.enter = f32[4,128,256]{2,1,0:T(8,128)S(1)} all-to-all(f32[4,128,256]{2,1,0:T(8,128)S(1)} %shard_map.199), channel_id=1, replica_groups=mesh['z'=16,'y'=4,'head'=8] {'y'}, dimensions={0} | all-to-all | bytes 1048576 | tf_op jit(solution)/shard_map/all_to_all | solution.py:469
  73.3 1.0 shard_map.200
  74.4 14.2 %all_to_all.59.stats = f32[8,8,128]{2,1,0:T(8,128)S(1)} all-to-all(f32[8,8,128]{2,1,0:T(8,128)S(1)} %get-tuple-element.42), channel_id=1, replica_groups=mesh['z'=16,'y'=4,'head'=8] {'head'}, dimensions={0} | all-to-all | bytes 65536 | tf_op jit(solution)/shard_map/all_to_all | solution.py:469
  88.6 2.9 %shard_map.201 = (bf16[128,1024]{1,0:T(8,128)(2,1)}, f32[128,1024]{1,0:T(8,128)S(1)}, f32[4,264,256]{2,1,0:T(8,128)S(1)}, f32[16,128]{1,0:T(8,128)S(1)}, f32[2,128,128]{2,1,0:T(8,128)S(1)}, /*index=5*/f32[1,128]{1,0:T(1,128)}) custom-call(f32[8,8,128]{2,1,0:T(8,128)S(1)} %all_to_all.59.stats, bf16[128,1024]{1,0:T(8,128)(2,1)S(1)} %copy-done.1, ...), custom_call_target="tpu_custom_call" | custom-call | tf_op jit(solution)/shard_map/pallas_call | solution.py:511
  91.4 17.2 %all_to_all.60.got = f32[4,264,256]{2,1,0:T(8,128)S(1)} all-to-all(f32[4,264,256]{2,1,0:T(8,128)S(1)} %get-tuple-element.47), channel_id=1, replica_groups=mesh['z'=16,'y'=4,'head'=8] {'y'}, dimensions={0} | all-to-all | bytes 2162688 | tf_op jit(solution)/shard_map/all_to_all | solution.py:469
  108.6 0.2 shard_map.202
  108.8 16.8 %all_to_all.61.got = f32[16,2,2432]{2,1,0:T(2,128)S(1)} all-to-all(f32[16,2,2432]{2,1,0:T(2,128)S(1)} %get-tuple-element.48), channel_id=1, replica_groups=mesh['z'=16,'y'=4,'head'=8] {'z'}, dimensions={0} | all-to-all | bytes 622592 | tf_op jit(solution)/shard_map/all_to_all | solution.py:469
  125.6 0.1 shard_map.203
  125.8 24.0 %all_to_all.62.late = f32[16,2,1152]{2,1,0:T(2,128)S(1)} all-to-all(f32[16,2,1152]{2,1,0:T(2,128)S(1)} %get-tuple-element.50), channel_id=1, replica_groups=mesh['z'=16,'y'=4,'head'=8] {'z'}, dimensions={0} | all-to-all | bytes 294912 | tf_op jit(solution)/shard_map/all_to_all | solution.py:469
  149.8 0.2 shard_map.204
  149.9 9.5 %all_to_all.63.late = f32[4,136,256]{2,1,0:T(8,128)S(1)} all-to-all(f32[4,136,256]{2,1,0:T(8,128)S(1)} %shard_map.204), channel_id=1, replica_groups=mesh['z'=16,'y'=4,'head'=8] {'y'}, dimensions={0} | all-to-all | bytes 1114112 | tf_op jit(solution)/shard_map/all_to_all | solution.py:469
  159.4 1.9 %shard_map.205 = (bf16[128,1024]{1,0:T(8,128)(2,1)}, f32[8,128]{1,0:T(8,128)}, f32[1,1024]{1,0:T(1,128)}, f32[1,8]{1,0:T(1,128)}, f32[1,8]{1,0:T(1,128)}, /*index=5*/f32[8,32,128]{2,1,0:T(8,128)S(1)}) custom-call(bf16[128,1024]{1,0:T(8,128)(2,1)S(1)} %copy-done.1, bf16[128,128]{1,0:T(8,128)(2,1)S(1)} %copy-done.4, f32[48,128]{1,0:T(8,128)S(1)} %copy-done.6, ...), custom_call_target="tpu_custom_call" | custom-call | tf_op jit(solution)/shard_map/pallas_call | solution.py:528
  161.3 12.7 %all_to_all.64.got = f32[8,32,128]{2,1,0:T(8,128)S(1)} all-to-all(f32[8,32,128]{2,1,0:T(8,128)S(1)} %get-tuple-element.55), channel_id=1, replica_groups=mesh['z'=16,'y'=4,'head'=8] {'head'}, dimensions={0} | all-to-all | bytes 262144 | tf_op jit(solution)/shard_map/all_to_all | solution.py:469
  174.0 8.5 %all_to_all.65.got = f32[8,32,128]{2,1,0:T(8,128)S(1)} all-to-all(f32[8,32,128]{2,1,0:T(8,128)S(1)} %shard_map.206), channel_id=1, replica_groups=mesh['z'=16,'y'=4,'head'=8] {'head'}, dimensions={0} | all-to-all | bytes 262144 | tf_op jit(solution)/shard_map/all_to_all | solution.py:469
  182.6 0.7 shard_map.207
  (21 shorter events, 0.1 us)
Async XLA Ops:
  0.6 14.9 %copy-start.9 = (s32[8,16]{1,0:T(8,128)S(1)}, s32[8,16]{1,0:T(8,128)}, u32[]{:S(2)}) copy-start(s32[8,16]{1,0:T(8,128)} %keep.1) | copy-start | bytes 1540
  15.6 1.6 copy-start.2
  17.2 29.3 %copy-start.5 = (f32[8,128,128]{2,1,0:T(8,128)S(1)}, f32[8,128,128]{2,1,0:T(8,128)}, u32[]{:S(2)}) copy-start(f32[8,128,128]{2,1,0:T(8,128)} %state_in.1) | copy-start | bytes 1572868
  63.5 9.8 %copy-start.1 = (bf16[128,1024]{1,0:T(8,128)(2,1)S(1)}, bf16[128,1024]{1,0:T(8,128)(2,1)}, u32[]{:S(2)}) copy-start(bf16[128,1024]{1,0:T(8,128)(2,1)} %x.5) | copy-start | bytes 786436
  63.5 9.8 %copy-start.3 = (bf16[128,1024]{1,0:T(8,128)(2,1)S(1)}, bf16[128,1024]{1,0:T(8,128)(2,1)}, u32[]{:S(2)}) copy-start(bf16[128,1024]{1,0:T(8,128)(2,1)} %z.3) | copy-start | bytes 786436
  63.5 9.8 %copy-start.4 = (bf16[128,128]{1,0:T(8,128)(2,1)S(1)}, bf16[128,128]{1,0:T(8,128)(2,1)}, u32[]{:S(2)}) copy-start(bf16[128,128]{1,0:T(8,128)(2,1)} %b.5) | copy-start | bytes 98308
  63.5 9.9 %copy-start.6 = (f32[48,128]{1,0:T(8,128)S(1)}, f32[48,128]{1,0:T(8,128)}, u32[]{:S(2)}) copy-start(f32[48,128]{1,0:T(8,128)} %get-tuple-element.36.tok) | copy-start | bytes 73732
  63.5 9.9 %copy-start.7 = (bf16[128,128]{1,0:T(8,128)(2,1)S(1)}, bf16[128,128]{1,0:T(8,128)(2,1)}, u32[]{:S(2)}) copy-start(bf16[128,128]{1,0:T(8,128)(2,1)} %c.3) | copy-start | bytes 98308
  63.5 9.9 %copy-start.8 = (f32[1024]{0:T(1024)S(1)}, f32[1024]{0:T(1024)}, u32[]{:S(2)}) copy-start(f32[1024]{0:T(1024)} %param.24) | copy-start | bytes 12292
  73.3 15.3 %copy-start = (f32[4,136,256]{2,1,0:T(8,128)S(1)}, f32[4,136,256]{2,1,0:T(8,128)}, u32[]{:S(2)}) copy-start(f32[4,136,256]{2,1,0:T(8,128)} %get-tuple-element.37.own) | copy-start | bytes 1671172
  73.3 15.3 %copy-start.10 = (f32[128]{0:T(128)S(1)}, f32[128]{0:T(128)}, u32[]{:S(2)}) copy-start(f32[128]{0:T(128)} %param.15) | copy-start | bytes 1540

commit v4 on v3

--- a/solution.py
+++ b/solution.py
@@ -121,6 +121,14 @@
     return [jnp.sum(a[:, h * PC : (h + 1) * PC], axis=1, keepdims=True) for h in range(HP)]
 
 
+def whole_sums(a):
+    return [jnp.sum(s, axis=0, keepdims=True) for s in head_sums(a)]
+
+
+def halved(a, b):
+    return jnp.where(iota((1, WIDE), 1) % PC < PC // 2, a, b)
+
+
 def two(row):
     return jnp.concatenate([row[:, :PC], row[:, PC:]], axis=0)
 
@@ -134,15 +142,17 @@
 
 
 def own_state_body(
-    x_hbm, b_hbm, dt_hbm, bias_hbm, alog_hbm, skip_hbm, send, tok, x, b, dt_t, bias, alog, skip, sem
+    x_hbm, b_hbm, dt_hbm, bias_hbm, alog_hbm, skip_hbm, send_hbm, tok, x, b, dt_t, bias, alog, skip, send, sem, quarter
 ):
     copies = [
         pltpu.make_async_copy(src, dst, sem.at[i])
         for i, (src, dst) in enumerate(
-            [(dt_hbm, dt_t), (bias_hbm, bias), (alog_hbm, alog), (skip_hbm, skip), (b_hbm, b), (x_hbm, x)]
+            [(dt_hbm, dt_t), (bias_hbm, bias), (alog_hbm, alog), (skip_hbm, skip), (b_hbm, b)]
         )
     ]
-    for copy in copies:
+    loads = [pltpu.make_async_copy(x_hbm.at[:, lanes(q)], x.at[:, lanes(q)], quarter.at[0, q]) for q in range(GROUP)]
+    stores = [pltpu.make_async_copy(send.at[q], send_hbm.at[q], quarter.at[1, q]) for q in range(GROUP)]
+    for copy in copies + loads:
         copy.start()
     for copy in copies:
         copy.wait()
@@ -160,8 +170,12 @@
     decay = lanes_of(jnp.exp(last(logs)))
     b_t = b[...].astype(F32).T.astype(BF16)
     for q in range(GROUP):
+        loads[q].wait()
         send[q, :NS, :] = mm_right(b_t, x[:, lanes(q)].astype(F32) * pair_cols(cols, q))
         send[q, NS:, :] = jnp.broadcast_to(decay[q], (8, WIDE))
+        stores[q].start()
+    for q in range(GROUP):
+        stores[q].wait()
 
 
 def to_slices(out, at, state):
@@ -179,7 +193,7 @@
             out[n : n + 1, h * PC : (h + 1) * PC] = ref[n // rows, h : h + 1, tile]
 
 
-def group_state_body(block_len, got, grad_full, keep, part, send, up):
+def group_state_body(got, part, send):
     state = got[0, :NS, :]
     whole = got[0, NS : NS + 1, :]
     part[0] = state
@@ -191,12 +205,6 @@
     to_slices(send, 0, state)
     for lap in range(send.shape[0]):
         send[lap, :, send.shape[2] - PC :] = two(whole)
-    blocks, kept = keep.shape
-    for i in range(blocks):
-        pick = (iota((kept, block_len), 1) == keep[i : i + 1, :].T).astype(BF16)
-        up[i * kept : (i + 1) * kept, :] = mm(pick, grad_full[i * block_len : (i + 1) * block_len, :])
-
-
 def spread(row, count):
     return jnp.concatenate([row] * count, axis=1)
 
@@ -223,7 +231,7 @@
     rows = lanes // PC
     state = jnp.zeros((HP, lanes), F32)
     cross = jnp.zeros((HP, lanes), F32)
-    total = jnp.zeros((HP, 3 * PC), F32)
+    total = jnp.zeros((HP, 2 * PC), F32)
     for lap in reversed(range(laps)):
         out[lap, :, :lanes] = state
         cross = cross + state * got[lap, :, lanes : 2 * lanes]
@@ -252,7 +260,11 @@
     return jnp.where(lower, jnp.exp(jnp.where(lower, diff, 0.0)), 0.0)
 
 
-def output_body(x, b, c, z, up, gain, tok, enter, y_out, stats):
+def output_body(block_len, x, b, c, z, grad_full, keep, gain, tok, enter, y_out, up, stats):
+    blocks, kept = keep.shape
+    for i in range(blocks):
+        pick = (iota((kept, block_len), 1) == keep[i : i + 1, :].T).astype(BF16)
+        up[i * kept : (i + 1) * kept, :] = mm(pick, grad_full[i * block_len : (i + 1) * block_len, :])
     logs, step = table(tok, T_LOGS), table(tok, T_STEP)
     cols = columns(logs, jnp.exp(logs))
     lower = iota((CHUNK, CHUNK), 0) >= iota((CHUNK, CHUNK), 1)
@@ -273,17 +285,16 @@
         gated = y * zq * sigmoid(zq)
         squares = squares + jnp.sum(gated * gated, axis=1, keepdims=True)
         crosses = crosses + jnp.sum(up[:, lanes(q)] * gated * gain[:, lanes(q)], axis=1, keepdims=True)
-    tile = jnp.concatenate([rows_of([squares, crosses]), jnp.zeros((6, CHUNK), F32)], axis=0)
-    stats[...] = jnp.broadcast_to(tile[None], stats.shape)
+    stats[...] = jnp.broadcast_to(rows_of([squares, crosses])[None], stats.shape)
 
 
 def output_back_body(
     total_width, stats, x, b, c, z, up, gain, router, tok, enter, own, y_in,
     gz, gx_out, send, small, maps, router_grad,
 ):
-    sums = stats[0, :2, :]
+    sums = stats[0]
     for i in range(1, stats.shape[0]):
-        sums = sums + stats[i, :2, :]
+        sums = sums + stats[i]
     rstd = lax.rsqrt(sums[:1] / total_width + EPS)
     cross = sums[1:]
     router_grad[...] = rstd * cross
@@ -305,7 +316,7 @@
     c_t = c[...].astype(F32).T.astype(BF16)
     dscores = jnp.zeros((CHUNK, CHUNK), F32)
     dc = jnp.zeros((CHUNK, NS), F32)
-    dots, xv, shared = [], [], []
+    dots, xv, shared, skips = [], [], [], []
     for q in range(GROUP):
         xb = x[:, lanes(q)]
         xq, zq, u, y = xb.astype(F32), z[:, lanes(q)].astype(F32), up[:, lanes(q)], y_in[:, lanes(q)]
@@ -316,9 +327,8 @@
         gg = scaled * gain[:, lanes(q)] - gated * cols[:, at_a + 1 : at_a + 2]
         gz[:, lanes(q)] = (gg * y * sig * (1.0 + zq * (1.0 - sig))).astype(BF16)
         gy = gg * gate
-        shared.append(
-            [jnp.sum(scaled * gated, axis=0, keepdims=True), jnp.sum(gy * xq, axis=0, keepdims=True)]
-        )
+        shared.append(jnp.sum(scaled * gated, axis=0, keepdims=True))
+        skips += whole_sums(gy * xq)
         dots += head_sums(gy * (y - d[q] * xq))
         gh, gl = split(gy)
         inner = []
@@ -346,10 +356,11 @@
     dla = jnp.dot(rows_of(dots) - step * xv, after, precision=lax.Precision.HIGHEST, preferred_element_type=F32)
     small[:HD] = dla
     small[HD:] = xv
-    decayed = dla * la
+    alogs = jnp.sum(dla * la, axis=1, keepdims=True)
     for q in range(GROUP):
-        rows = shared[q] + [one(decayed[q * HP : (q + 1) * HP]), jnp.zeros((5, WIDE), F32)]
-        send[q, 2 * NS :, :] = jnp.concatenate(rows, axis=0)
+        r = q * HP
+        row = halved(pair(skips[r], skips[r + 1], 1), pair(alogs[r : r + 1], alogs[r + 1 : r + 2], 1))
+        send[q, 2 * NS :, :] = jnp.concatenate([shared[q], row, jnp.zeros((6, WIDE), F32)], axis=0)
 
 
 def group_back_body(got, own, back, send):
@@ -357,14 +368,14 @@
     tangent = got[GROUP - 1, NS : 2 * NS, :]
     reach = own[GROUP - 1, NS : NS + 1, :]
     back[GROUP - 1] = jnp.zeros((NS, WIDE), F32)
-    extra = got[GROUP - 1, 2 * NS : 2 * NS + 3, :]
+    extra = got[GROUP - 1, 2 * NS : 2 * NS + 2, :]
     cross = jnp.zeros((1, WIDE), F32)
     for k in reversed(range(GROUP - 1)):
         q = got[k, NS : 2 * NS, :]
         back[k] = grad
         cross = cross + jnp.sum(grad * q, axis=0, keepdims=True)
         tangent = tangent + reach * q
-        extra = extra + got[k, 2 * NS : 2 * NS + 3, :]
+        extra = extra + got[k, 2 * NS : 2 * NS + 2, :]
         decay = own[k, NS : NS + 1, :]
         reach = reach * decay
         grad = decay * grad + got[k, :NS, :]
@@ -372,7 +383,9 @@
     rows = NS // laps
     to_slices(send, 0, grad)
     to_slices(send, rows, tangent)
-    tail = jnp.concatenate([two(extra[:1]), two(extra[1:2]), two(extra[2:] + cross)], axis=1)
+    cross = head_sums(cross)
+    scalars = extra[1:] + halved(jnp.zeros((1, WIDE), F32), pair(cross[0], cross[1], 1))
+    tail = jnp.concatenate([two(extra[:1]), two(scalars)], axis=1)
     for lap in range(laps):
         send[lap, :, 2 * rows * PC :] = tail
 
@@ -380,12 +393,15 @@
 def leave_body(late, done, back, own, send, flat):
     from_slices(late, flat)
     grad = flat[...]
-    alog = done[:, 2 * PC :]
     at = late.shape[2] - PC
-    for lap in range(late.shape[0]):
+    alog = late[0, :, at:]
+    for lap in range(1, late.shape[0]):
         alog = alog + late[lap, :, at:]
+    alog = jnp.sum(alog, axis=1, keepdims=True) + done[:, 2 * PC - 1 :]
+    skip = done[:, PC : PC + 1]
     extra = jnp.concatenate(
-        [one(done[:, :PC]), one(done[:, PC : 2 * PC]), one(alog), jnp.zeros((5, WIDE), F32)], axis=0
+        [one(done[:, :PC]), pair(skip[:1], skip[1:], 1), pair(alog[:1], alog[1:], 1), jnp.zeros((5, WIDE), F32)],
+        axis=0,
     )
     reach = jnp.ones((1, WIDE), F32)
     for k in reversed(range(GROUP)):
@@ -417,13 +433,12 @@
         db = db + (mm(sh, gh, NT) + (mm(sh, gl, NT) + mm(sl, gh, NT)))
         xv += head_sums(xq * v)
         leaving = decay[q] * enter[q] + own[q, :NS, :]
-        ends += [jnp.sum(e, axis=0, keepdims=True) for e in head_sums(grad * leaving)]
+        ends += whole_sums(grad * leaving)
         gain[:, lanes(q)] = late[q, NS : NS + 1, :]
         for h in range(HP):
             here = lane == q * HP + h
-            sl = slice(h * PC, (h + 1) * PC)
-            s = s + jnp.where(here, jnp.sum(late[q, NS + 1 : NS + 2, sl], axis=1, keepdims=True), 0.0)
-            a = a + jnp.where(here, jnp.sum(late[q, NS + 2 : NS + 3, sl], axis=1, keepdims=True), 0.0)
+            s = jnp.where(here, late[q, NS + 1 : NS + 2, h * PC : h * PC + 1], s)
+            a = jnp.where(here, late[q, NS + 2 : NS + 3, h * PC : h * PC + 1], a)
     alog[...] = a
     skip[...] = s
     xv = rows_of(xv)
@@ -453,11 +468,11 @@
         dc[i * rows : (i + 1) * rows, :] = got[i, rows:, :]
 
 
-def call(body, ins, outs, scratch=(), limit=LIMIT):
+def call(body, ins, outs, scratch=(), limit=LIMIT, places=None):
     out = pl.pallas_call(
         body,
         in_specs=ins,
-        out_specs=[VMEM] * len(outs),
+        out_specs=places or [VMEM] * len(outs),
         out_shape=[jax.ShapeDtypeStruct(s, t) for s, t in outs],
         scratch_shapes=scratch,
         compiler_params=pltpu.CompilerParams(vmem_limit_bytes=limit),
@@ -491,13 +506,12 @@
         own_state_body, [ANY] * 6, [((GROUP, ROWS_S, WIDE), F32), ((ROWS_T, CHUNK), F32)],
         [
             pltpu.VMEM((CHUNK, width), BF16), pltpu.VMEM((CHUNK, NS), BF16), pltpu.VMEM((heads, CHUNK), F32),
-            pltpu.SMEM((heads,), F32), pltpu.SMEM((heads,), F32), pltpu.SMEM((heads,), F32), dma((6,)),
-        ], FULL,
+            pltpu.SMEM((heads,), F32), pltpu.SMEM((heads,), F32), pltpu.SMEM((heads,), F32),
+            pltpu.VMEM((GROUP, ROWS_S, WIDE), F32), dma((5,)), dma((2, GROUP)),
+        ], FULL, [ANY, VMEM],
     )(x_in, b_in, dt_raw.T, dt_bias, a_log, d_skip)
     group = swap(own, "y")
-    part, send, up = call(
-        bind(group_state_body, block_len), [VMEM] * 3, [states, ((laps, HP, tile + PC), F32), slab]
-    )(group, grad_full, keep)
+    part, send = call(group_state_body, [VMEM], [states, ((laps, HP, tile + PC), F32)])(group)
     send, decay = call(
         scan_body, [VMEM] * 2, [((laps, HP, tile), F32), ((laps, HP, PC), F32)],
         [pltpu.VMEM((NS, PC), F32), pltpu.VMEM((HP, tile), F32)],
@@ -505,8 +519,8 @@
     (enter,) = call(enter_body, [VMEM] * 3, [states], [flat])(swap(send, "z"), group, part)
     enter = swap(enter, "y")
 
-    y, stats = call(output_body, [VMEM] * 8, [slab, ((ranks, 8, CHUNK), F32)])(
-        x_in, b_in, c_in, z_in, up, gain, tok, enter
+    y, up, stats = call(bind(output_body, block_len), [VMEM] * 9, [slab, slab, ((ranks, 2, CHUNK), F32)])(
+        x_in, b_in, c_in, z_in, grad_full, keep, gain, tok, enter
     )
     grad_z, gx, send, small, maps, router_grad = call(
         bind(output_back_body, total_width), [VMEM] * 12,
@@ -515,10 +529,10 @@
             ((2, CHUNK, NS), F32), ((1, CHUNK), F32),
         ],
     )(swap(stats, "head"), x_in, b_in, c_in, z_in, up, gain, router, tok, enter, own, y)
-    back, send = call(group_back_body, [VMEM] * 2, [states, ((laps, HP, 2 * tile + 3 * PC), F32)])(
+    back, send = call(group_back_body, [VMEM] * 2, [states, ((laps, HP, 2 * tile + 2 * PC), F32)])(
         swap(send, "y"), group
     )
-    send, done = call(scan_back_body, [VMEM] * 2, [((laps, HP, tile + PC), F32), ((HP, 3 * PC), F32)])(
+    send, done = call(scan_back_body, [VMEM] * 2, [((laps, HP, tile + PC), F32), ((HP, 2 * PC), F32)])(
         swap(send, "z"), decay
     )
     (late,) = call(leave_body, [VMEM] * 4, [((GROUP, ROWS_S, WIDE), F32)], [flat])(

time: 184 us -> 183 us (level)
  no operation moved by 1% of the time
where the time goes in v4:
time: 183 us; the launch traced here: 182 us
  blocking collectives  169 us (92%)
  Pallas kernels  12.3 us (7%)
    all_to_all x11, blocking collectives, swap(): return lax.all_to_all(a, axis, 0, 0, tiled=True)  169 us
    pallas_call x1, Pallas kernels, shards(): call(own_state_body, [ANY] * 6, [((GROUP, ROWS_S, WIDE), F32), ((ROWS_T,...  3.91 us

profile of v4, /device:TPU:1, one launch (start us, length us, event | category | flops | bytes accessed | tf_op | source)
XLA Modules:
  0.0 182.4 jit_solution(17561598317904875367)
XLA Ops:
  0.7 3.9 %shard_map.196 = (f32[4,136,256]{2,1,0:T(8,128)}, f32[48,128]{1,0:T(8,128)}) custom-call(bf16[128,1024]{1,0:T(8,128)(2,1)} %x.5, bf16[128,128]{1,0:T(8,128)(2,1)} %b.5, f32[8,128]{1,0:T(8,128)} %bitcast.11, f32[8]{0:T(128)} %bias_hbm.1, f32[8]{0:T(128)} %alog_hbm.1, f32[8]{0:T(128)} %skip_hbm.1), custom_call_target="tpu_custom_call" | custom-call | tf_op jit(solution)/shard_map/pallas_call | solution.py:505
  4.6 12.1 %all_to_all.55.got.own = f32[4,136,256]{2,1,0:T(8,128)S(1)} all-to-all(f32[4,136,256]{2,1,0:T(8,128)} %get-tuple-element.37.own), channel_id=1, replica_groups=mesh['z'=16,'y'=4,'head'=8] {'y'}, dimensions={0} | all-to-all | bytes 1114112 | tf_op jit(solution)/shard_map/all_to_all | solution.py:484
  16.7 0.1 shard_map.197
  16.8 28.4 %all_to_all.56.got = f32[16,2,1152]{2,1,0:T(2,128)S(1)} all-to-all(f32[16,2,1152]{2,1,0:T(2,128)S(1)} %get-tuple-element.38), channel_id=1, replica_groups=mesh['z'=16,'y'=4,'head'=8] {'z'}, dimensions={0} | all-to-all | bytes 294912 | tf_op jit(solution)/shard_map/all_to_all | solution.py:484
  45.2 0.2 shard_map.198
  45.4 16.8 %all_to_all.57.got = f32[16,2,1024]{2,1,0:T(2,128)S(1)} all-to-all(f32[16,2,1024]{2,1,0:T(2,128)S(1)} %get-tuple-element.39), channel_id=1, replica_groups=mesh['z'=16,'y'=4,'head'=8] {'z'}, dimensions={0} | all-to-all | bytes 262144 | tf_op jit(solution)/shard_map/all_to_all | solution.py:484
  62.2 0.0 copy-start.7
  62.2 0.0 copy-start.8
  62.3 0.1 shard_map.199
  62.4 9.6 %all_to_all.58.enter = f32[4,128,256]{2,1,0:T(8,128)S(1)} all-to-all(f32[4,128,256]{2,1,0:T(8,128)S(1)} %shard_map.199), channel_id=1, replica_groups=mesh['z'=16,'y'=4,'head'=8] {'y'}, dimensions={0} | all-to-all | bytes 1048576 | tf_op jit(solution)/shard_map/all_to_all | solution.py:484
  72.1 1.6 shard_map.200
  73.7 14.1 %all_to_all.59.stats = f32[8,2,128]{2,1,0:T(2,128)S(1)} all-to-all(f32[8,2,128]{2,1,0:T(2,128)S(1)} %get-tuple-element.41), channel_id=1, replica_groups=mesh['z'=16,'y'=4,'head'=8] {'head'}, dimensions={0} | all-to-all | bytes 16384 | tf_op jit(solution)/shard_map/all_to_all | solution.py:484
  87.8 3.3 %shard_map.201 = (bf16[128,1024]{1,0:T(8,128)(2,1)}, f32[128,1024]{1,0:T(8,128)S(1)}, f32[4,264,256]{2,1,0:T(8,128)S(1)}, f32[16,128]{1,0:T(8,128)S(1)}, f32[2,128,128]{2,1,0:T(8,128)S(1)}, /*index=5*/f32[1,128]{1,0:T(1,128)}) custom-call(f32[8,2,128]{2,1,0:T(2,128)S(1)} %all_to_all.59.stats, bf16[128,1024]{1,0:T(8,128)(2,1)S(1)} %copy-done.1, ...), custom_call_target="tpu_custom_call" | custom-call | tf_op jit(solution)/shard_map/pallas_call | solution.py:525
  91.1 17.2 %all_to_all.60.got = f32[4,264,256]{2,1,0:T(8,128)S(1)} all-to-all(f32[4,264,256]{2,1,0:T(8,128)S(1)} %get-tuple-element.47), channel_id=1, replica_groups=mesh['z'=16,'y'=4,'head'=8] {'y'}, dimensions={0} | all-to-all | bytes 2162688 | tf_op jit(solution)/shard_map/all_to_all | solution.py:484
  108.3 0.2 shard_map.202
  108.5 16.5 %all_to_all.61.got = f32[16,2,2304]{2,1,0:T(2,128)S(1)} all-to-all(f32[16,2,2304]{2,1,0:T(2,128)S(1)} %get-tuple-element.48), channel_id=1, replica_groups=mesh['z'=16,'y'=4,'head'=8] {'z'}, dimensions={0} | all-to-all | bytes 589824 | tf_op jit(solution)/shard_map/all_to_all | solution.py:484
  125.0 0.1 shard_map.203
  125.2 23.8 %all_to_all.62.late = f32[16,2,1152]{2,1,0:T(2,128)S(1)} all-to-all(f32[16,2,1152]{2,1,0:T(2,128)S(1)} %get-tuple-element.50), channel_id=1, replica_groups=mesh['z'=16,'y'=4,'head'=8] {'z'}, dimensions={0} | all-to-all | bytes 294912 | tf_op jit(solution)/shard_map/all_to_all | solution.py:484
  148.9 0.2 shard_map.204
  149.1 9.5 %all_to_all.63.late = f32[4,136,256]{2,1,0:T(8,128)S(1)} all-to-all(f32[4,136,256]{2,1,0:T(8,128)S(1)} %shard_map.204), channel_id=1, replica_groups=mesh['z'=16,'y'=4,'head'=8] {'y'}, dimensions={0} | all-to-all | bytes 1114112 | tf_op jit(solution)/shard_map/all_to_all | solution.py:484
  158.6 1.8 %shard_map.205 = (bf16[128,1024]{1,0:T(8,128)(2,1)}, f32[8,128]{1,0:T(8,128)}, f32[1,1024]{1,0:T(1,128)}, f32[1,8]{1,0:T(1,128)}, f32[1,8]{1,0:T(1,128)}, /*index=5*/f32[8,32,128]{2,1,0:T(8,128)S(1)}) custom-call(bf16[128,1024]{1,0:T(8,128)(2,1)S(1)} %copy-done.1, bf16[128,128]{1,0:T(8,128)(2,1)S(1)} %copy-done.4, f32[48,128]{1,0:T(8,128)S(1)} %copy-done.6, ...), custom_call_target="tpu_custom_call" | custom-call | tf_op jit(solution)/shard_map/pallas_call | solution.py:542
  160.5 12.7 %all_to_all.64.got = f32[8,32,128]{2,1,0:T(8,128)S(1)} all-to-all(f32[8,32,128]{2,1,0:T(8,128)S(1)} %get-tuple-element.55), channel_id=1, replica_groups=mesh['z'=16,'y'=4,'head'=8] {'head'}, dimensions={0} | all-to-all | bytes 262144 | tf_op jit(solution)/shard_map/all_to_all | solution.py:484
  173.2 8.5 %all_to_all.65.got = f32[8,32,128]{2,1,0:T(8,128)S(1)} all-to-all(f32[8,32,128]{2,1,0:T(8,128)S(1)} %shard_map.206), channel_id=1, replica_groups=mesh['z'=16,'y'=4,'head'=8] {'head'}, dimensions={0} | all-to-all | bytes 262144 | tf_op jit(solution)/shard_map/all_to_all | solution.py:484
  181.7 0.7 shard_map.207
  (21 shorter events, 0.1 us)
Async XLA Ops:
  0.6 44.6 %copy-start.5 = (f32[8,128,128]{2,1,0:T(8,128)S(1)}, f32[8,128,128]{2,1,0:T(8,128)}, u32[]{:S(2)}) copy-start(f32[8,128,128]{2,1,0:T(8,128)} %state_in.1) | copy-start | bytes 1572868
  62.2 9.8 %copy-start.1 = (bf16[128,1024]{1,0:T(8,128)(2,1)S(1)}, bf16[128,1024]{1,0:T(8,128)(2,1)}, u32[]{:S(2)}) copy-start(bf16[128,1024]{1,0:T(8,128)(2,1)} %x.5) | copy-start | bytes 786436
  62.2 9.8 %copy-start.2 = (bf16[1024,1024]{1,0:T(8,128)(2,1)S(1)}, bf16[1024,1024]{1,0:T(8,128)(2,1)}, u32[]{:S(2)}) copy-start(bf16[1024,1024]{1,0:T(8,128)(2,1)} %grad_full.1) | copy-start | bytes 6291460
  62.2 9.8 %copy-start.3 = (bf16[128,1024]{1,0:T(8,128)(2,1)S(1)}, bf16[128,1024]{1,0:T(8,128)(2,1)}, u32[]{:S(2)}) copy-start(bf16[128,1024]{1,0:T(8,128)(2,1)} %z.3) | copy-start | bytes 786436
  62.2 9.9 %copy-start.4 = (bf16[128,128]{1,0:T(8,128)(2,1)S(1)}, bf16[128,128]{1,0:T(8,128)(2,1)}, u32[]{:S(2)}) copy-start(bf16[128,128]{1,0:T(8,128)(2,1)} %b.5) | copy-start | bytes 98308
  62.2 9.9 %copy-start.6 = (f32[48,128]{1,0:T(8,128)S(1)}, f32[48,128]{1,0:T(8,128)}, u32[]{:S(2)}) copy-start(f32[48,128]{1,0:T(8,128)} %get-tuple-element.36.tok) | copy-start | bytes 73732
  62.2 9.9 %copy-start.7 = (bf16[128,128]{1,0:T(8,128)(2,1)S(1)}, bf16[128,128]{1,0:T(8,128)(2,1)}, u32[]{:S(2)}) copy-start(bf16[128,128]{1,0:T(8,128)(2,1)} %c.3) | copy-start | bytes 98308
  62.2 9.9 %copy-start.8 = (f32[1024]{0:T(1024)S(1)}, f32[1024]{0:T(1024)}, u32[]{:S(2)}) copy-start(f32[1024]{0:T(1024)} %param.24) | copy-start | bytes 12292
  62.2 9.8 %copy-start.9 = (s32[8,16]{1,0:T(8,128)S(1)}, s32[8,16]{1,0:T(8,128)}, u32[]{:S(2)}) copy-start(s32[8,16]{1,0:T(8,128)} %keep.1) | copy-start | bytes 1540
  72.1 15.7 %copy-start = (f32[4,136,256]{2,1,0:T(8,128)S(1)}, f32[4,136,256]{2,1,0:T(8,128)}, u32[]{:S(2)}) copy-start(f32[4,136,256]{2,1,0:T(8,128)} %get-tuple-element.37.own) | copy-start | bytes 1671172
  72.1 15.7 %copy-start.10 = (f32[128]{0:T(128)S(1)}, f32[128]{0:T(128)}, u32[]{:S(2)}) copy-start(f32[128]{0:T(128)} %param.15) | copy-start | bytes 1540

commit v5 on v4

--- a/solution.py
+++ b/solution.py
@@ -41,20 +41,25 @@
     return high, (a - high.astype(F32)).astype(BF16)
 
 
+def stack(parts, dim):
+    return jnp.concatenate(parts, axis=dim)
+
+
 def mm_left(a, exact, dims=NN):
-    high, low = split(a)
-    return mm(high, exact, dims) + mm(low, exact, dims)
+    return mm(stack(split(a), 1), stack([exact, exact], dims[1][0]), dims)
 
 
 def mm_right(exact, b, dims=NN):
-    high, low = split(b)
-    return mm(exact, high, dims) + mm(exact, low, dims)
+    return mm(stack([exact, exact], 1), stack(split(b), dims[1][0]), dims)
+
+
+def mm_halves(a, b, dims=NN):
+    (ah, al), (bh, bl) = a, b
+    return mm(stack([ah, al], 1), stack([bh, bh], dims[1][0]), dims) + mm(ah, bl, dims)
 
 
 def mm_both(a, b, dims=NN):
-    ah, al = split(a)
-    bh, bl = split(b)
-    return mm(ah, bh, dims) + (mm(ah, bl, dims) + mm(al, bh, dims))
+    return mm_halves(split(a), split(b), dims)
 
 
 def iota(shape, dim):
@@ -122,7 +127,7 @@
 
 
 def whole_sums(a):
-    return [jnp.sum(s, axis=0, keepdims=True) for s in head_sums(a)]
+    return head_sums(jnp.sum(a, axis=0, keepdims=True))
 
 
 def halved(a, b):
@@ -147,12 +152,11 @@
     copies = [
         pltpu.make_async_copy(src, dst, sem.at[i])
         for i, (src, dst) in enumerate(
-            [(dt_hbm, dt_t), (bias_hbm, bias), (alog_hbm, alog), (skip_hbm, skip), (b_hbm, b)]
+            [(dt_hbm, dt_t), (bias_hbm, bias), (alog_hbm, alog), (skip_hbm, skip), (b_hbm, b), (x_hbm, x)]
         )
     ]
-    loads = [pltpu.make_async_copy(x_hbm.at[:, lanes(q)], x.at[:, lanes(q)], quarter.at[0, q]) for q in range(GROUP)]
-    stores = [pltpu.make_async_copy(send.at[q], send_hbm.at[q], quarter.at[1, q]) for q in range(GROUP)]
-    for copy in copies + loads:
+    stores = [pltpu.make_async_copy(send.at[q], send_hbm.at[q], quarter.at[q]) for q in range(GROUP)]
+    for copy in copies:
         copy.start()
     for copy in copies:
         copy.wait()
@@ -170,7 +174,6 @@
     decay = lanes_of(jnp.exp(last(logs)))
     b_t = b[...].astype(F32).T.astype(BF16)
     for q in range(GROUP):
-        loads[q].wait()
         send[q, :NS, :] = mm_right(b_t, x[:, lanes(q)].astype(F32) * pair_cols(cols, q))
         send[q, NS:, :] = jnp.broadcast_to(decay[q], (8, WIDE))
         stores[q].start()
@@ -335,12 +338,11 @@
         for h in range(HP):
             r = q * HP + h
             sl = slice(h * PC, (h + 1) * PC)
-            dmixed = mm(gh[:, sl], xb[:, sl], NT) + mm(gl[:, sl], xb[:, sl], NT)
+            dmixed = mm(stack([gh[:, sl], gl[:, sl]], 1), stack([xb[:, sl], xb[:, sl]], 1), NT)
             dscores = dscores + decays(logs, cols, r, lower) * dmixed * step[r : r + 1]
             diff = logs[r : r + 1] - cols[:, r : r + 1]
             mixed_t = jnp.where(upper, jnp.exp(jnp.where(upper, diff, 0.0)), 0.0) * scores_t
-            mh, ml = split(mixed_t)
-            inner.append(mm(mh, gh[:, sl]) + (mm(mh, gl[:, sl]) + mm(ml, gh[:, sl])))
+            inner.append(mm_halves(split(mixed_t), (gh[:, sl], gl[:, sl])))
         v = jnp.concatenate(inner, axis=1)
         gx_out[:, lanes(q)] = pair_cols(cols, q, 2 * HD) * v + d[q] * gy
         xv += head_sums(xq * v)
@@ -426,11 +428,9 @@
         xq = x[:, lanes(q)].astype(F32)
         tail = pair_cols(cols, q)
         stepc = pair_cols(cols, q, HD)
-        gh, gl = split(grad)
-        v = tail * (mm(b[...], gh) + mm(b[...], gl))
+        v = tail * mm_right(b[...], grad)
         gx[:, lanes(q)] = (gx_in[:, lanes(q)] + stepc * v).astype(BF16)
-        sh, sl = split(tail * stepc * xq)
-        db = db + (mm(sh, gh, NT) + (mm(sh, gl, NT) + mm(sl, gh, NT)))
+        db = db + mm_both(tail * stepc * xq, grad, NT)
         xv += head_sums(xq * v)
         leaving = decay[q] * enter[q] + own[q, :NS, :]
         ends += whole_sums(grad * leaving)
@@ -507,7 +507,7 @@
         [
             pltpu.VMEM((CHUNK, width), BF16), pltpu.VMEM((CHUNK, NS), BF16), pltpu.VMEM((heads, CHUNK), F32),
             pltpu.SMEM((heads,), F32), pltpu.SMEM((heads,), F32), pltpu.SMEM((heads,), F32),
-            pltpu.VMEM((GROUP, ROWS_S, WIDE), F32), dma((5,)), dma((2, GROUP)),
+            pltpu.VMEM((GROUP, ROWS_S, WIDE), F32), dma((6,)), dma((GROUP,)),
         ], FULL, [ANY, VMEM],
     )(x_in, b_in, dt_raw.T, dt_bias, a_log, d_skip)
     group = swap(own, "y")

time: 183 us -> 182 us (level)
  no operation moved by 1% of the time
where the time goes in v5:
time: 182 us
  blocking collectives  169 us (93%)
  Pallas kernels  11.4 us (6%)
    all_to_all x11, blocking collectives, swap(): return lax.all_to_all(a, axis, 0, 0, tiled=True)  169 us

profile of v5, /device:TPU:1, one launch (start us, length us, event | category | flops | bytes accessed | tf_op | source)
XLA Modules:
  0.0 181.5 jit_solution(3498006468855679993)
XLA Ops:
  0.7 3.3 %shard_map.196 = (f32[4,136,256]{2,1,0:T(8,128)}, f32[48,128]{1,0:T(8,128)}) custom-call(bf16[128,1024]{1,0:T(8,128)(2,1)} %x.5, bf16[128,128]{1,0:T(8,128)(2,1)} %b.5, f32[8,128]{1,0:T(8,128)} %bitcast.11, f32[8]{0:T(128)} %bias_hbm.1, f32[8]{0:T(128)} %alog_hbm.1, f32[8]{0:T(128)} %skip_hbm.1), custom_call_target="tpu_custom_call" | custom-call | tf_op jit(solution)/shard_map/pallas_call | solution.py:505
  3.9 12.1 %all_to_all.55.got.own = f32[4,136,256]{2,1,0:T(8,128)S(1)} all-to-all(f32[4,136,256]{2,1,0:T(8,128)} %get-tuple-element.37.own), channel_id=1, replica_groups=mesh['z'=16,'y'=4,'head'=8] {'y'}, dimensions={0} | all-to-all | bytes 1114112 | tf_op jit(solution)/shard_map/all_to_all | solution.py:484
  16.1 0.1 shard_map.197
  16.2 28.4 %all_to_all.56.got = f32[16,2,1152]{2,1,0:T(2,128)S(1)} all-to-all(f32[16,2,1152]{2,1,0:T(2,128)S(1)} %get-tuple-element.38), channel_id=1, replica_groups=mesh['z'=16,'y'=4,'head'=8] {'z'}, dimensions={0} | all-to-all | bytes 294912 | tf_op jit(solution)/shard_map/all_to_all | solution.py:484
  44.6 0.2 shard_map.198
  44.8 16.8 %all_to_all.57.got = f32[16,2,1024]{2,1,0:T(2,128)S(1)} all-to-all(f32[16,2,1024]{2,1,0:T(2,128)S(1)} %get-tuple-element.39), channel_id=1, replica_groups=mesh['z'=16,'y'=4,'head'=8] {'z'}, dimensions={0} | all-to-all | bytes 262144 | tf_op jit(solution)/shard_map/all_to_all | solution.py:484
  61.6 0.0 copy-start.6
  61.6 0.0 copy-start.9
  61.6 0.1 shard_map.199
  61.8 9.7 %all_to_all.58.enter = f32[4,128,256]{2,1,0:T(8,128)S(1)} all-to-all(f32[4,128,256]{2,1,0:T(8,128)S(1)} %shard_map.199), channel_id=1, replica_groups=mesh['z'=16,'y'=4,'head'=8] {'y'}, dimensions={0} | all-to-all | bytes 1048576 | tf_op jit(solution)/shard_map/all_to_all | solution.py:484
  71.5 1.6 shard_map.200
  73.1 14.1 %all_to_all.59.stats = f32[8,2,128]{2,1,0:T(2,128)S(1)} all-to-all(f32[8,2,128]{2,1,0:T(2,128)S(1)} %get-tuple-element.41), channel_id=1, replica_groups=mesh['z'=16,'y'=4,'head'=8] {'head'}, dimensions={0} | all-to-all | bytes 16384 | tf_op jit(solution)/shard_map/all_to_all | solution.py:484
  87.2 3.0 %shard_map.201 = (bf16[128,1024]{1,0:T(8,128)(2,1)}, f32[128,1024]{1,0:T(8,128)S(1)}, f32[4,264,256]{2,1,0:T(8,128)S(1)}, f32[16,128]{1,0:T(8,128)S(1)}, f32[2,128,128]{2,1,0:T(8,128)S(1)}, /*index=5*/f32[1,128]{1,0:T(1,128)}) custom-call(f32[8,2,128]{2,1,0:T(2,128)S(1)} %all_to_all.59.stats, bf16[128,1024]{1,0:T(8,128)(2,1)S(1)} %copy-done.1, ...), custom_call_target="tpu_custom_call" | custom-call | tf_op jit(solution)/shard_map/pallas_call | solution.py:525
  90.3 17.2 %all_to_all.60.got = f32[4,264,256]{2,1,0:T(8,128)S(1)} all-to-all(f32[4,264,256]{2,1,0:T(8,128)S(1)} %get-tuple-element.47), channel_id=1, replica_groups=mesh['z'=16,'y'=4,'head'=8] {'y'}, dimensions={0} | all-to-all | bytes 2162688 | tf_op jit(solution)/shard_map/all_to_all | solution.py:484
  107.5 0.2 shard_map.202
  107.7 16.5 %all_to_all.61.got = f32[16,2,2304]{2,1,0:T(2,128)S(1)} all-to-all(f32[16,2,2304]{2,1,0:T(2,128)S(1)} %get-tuple-element.48), channel_id=1, replica_groups=mesh['z'=16,'y'=4,'head'=8] {'z'}, dimensions={0} | all-to-all | bytes 589824 | tf_op jit(solution)/shard_map/all_to_all | solution.py:484
  124.2 0.1 shard_map.203
  124.4 23.8 %all_to_all.62.late = f32[16,2,1152]{2,1,0:T(2,128)S(1)} all-to-all(f32[16,2,1152]{2,1,0:T(2,128)S(1)} %get-tuple-element.50), channel_id=1, replica_groups=mesh['z'=16,'y'=4,'head'=8] {'z'}, dimensions={0} | all-to-all | bytes 294912 | tf_op jit(solution)/shard_map/all_to_all | solution.py:484
  148.1 0.2 shard_map.204
  148.3 9.5 %all_to_all.63.late = f32[4,136,256]{2,1,0:T(8,128)S(1)} all-to-all(f32[4,136,256]{2,1,0:T(8,128)S(1)} %shard_map.204), channel_id=1, replica_groups=mesh['z'=16,'y'=4,'head'=8] {'y'}, dimensions={0} | all-to-all | bytes 1114112 | tf_op jit(solution)/shard_map/all_to_all | solution.py:484
  157.8 1.8 %shard_map.205 = (bf16[128,1024]{1,0:T(8,128)(2,1)}, f32[8,128]{1,0:T(8,128)}, f32[1,1024]{1,0:T(1,128)}, f32[1,8]{1,0:T(1,128)}, f32[1,8]{1,0:T(1,128)}, /*index=5*/f32[8,32,128]{2,1,0:T(8,128)S(1)}) custom-call(bf16[128,1024]{1,0:T(8,128)(2,1)S(1)} %copy-done.1, bf16[128,128]{1,0:T(8,128)(2,1)S(1)} %copy-done.4, f32[48,128]{1,0:T(8,128)S(1)} %copy-done.6, ...), custom_call_target="tpu_custom_call" | custom-call | tf_op jit(solution)/shard_map/pallas_call | solution.py:542
  159.6 12.7 %all_to_all.64.got = f32[8,32,128]{2,1,0:T(8,128)S(1)} all-to-all(f32[8,32,128]{2,1,0:T(8,128)S(1)} %get-tuple-element.55), channel_id=1, replica_groups=mesh['z'=16,'y'=4,'head'=8] {'head'}, dimensions={0} | all-to-all | bytes 262144 | tf_op jit(solution)/shard_map/all_to_all | solution.py:484
  172.4 8.5 %all_to_all.65.got = f32[8,32,128]{2,1,0:T(8,128)S(1)} all-to-all(f32[8,32,128]{2,1,0:T(8,128)S(1)} %shard_map.206), channel_id=1, replica_groups=mesh['z'=16,'y'=4,'head'=8] {'head'}, dimensions={0} | all-to-all | bytes 262144 | tf_op jit(solution)/shard_map/all_to_all | solution.py:484
  180.9 0.7 shard_map.207
  (21 shorter events, 0.1 us)
Async XLA Ops:
  0.6 43.9 %copy-start.5 = (f32[8,128,128]{2,1,0:T(8,128)S(1)}, f32[8,128,128]{2,1,0:T(8,128)}, u32[]{:S(2)}) copy-start(f32[8,128,128]{2,1,0:T(8,128)} %state_in.1) | copy-start | bytes 1572868
  61.6 9.9 %copy-start.1 = (bf16[128,1024]{1,0:T(8,128)(2,1)S(1)}, bf16[128,1024]{1,0:T(8,128)(2,1)}, u32[]{:S(2)}) copy-start(bf16[128,1024]{1,0:T(8,128)(2,1)} %x.5) | copy-start | bytes 786436
  61.6 9.9 %copy-start.2 = (bf16[1024,1024]{1,0:T(8,128)(2,1)S(1)}, bf16[1024,1024]{1,0:T(8,128)(2,1)}, u32[]{:S(2)}) copy-start(bf16[1024,1024]{1,0:T(8,128)(2,1)} %grad_full.1) | copy-start | bytes 6291460
  61.6 9.9 %copy-start.3 = (bf16[128,1024]{1,0:T(8,128)(2,1)S(1)}, bf16[128,1024]{1,0:T(8,128)(2,1)}, u32[]{:S(2)}) copy-start(bf16[128,1024]{1,0:T(8,128)(2,1)} %z.3) | copy-start | bytes 786436
  61.6 9.9 %copy-start.4 = (bf16[128,128]{1,0:T(8,128)(2,1)S(1)}, bf16[128,128]{1,0:T(8,128)(2,1)}, u32[]{:S(2)}) copy-start(bf16[128,128]{1,0:T(8,128)(2,1)} %b.5) | copy-start | bytes 98308
  61.6 9.9 %copy-start.6 = (f32[48,128]{1,0:T(8,128)S(1)}, f32[48,128]{1,0:T(8,128)}, u32[]{:S(2)}) copy-start(f32[48,128]{1,0:T(8,128)} %get-tuple-element.36.tok) | copy-start | bytes 73732
  61.6 9.9 %copy-start.7 = (bf16[128,128]{1,0:T(8,128)(2,1)S(1)}, bf16[128,128]{1,0:T(8,128)(2,1)}, u32[]{:S(2)}) copy-start(bf16[128,128]{1,0:T(8,128)(2,1)} %c.3) | copy-start | bytes 98308
  61.6 9.9 %copy-start.8 = (f32[1024]{0:T(1024)S(1)}, f32[1024]{0:T(1024)}, u32[]{:S(2)}) copy-start(f32[1024]{0:T(1024)} %param.24) | copy-start | bytes 12292
  61.6 9.9 %copy-start.9 = (s32[8,16]{1,0:T(8,128)S(1)}, s32[8,16]{1,0:T(8,128)}, u32[]{:S(2)}) copy-start(s32[8,16]{1,0:T(8,128)} %keep.1) | copy-start | bytes 1540
  71.5 15.7 %copy-start = (f32[4,136,256]{2,1,0:T(8,128)S(1)}, f32[4,136,256]{2,1,0:T(8,128)}, u32[]{:S(2)}) copy-start(f32[4,136,256]{2,1,0:T(8,128)} %get-tuple-element.37.own) | copy-start | bytes 1671172
  71.5 15.7 %copy-start.10 = (f32[128]{0:T(128)S(1)}, f32[128]{0:T(128)}, u32[]{:S(2)}) copy-start(f32[128]{0:T(128)} %param.15) | copy-start | bytes 1540

commit v6 on v5

--- a/solution.py
+++ b/solution.py
@@ -10,9 +10,10 @@
 from jax.sharding import PartitionSpec as P
 
 EPS = 1e-05
-GROUP = 4
+GROUP = 8
 CHUNK = 128
-HP = 2
+HP = 1
+SUB = 2
 PC = 128
 NS = 128
 WIDE = HP * PC
@@ -74,10 +75,6 @@
     return 1.0 / (1.0 + jnp.exp(-v))
 
 
-def own_heads():
-    return lax.axis_index("y") * HP
-
-
 def head_col(ref):
     row = iota((HD, 1), 0)
     out = jnp.zeros((HD, 1), F32)
@@ -107,19 +104,16 @@
     return jnp.concatenate(list(cols) + [pad], axis=1).T[: len(cols)]
 
 
-def pair(a, b, rows):
-    return jnp.concatenate(
-        [jnp.broadcast_to(a, (rows, PC)), jnp.broadcast_to(b, (rows, PC))], axis=1
-    )
+def over(value, rows=1):
+    return jnp.broadcast_to(value, (rows, WIDE))
 
 
 def lanes_of(values):
-    return [pair(values[q * HP : q * HP + 1], values[q * HP + 1 : q * HP + 2], 1) for q in range(GROUP)]
-
-
-def pair_cols(cols, q, at=0):
-    c = at + q * HP
-    return pair(cols[:, c : c + 1], cols[:, c + 1 : c + 2], CHUNK)
+    return [over(values[q : q + 1]) for q in range(GROUP)]
+
+
+def head_cols(cols, q, at=0):
+    return over(cols[:, at + q : at + q + 1], CHUNK)
 
 
 def head_sums(a):
@@ -134,20 +128,12 @@
     return jnp.where(iota((1, WIDE), 1) % PC < PC // 2, a, b)
 
 
-def two(row):
-    return jnp.concatenate([row[:, :PC], row[:, PC:]], axis=0)
-
-
-def one(rows):
-    return jnp.concatenate([rows[:1], rows[1:]], axis=1)
-
-
 def lanes(q):
     return slice(q * WIDE, (q + 1) * WIDE)
 
 
 def own_state_body(
-    x_hbm, b_hbm, dt_hbm, bias_hbm, alog_hbm, skip_hbm, send_hbm, tok, x, b, dt_t, bias, alog, skip, send, sem, quarter
+    x_hbm, b_hbm, dt_hbm, bias_hbm, alog_hbm, skip_hbm, send, tok, x, b, dt_t, bias, alog, skip, sem
 ):
     copies = [
         pltpu.make_async_copy(src, dst, sem.at[i])
@@ -155,7 +141,6 @@
             [(dt_hbm, dt_t), (bias_hbm, bias), (alog_hbm, alog), (skip_hbm, skip), (b_hbm, b), (x_hbm, x)]
         )
     ]
-    stores = [pltpu.make_async_copy(send.at[q], send_hbm.at[q], quarter.at[q]) for q in range(GROUP)]
     for copy in copies:
         copy.start()
     for copy in copies:
@@ -174,26 +159,22 @@
     decay = lanes_of(jnp.exp(last(logs)))
     b_t = b[...].astype(F32).T.astype(BF16)
     for q in range(GROUP):
-        send[q, :NS, :] = mm_right(b_t, x[:, lanes(q)].astype(F32) * pair_cols(cols, q))
+        send[q, :NS, :] = mm_right(b_t, x[:, lanes(q)].astype(F32) * head_cols(cols, q))
         send[q, NS:, :] = jnp.broadcast_to(decay[q], (8, WIDE))
-        stores[q].start()
-    for q in range(GROUP):
-        stores[q].wait()
 
 
 def to_slices(out, at, state):
     rows = NS // out.shape[0]
-    for n in range(NS):
-        tile = slice((at + n % rows) * PC, (at + n % rows + 1) * PC)
-        out[n // rows, :, tile] = jnp.concatenate([state[n : n + 1, :PC], state[n : n + 1, PC:]], axis=0)
+    for n in range(0, NS, SUB):
+        tile = at + n % rows // SUB
+        out[n // rows, :, tile * PC : (tile + 1) * PC] = state[n : n + SUB, :]
 
 
 def from_slices(ref, out):
     rows = NS // ref.shape[0]
-    for n in range(NS):
-        tile = slice(n % rows * PC, (n % rows + 1) * PC)
-        for h in range(HP):
-            out[n : n + 1, h * PC : (h + 1) * PC] = ref[n // rows, h : h + 1, tile]
+    for n in range(0, NS, SUB):
+        tile = n % rows // SUB
+        out[n : n + SUB, :] = ref[n // rows, :, tile * PC : (tile + 1) * PC]
 
 
 def group_state_body(got, part, send):
@@ -207,45 +188,45 @@
         part[k] = state
     to_slices(send, 0, state)
     for lap in range(send.shape[0]):
-        send[lap, :, send.shape[2] - PC :] = two(whole)
+        send[lap, :, send.shape[2] - PC :] = jnp.broadcast_to(whole, (SUB, PC))
 def spread(row, count):
     return jnp.concatenate([row] * count, axis=1)
 
 
 def scan_body(got, state_in, out, decay, flat, first):
-    laps, _, lanes = out.shape
-    rows = lanes // PC
-    base = own_heads()
-    for h in range(HP):
-        flat[...] = state_in[base + h].T
-        for j in range(rows):
-            first[h : h + 1, j * PC : (j + 1) * PC] = flat[pl.ds(lax.axis_index("z") * rows + j, 1), :]
+    laps, _, width = out.shape
+    tiles = width // PC
+    flat[...] = state_in[lax.axis_index("y")].T
+    for j in range(tiles):
+        for r in range(SUB):
+            row = lax.axis_index("z") * (tiles * SUB) + (j * SUB + r)
+            first[r : r + 1, j * PC : (j + 1) * PC] = flat[pl.ds(row, 1), :]
     state = first[...]
     for lap in range(laps):
         out[lap] = state
-        factor = got[lap, :, lanes:]
+        factor = got[lap, :, width:]
         decay[lap] = factor
-        state = spread(factor, rows) * state + got[lap, :, :lanes]
+        state = spread(factor, tiles) * state + got[lap, :, :width]
 
 
 def scan_back_body(got, decay, out, done):
     laps = got.shape[0]
-    lanes = out.shape[2] - PC
-    rows = lanes // PC
-    state = jnp.zeros((HP, lanes), F32)
-    cross = jnp.zeros((HP, lanes), F32)
-    total = jnp.zeros((HP, 2 * PC), F32)
+    width = out.shape[2] - PC
+    tiles = width // PC
+    state = jnp.zeros((SUB, width), F32)
+    cross = jnp.zeros((SUB, width), F32)
+    total = jnp.zeros((SUB, PC), F32)
     for lap in reversed(range(laps)):
-        out[lap, :, :lanes] = state
-        cross = cross + state * got[lap, :, lanes : 2 * lanes]
-        state = spread(decay[lap], rows) * state + got[lap, :, :lanes]
-        total = total + got[lap, :, 2 * lanes :]
+        out[lap, :, :width] = state
+        cross = cross + state * got[lap, :, width : 2 * width]
+        state = spread(decay[lap], tiles) * state + got[lap, :, :width]
+        total = total + got[lap, :, 2 * width :]
     done[...] = total
     extra = cross[:, :PC]
-    for j in range(1, rows):
+    for j in range(1, tiles):
         extra = extra + cross[:, j * PC : (j + 1) * PC]
     for lap in range(laps):
-        out[lap, :, lanes:] = extra
+        out[lap, :, width:] = extra
 
 
 def enter_body(got, own, part, send, flat):
@@ -281,7 +262,7 @@
             r = q * HP + h
             mixed = decays(logs, cols, r, lower) * scores * step[r : r + 1]
             inner.append(mm_left(mixed, x[:, r * PC : (r + 1) * PC]))
-        carried = mm_right(c[...], enter[q]) * pair_cols(cols, q, HD)
+        carried = mm_right(c[...], enter[q]) * head_cols(cols, q, HD)
         y = jnp.concatenate(inner, axis=1) + carried + d[q] * x[:, lanes(q)].astype(F32)
         y_out[:, lanes(q)] = y
         zq = z[:, lanes(q)].astype(F32)
@@ -344,13 +325,13 @@
             mixed_t = jnp.where(upper, jnp.exp(jnp.where(upper, diff, 0.0)), 0.0) * scores_t
             inner.append(mm_halves(split(mixed_t), (gh[:, sl], gl[:, sl])))
         v = jnp.concatenate(inner, axis=1)
-        gx_out[:, lanes(q)] = pair_cols(cols, q, 2 * HD) * v + d[q] * gy
+        gx_out[:, lanes(q)] = head_cols(cols, q, 2 * HD) * v + d[q] * gy
         xv += head_sums(xq * v)
-        eg = pair_cols(cols, q, HD) * gy
+        eg = head_cols(cols, q, HD) * gy
         dc = dc + mm_both(eg, enter[q], NT)
         send[q, :NS, :] = mm_right(c_t, eg)
         leaving = decay[q] * enter[q] + own[q, :NS, :]
-        send[q, NS : 2 * NS, :] = near[q] * leaving - mm_right(b_t, xq * pair_cols(cols, q, 3 * HD))
+        send[q, NS : 2 * NS, :] = near[q] * leaving - mm_right(b_t, xq * head_cols(cols, q, 3 * HD))
     maps[0] = mm_left(dscores.T, c[...])
     maps[1] = dc + mm_left(dscores, b[...])
     xv = rows_of(xv)
@@ -360,8 +341,7 @@
     small[HD:] = xv
     alogs = jnp.sum(dla * la, axis=1, keepdims=True)
     for q in range(GROUP):
-        r = q * HP
-        row = halved(pair(skips[r], skips[r + 1], 1), pair(alogs[r : r + 1], alogs[r + 1 : r + 2], 1))
+        row = halved(over(skips[q]), over(alogs[q : q + 1]))
         send[q, 2 * NS :, :] = jnp.concatenate([shared[q], row, jnp.zeros((6, WIDE), F32)], axis=0)
 
 
@@ -382,14 +362,13 @@
         reach = reach * decay
         grad = decay * grad + got[k, :NS, :]
     laps = send.shape[0]
-    rows = NS // laps
+    tiles = NS // laps // SUB
     to_slices(send, 0, grad)
-    to_slices(send, rows, tangent)
-    cross = head_sums(cross)
-    scalars = extra[1:] + halved(jnp.zeros((1, WIDE), F32), pair(cross[0], cross[1], 1))
-    tail = jnp.concatenate([two(extra[:1]), two(scalars)], axis=1)
+    to_slices(send, tiles, tangent)
+    scalars = extra[1:] + halved(jnp.zeros((1, WIDE), F32), over(head_sums(cross)[0]))
+    tail = jnp.concatenate([extra[:1], scalars], axis=0)
     for lap in range(laps):
-        send[lap, :, 2 * rows * PC :] = tail
+        send[lap, :, 2 * tiles * PC :] = tail
 
 
 def leave_body(late, done, back, own, send, flat):
@@ -399,12 +378,8 @@
     alog = late[0, :, at:]
     for lap in range(1, late.shape[0]):
         alog = alog + late[lap, :, at:]
-    alog = jnp.sum(alog, axis=1, keepdims=True) + done[:, 2 * PC - 1 :]
-    skip = done[:, PC : PC + 1]
-    extra = jnp.concatenate(
-        [one(done[:, :PC]), pair(skip[:1], skip[1:], 1), pair(alog[:1], alog[1:], 1), jnp.zeros((5, WIDE), F32)],
-        axis=0,
-    )
+    alog = jnp.sum(jnp.sum(alog, axis=0, keepdims=True), axis=1, keepdims=True) + done[1:, PC - 1 :]
+    extra = jnp.concatenate([done[:1], over(done[1:, :1]), over(alog), jnp.zeros((5, WIDE), F32)], axis=0)
     reach = jnp.ones((1, WIDE), F32)
     for k in reversed(range(GROUP)):
         send[k, :NS, :] = back[k] + reach * grad
@@ -426,8 +401,8 @@
     for q in range(GROUP):
         grad = late[q, :NS, :]
         xq = x[:, lanes(q)].astype(F32)
-        tail = pair_cols(cols, q)
-        stepc = pair_cols(cols, q, HD)
+        tail = head_cols(cols, q)
+        stepc = head_cols(cols, q, HD)
         v = tail * mm_right(b[...], grad)
         gx[:, lanes(q)] = (gx_in[:, lanes(q)] + stepc * v).astype(BF16)
         db = db + mm_both(tail * stepc * xq, grad, NT)
@@ -468,11 +443,11 @@
         dc[i * rows : (i + 1) * rows, :] = got[i, rows:, :]
 
 
-def call(body, ins, outs, scratch=(), limit=LIMIT, places=None):
+def call(body, ins, outs, scratch=(), limit=LIMIT):
     out = pl.pallas_call(
         body,
         in_specs=ins,
-        out_specs=places or [VMEM] * len(outs),
+        out_specs=[VMEM] * len(outs),
         out_shape=[jax.ShapeDtypeStruct(s, t) for s, t in outs],
         scratch_shapes=scratch,
         compiler_params=pltpu.CompilerParams(vmem_limit_bytes=limit),
@@ -495,7 +470,7 @@
     block_len = grad_full.shape[0] // keep.shape[0]
     states = ((GROUP, NS, WIDE), F32)
     slab = ((CHUNK, width), F32)
-    tile = NS // laps * PC
+    tile = NS // laps // SUB * PC
     bind = functools.partial
     dma = pltpu.SemaphoreType.DMA
     router = router_score.reshape(1, CHUNK)
@@ -507,14 +482,14 @@
         [
             pltpu.VMEM((CHUNK, width), BF16), pltpu.VMEM((CHUNK, NS), BF16), pltpu.VMEM((heads, CHUNK), F32),
             pltpu.SMEM((heads,), F32), pltpu.SMEM((heads,), F32), pltpu.SMEM((heads,), F32),
-            pltpu.VMEM((GROUP, ROWS_S, WIDE), F32), dma((6,)), dma((GROUP,)),
-        ], FULL, [ANY, VMEM],
+            dma((6,)),
+        ], FULL,
     )(x_in, b_in, dt_raw.T, dt_bias, a_log, d_skip)
     group = swap(own, "y")
-    part, send = call(group_state_body, [VMEM], [states, ((laps, HP, tile + PC), F32)])(group)
+    part, send = call(group_state_body, [VMEM], [states, ((laps, SUB, tile + PC), F32)])(group)
     send, decay = call(
-        scan_body, [VMEM] * 2, [((laps, HP, tile), F32), ((laps, HP, PC), F32)],
-        [pltpu.VMEM((NS, PC), F32), pltpu.VMEM((HP, tile), F32)],
+        scan_body, [VMEM] * 2, [((laps, SUB, tile), F32), ((laps, SUB, PC), F32)],
+        [pltpu.VMEM((NS, PC), F32), pltpu.VMEM((SUB, tile), F32)],
     )(swap(send, "z"), state_in)
     (enter,) = call(enter_body, [VMEM] * 3, [states], [flat])(swap(send, "z"), group, part)
     enter = swap(enter, "y")
@@ -529,10 +504,10 @@
             ((2, CHUNK, NS), F32), ((1, CHUNK), F32),
         ],
     )(swap(stats, "head"), x_in, b_in, c_in, z_in, up, gain, router, tok, enter, own, y)
-    back, send = call(group_back_body, [VMEM] * 2, [states, ((laps, HP, 2 * tile + 2 * PC), F32)])(
+    back, send = call(group_back_body, [VMEM] * 2, [states, ((laps, SUB, 2 * tile + PC), F32)])(
         swap(send, "y"), group
     )
-    send, done = call(scan_back_body, [VMEM] * 2, [((laps, HP, tile + PC), F32), ((HP, 2 * PC), F32)])(
+    send, done = call(scan_back_body, [VMEM] * 2, [((laps, SUB, tile + PC), F32), ((SUB, PC), F32)])(
         swap(send, "z"), decay
     )
     (late,) = call(leave_body, [VMEM] * 4, [((GROUP, ROWS_S, WIDE), F32)], [flat])(

time: 182 us -> 177 us (0.973)
  blocking collectives: 169 us -> 163 us
    all_to_all x11, blocking collectives: 169 us -> 163 us  [swap(): return lax.all_to_all(a, axis, 0, 0, tiled=True)]
where the time goes in v6:
time: 177 us; the launch traced here: 176 us
  blocking collectives  163 us (92%)
  Pallas kernels  12.6 us (7%)
    all_to_all x11, blocking collectives, swap(): return lax.all_to_all(a, axis, 0, 0, tiled=True)  163 us
    pallas_call x1, Pallas kernels, shards(): call(bind(output_back_body, total_width), [VMEM] * 12, [((CHUNK, width),...  4.06 us

profile of v6, /device:TPU:1, one launch (start us, length us, event | category | flops | bytes accessed | tf_op | source)
XLA Modules:
  0.0 176.3 jit_solution(3186734110964148157)
XLA Ops:
  0.7 2.8 %shard_map.196 = (f32[8,136,128]{2,1,0:T(8,128)}, f32[48,128]{1,0:T(8,128)}) custom-call(bf16[128,1024]{1,0:T(8,128)(2,1)} %x.5, bf16[128,128]{1,0:T(8,128)(2,1)} %b.5, f32[8,128]{1,0:T(8,128)} %bitcast.11, f32[8]{0:T(128)} %bias_hbm.1, f32[8]{0:T(128)} %alog_hbm.1, f32[8]{0:T(128)} %skip_hbm.1), custom_call_target="tpu_custom_call" | custom-call | tf_op jit(solution)/shard_map/pallas_call | solution.py:480
  3.5 14.3 %all_to_all.55.got.own = f32[8,136,128]{2,1,0:T(8,128)S(1)} all-to-all(f32[8,136,128]{2,1,0:T(8,128)} %get-tuple-element.37.own), channel_id=1, replica_groups=mesh['z'=8,'y'=8,'head'=8] {'y'}, dimensions={0} | all-to-all | bytes 1114112 | tf_op jit(solution)/shard_map/all_to_all | solution.py:459
  17.8 0.1 shard_map.197
  17.8 27.5 %all_to_all.56.got = f32[8,2,1152]{2,1,0:T(2,128)S(1)} all-to-all(f32[8,2,1152]{2,1,0:T(2,128)S(1)} %get-tuple-element.38), channel_id=1, replica_groups=mesh['z'=8,'y'=8,'head'=8] {'z'}, dimensions={0} | all-to-all | bytes 147456 | tf_op jit(solution)/shard_map/all_to_all | solution.py:459
  45.3 0.1 shard_map.198
  45.5 14.6 %all_to_all.57.got = f32[8,2,1024]{2,1,0:T(2,128)S(1)} all-to-all(f32[8,2,1024]{2,1,0:T(2,128)S(1)} %get-tuple-element.39), channel_id=1, replica_groups=mesh['z'=8,'y'=8,'head'=8] {'z'}, dimensions={0} | all-to-all | bytes 131072 | tf_op jit(solution)/shard_map/all_to_all | solution.py:459
  60.1 0.0 copy-start.7
  60.1 0.0 copy-start.8
  60.1 0.1 shard_map.199
  60.2 10.0 %all_to_all.58.enter = f32[8,128,128]{2,1,0:T(8,128)S(1)} all-to-all(f32[8,128,128]{2,1,0:T(8,128)S(1)} %shard_map.199), channel_id=1, replica_groups=mesh['z'=8,'y'=8,'head'=8] {'y'}, dimensions={0} | all-to-all | bytes 1048576 | tf_op jit(solution)/shard_map/all_to_all | solution.py:459
  70.3 1.7 shard_map.200
  72.0 15.2 %all_to_all.59.stats = f32[8,2,128]{2,1,0:T(2,128)S(1)} all-to-all(f32[8,2,128]{2,1,0:T(2,128)S(1)} %get-tuple-element.41), channel_id=1, replica_groups=mesh['z'=8,'y'=8,'head'=8] {'head'}, dimensions={0} | all-to-all | bytes 16384 | tf_op jit(solution)/shard_map/all_to_all | solution.py:459
  87.2 4.1 %shard_map.201 = (bf16[128,1024]{1,0:T(8,128)(2,1)}, f32[128,1024]{1,0:T(8,128)S(1)}, f32[8,264,128]{2,1,0:T(8,128)S(1)}, f32[16,128]{1,0:T(8,128)S(1)}, f32[2,128,128]{2,1,0:T(8,128)S(1)}, /*index=5*/f32[1,128]{1,0:T(1,128)}) custom-call(f32[8,2,128]{2,1,0:T(2,128)S(1)} %all_to_all.59.stats, bf16[128,1024]{1,0:T(8,128)(2,1)S(1)} %copy-done.1, ...), custom_call_target="tpu_custom_call" | custom-call | tf_op jit(solution)/shard_map/pallas_call | solution.py:500
  91.2 17.5 %all_to_all.60.got = f32[8,264,128]{2,1,0:T(8,128)S(1)} all-to-all(f32[8,264,128]{2,1,0:T(8,128)S(1)} %get-tuple-element.47), channel_id=1, replica_groups=mesh['z'=8,'y'=8,'head'=8] {'y'}, dimensions={0} | all-to-all | bytes 2162688 | tf_op jit(solution)/shard_map/all_to_all | solution.py:459
  108.8 0.2 shard_map.202
  109.0 15.3 %all_to_all.61.got = f32[8,2,2176]{2,1,0:T(2,128)S(1)} all-to-all(f32[8,2,2176]{2,1,0:T(2,128)S(1)} %get-tuple-element.48), channel_id=1, replica_groups=mesh['z'=8,'y'=8,'head'=8] {'z'}, dimensions={0} | all-to-all | bytes 278528 | tf_op jit(solution)/shard_map/all_to_all | solution.py:459
  124.3 0.1 shard_map.203
  124.4 15.7 %all_to_all.62.late = f32[8,2,1152]{2,1,0:T(2,128)S(1)} all-to-all(f32[8,2,1152]{2,1,0:T(2,128)S(1)} %get-tuple-element.50), channel_id=1, replica_groups=mesh['z'=8,'y'=8,'head'=8] {'z'}, dimensions={0} | all-to-all | bytes 147456 | tf_op jit(solution)/shard_map/all_to_all | solution.py:459
  140.1 0.2 shard_map.204
  140.3 10.3 %all_to_all.63.late = f32[8,136,128]{2,1,0:T(8,128)S(1)} all-to-all(f32[8,136,128]{2,1,0:T(8,128)S(1)} %shard_map.204), channel_id=1, replica_groups=mesh['z'=8,'y'=8,'head'=8] {'y'}, dimensions={0} | all-to-all | bytes 1114112 | tf_op jit(solution)/shard_map/all_to_all | solution.py:459
  150.6 2.6 %shard_map.205 = (bf16[128,1024]{1,0:T(8,128)(2,1)}, f32[8,128]{1,0:T(8,128)}, f32[1,1024]{1,0:T(1,128)}, f32[1,8]{1,0:T(1,128)}, f32[1,8]{1,0:T(1,128)}, /*index=5*/f32[8,32,128]{2,1,0:T(8,128)S(1)}) custom-call(bf16[128,1024]{1,0:T(8,128)(2,1)S(1)} %copy-done.1, bf16[128,128]{1,0:T(8,128)(2,1)S(1)} %copy-done.4, f32[48,128]{1,0:T(8,128)S(1)} %copy-done.6, ...), custom_call_target="tpu_custom_call" | custom-call | tf_op jit(solution)/shard_map/pallas_call | solution.py:517
  153.2 13.9 %all_to_all.64.got = f32[8,32,128]{2,1,0:T(8,128)S(1)} all-to-all(f32[8,32,128]{2,1,0:T(8,128)S(1)} %get-tuple-element.55), channel_id=1, replica_groups=mesh['z'=8,'y'=8,'head'=8] {'head'}, dimensions={0} | all-to-all | bytes 262144 | tf_op jit(solution)/shard_map/all_to_all | solution.py:459
  167.1 8.5 %all_to_all.65.got = f32[8,32,128]{2,1,0:T(8,128)S(1)} all-to-all(f32[8,32,128]{2,1,0:T(8,128)S(1)} %shard_map.206), channel_id=1, replica_groups=mesh['z'=8,'y'=8,'head'=8] {'head'}, dimensions={0} | all-to-all | bytes 262144 | tf_op jit(solution)/shard_map/all_to_all | solution.py:459
  175.6 0.7 shard_map.207
  (21 shorter events, 0.1 us)
Async XLA Ops:
  0.6 44.7 %copy-start.5 = (f32[8,128,128]{2,1,0:T(8,128)S(1)}, f32[8,128,128]{2,1,0:T(8,128)}, u32[]{:S(2)}) copy-start(f32[8,128,128]{2,1,0:T(8,128)} %state_in.1) | copy-start | bytes 1572868
  60.0 10.1 %copy-start.1 = (bf16[128,1024]{1,0:T(8,128)(2,1)S(1)}, bf16[128,1024]{1,0:T(8,128)(2,1)}, u32[]{:S(2)}) copy-start(bf16[128,1024]{1,0:T(8,128)(2,1)} %x.5) | copy-start | bytes 786436
  60.0 10.1 %copy-start.2 = (bf16[1024,1024]{1,0:T(8,128)(2,1)S(1)}, bf16[1024,1024]{1,0:T(8,128)(2,1)}, u32[]{:S(2)}) copy-start(bf16[1024,1024]{1,0:T(8,128)(2,1)} %grad_full.1) | copy-start | bytes 6291460
  60.0 10.1 %copy-start.3 = (bf16[128,1024]{1,0:T(8,128)(2,1)S(1)}, bf16[128,1024]{1,0:T(8,128)(2,1)}, u32[]{:S(2)}) copy-start(bf16[128,1024]{1,0:T(8,128)(2,1)} %z.3) | copy-start | bytes 786436
  60.0 10.1 %copy-start.4 = (bf16[128,128]{1,0:T(8,128)(2,1)S(1)}, bf16[128,128]{1,0:T(8,128)(2,1)}, u32[]{:S(2)}) copy-start(bf16[128,128]{1,0:T(8,128)(2,1)} %b.5) | copy-start | bytes 98308
  60.1 10.2 %copy-start.6 = (f32[48,128]{1,0:T(8,128)S(1)}, f32[48,128]{1,0:T(8,128)}, u32[]{:S(2)}) copy-start(f32[48,128]{1,0:T(8,128)} %get-tuple-element.36.tok) | copy-start | bytes 73732
  60.1 10.2 %copy-start.7 = (bf16[128,128]{1,0:T(8,128)(2,1)S(1)}, bf16[128,128]{1,0:T(8,128)(2,1)}, u32[]{:S(2)}) copy-start(bf16[128,128]{1,0:T(8,128)(2,1)} %c.3) | copy-start | bytes 98308
  60.1 10.2 %copy-start.8 = (f32[1024]{0:T(1024)S(1)}, f32[1024]{0:T(1024)}, u32[]{:S(2)}) copy-start(f32[1024]{0:T(1024)} %param.24) | copy-start | bytes 12292
  60.1 10.1 %copy-start.9 = (s32[8,16]{1,0:T(8,128)S(1)}, s32[8,16]{1,0:T(8,128)}, u32[]{:S(2)}) copy-start(s32[8,16]{1,0:T(8,128)} %keep.1) | copy-start | bytes 1540
  70.2 16.9 %copy-start = (f32[8,136,128]{2,1,0:T(8,128)S(1)}, f32[8,136,128]{2,1,0:T(8,128)}, u32[]{:S(2)}) copy-start(f32[8,136,128]{2,1,0:T(8,128)} %get-tuple-element.37.own) | copy-start | bytes 1671172
  70.3 16.9 %copy-start.10 = (f32[128]{0:T(128)S(1)}, f32[128]{0:T(128)}, u32[]{:S(2)}) copy-start(f32[128]{0:T(128)} %param.15) | copy-start | bytes 1540

commit v7 on v6

--- a/solution.py
+++ b/solution.py
@@ -13,6 +13,7 @@
 GROUP = 8
 CHUNK = 128
 HP = 1
+PAIR = 2
 SUB = 2
 PC = 128
 NS = 128
@@ -121,11 +122,37 @@
 
 
 def whole_sums(a):
-    return head_sums(jnp.sum(a, axis=0, keepdims=True))
+    return pair_sums(jnp.sum(a, axis=0, keepdims=True))
 
 
 def halved(a, b):
     return jnp.where(iota((1, WIDE), 1) % PC < PC // 2, a, b)
+
+
+def pairs_of(values):
+    return [jnp.concatenate([over(values[r : r + 1]), over(values[r + 1 : r + 2])], axis=1) for r in range(0, HD, PAIR)]
+
+
+def both_cols(cols, q, at=0):
+    c = at + q * PAIR
+    return jnp.concatenate([over(cols[:, c : c + 1], CHUNK), over(cols[:, c + 1 : c + 2], CHUNK)], axis=1)
+
+
+def both(ref, q, lo, hi):
+    return jnp.concatenate([ref[q * PAIR, lo:hi, :], ref[q * PAIR + 1, lo:hi, :]], axis=1)
+
+
+def put(ref, q, lo, hi, value):
+    for h in range(PAIR):
+        ref[q * PAIR + h, lo:hi, :] = value[:, h * PC : (h + 1) * PC]
+
+
+def pair_sums(a):
+    return [jnp.sum(a[:, h * PC : (h + 1) * PC], axis=1, keepdims=True) for h in range(PAIR)]
+
+
+def two_lanes(q):
+    return slice(q * PAIR * WIDE, (q + 1) * PAIR * WIDE)
 
 
 def lanes(q):
@@ -252,23 +279,23 @@
     logs, step = table(tok, T_LOGS), table(tok, T_STEP)
     cols = columns(logs, jnp.exp(logs))
     lower = iota((CHUNK, CHUNK), 0) >= iota((CHUNK, CHUNK), 1)
-    d = lanes_of(last(table(tok, T_SKIP)))
+    d = pairs_of(last(table(tok, T_SKIP)))
     scores = mm(c[...], b[...], NT)
     squares = jnp.zeros((CHUNK, 1), F32)
     crosses = jnp.zeros((CHUNK, 1), F32)
-    for q in range(GROUP):
+    for q in range(HD // PAIR):
         inner = []
-        for h in range(HP):
-            r = q * HP + h
+        for h in range(PAIR):
+            r = q * PAIR + h
             mixed = decays(logs, cols, r, lower) * scores * step[r : r + 1]
             inner.append(mm_left(mixed, x[:, r * PC : (r + 1) * PC]))
-        carried = mm_right(c[...], enter[q]) * head_cols(cols, q, HD)
-        y = jnp.concatenate(inner, axis=1) + carried + d[q] * x[:, lanes(q)].astype(F32)
-        y_out[:, lanes(q)] = y
-        zq = z[:, lanes(q)].astype(F32)
+        carried = mm_right(c[...], both(enter, q, 0, NS)) * both_cols(cols, q, HD)
+        y = jnp.concatenate(inner, axis=1) + carried + d[q] * x[:, two_lanes(q)].astype(F32)
+        y_out[:, two_lanes(q)] = y
+        zq = z[:, two_lanes(q)].astype(F32)
         gated = y * zq * sigmoid(zq)
         squares = squares + jnp.sum(gated * gated, axis=1, keepdims=True)
-        crosses = crosses + jnp.sum(up[:, lanes(q)] * gated * gain[:, lanes(q)], axis=1, keepdims=True)
+        crosses = crosses + jnp.sum(up[:, two_lanes(q)] * gated * gain[:, two_lanes(q)], axis=1, keepdims=True)
     stats[...] = jnp.broadcast_to(rows_of([squares, crosses])[None], stats.shape)
 
 
@@ -292,32 +319,32 @@
     at_a = 4 * HD
     lower = iota((CHUNK, CHUNK), 0) >= iota((CHUNK, CHUNK), 1)
     upper = iota((CHUNK, CHUNK), 0) <= iota((CHUNK, CHUNK), 1)
-    d = lanes_of(last(table(tok, T_SKIP)))
-    decay = lanes_of(jnp.exp(total))
-    near = lanes_of(total)
+    d = pairs_of(last(table(tok, T_SKIP)))
+    decay = pairs_of(jnp.exp(total))
+    near = pairs_of(total)
     scores_t = mm(b[...], c[...], NT)
     b_t = b[...].astype(F32).T.astype(BF16)
     c_t = c[...].astype(F32).T.astype(BF16)
     dscores = jnp.zeros((CHUNK, CHUNK), F32)
     dc = jnp.zeros((CHUNK, NS), F32)
     dots, xv, shared, skips = [], [], [], []
-    for q in range(GROUP):
-        xb = x[:, lanes(q)]
-        xq, zq, u, y = xb.astype(F32), z[:, lanes(q)].astype(F32), up[:, lanes(q)], y_in[:, lanes(q)]
+    for q in range(HD // PAIR):
+        xb = x[:, two_lanes(q)]
+        xq, zq, u, y = xb.astype(F32), z[:, two_lanes(q)].astype(F32), up[:, two_lanes(q)], y_in[:, two_lanes(q)]
         sig = sigmoid(zq)
         gate = zq * sig
         gated = y * gate
         scaled = cols[:, at_a : at_a + 1] * u
-        gg = scaled * gain[:, lanes(q)] - gated * cols[:, at_a + 1 : at_a + 2]
-        gz[:, lanes(q)] = (gg * y * sig * (1.0 + zq * (1.0 - sig))).astype(BF16)
+        gg = scaled * gain[:, two_lanes(q)] - gated * cols[:, at_a + 1 : at_a + 2]
+        gz[:, two_lanes(q)] = (gg * y * sig * (1.0 + zq * (1.0 - sig))).astype(BF16)
         gy = gg * gate
         shared.append(jnp.sum(scaled * gated, axis=0, keepdims=True))
         skips += whole_sums(gy * xq)
-        dots += head_sums(gy * (y - d[q] * xq))
+        dots += pair_sums(gy * (y - d[q] * xq))
         gh, gl = split(gy)
         inner = []
-        for h in range(HP):
-            r = q * HP + h
+        for h in range(PAIR):
+            r = q * PAIR + h
             sl = slice(h * PC, (h + 1) * PC)
             dmixed = mm(stack([gh[:, sl], gl[:, sl]], 1), stack([xb[:, sl], xb[:, sl]], 1), NT)
             dscores = dscores + decays(logs, cols, r, lower) * dmixed * step[r : r + 1]
@@ -325,13 +352,13 @@
             mixed_t = jnp.where(upper, jnp.exp(jnp.where(upper, diff, 0.0)), 0.0) * scores_t
             inner.append(mm_halves(split(mixed_t), (gh[:, sl], gl[:, sl])))
         v = jnp.concatenate(inner, axis=1)
-        gx_out[:, lanes(q)] = head_cols(cols, q, 2 * HD) * v + d[q] * gy
-        xv += head_sums(xq * v)
-        eg = head_cols(cols, q, HD) * gy
-        dc = dc + mm_both(eg, enter[q], NT)
-        send[q, :NS, :] = mm_right(c_t, eg)
-        leaving = decay[q] * enter[q] + own[q, :NS, :]
-        send[q, NS : 2 * NS, :] = near[q] * leaving - mm_right(b_t, xq * head_cols(cols, q, 3 * HD))
+        gx_out[:, two_lanes(q)] = both_cols(cols, q, 2 * HD) * v + d[q] * gy
+        xv += pair_sums(xq * v)
+        eg = both_cols(cols, q, HD) * gy
+        dc = dc + mm_both(eg, both(enter, q, 0, NS), NT)
+        put(send, q, 0, NS, mm_right(c_t, eg))
+        leaving = decay[q] * both(enter, q, 0, NS) + both(own, q, 0, NS)
+        put(send, q, NS, 2 * NS, near[q] * leaving - mm_right(b_t, xq * both_cols(cols, q, 3 * HD)))
     maps[0] = mm_left(dscores.T, c[...])
     maps[1] = dc + mm_left(dscores, b[...])
     xv = rows_of(xv)
@@ -340,9 +367,10 @@
     small[:HD] = dla
     small[HD:] = xv
     alogs = jnp.sum(dla * la, axis=1, keepdims=True)
-    for q in range(GROUP):
-        row = halved(over(skips[q]), over(alogs[q : q + 1]))
-        send[q, 2 * NS :, :] = jnp.concatenate([shared[q], row, jnp.zeros((6, WIDE), F32)], axis=0)
+    for r in range(HD):
+        gain_row = shared[r // PAIR][:, r % PAIR * PC : (r % PAIR + 1) * PC]
+        row = halved(over(skips[r]), over(alogs[r : r + 1]))
+        send[r, 2 * NS :, :] = jnp.concatenate([gain_row, row, jnp.zeros((6, WIDE), F32)], axis=0)
 
 
 def group_back_body(got, own, back, send):
@@ -392,28 +420,28 @@
     logs = table(tok, T_LOGS)
     total = last(logs)
     cols = columns(jnp.exp(total - logs), step)
-    decay = lanes_of(jnp.exp(total))
+    decay = pairs_of(jnp.exp(total))
     db = maps[0]
     ends, xv = [], []
     lane = iota((1, HD), 1)
     a = jnp.zeros((1, HD), F32)
     s = jnp.zeros((1, HD), F32)
-    for q in range(GROUP):
-        grad = late[q, :NS, :]
-        xq = x[:, lanes(q)].astype(F32)
-        tail = head_cols(cols, q)
-        stepc = head_cols(cols, q, HD)
+    for q in range(HD // PAIR):
+        grad = both(late, q, 0, NS)
+        xq = x[:, two_lanes(q)].astype(F32)
+        tail = both_cols(cols, q)
+        stepc = both_cols(cols, q, HD)
         v = tail * mm_right(b[...], grad)
-        gx[:, lanes(q)] = (gx_in[:, lanes(q)] + stepc * v).astype(BF16)
+        gx[:, two_lanes(q)] = (gx_in[:, two_lanes(q)] + stepc * v).astype(BF16)
         db = db + mm_both(tail * stepc * xq, grad, NT)
-        xv += head_sums(xq * v)
-        leaving = decay[q] * enter[q] + own[q, :NS, :]
+        xv += pair_sums(xq * v)
+        leaving = decay[q] * both(enter, q, 0, NS) + both(own, q, 0, NS)
         ends += whole_sums(grad * leaving)
-        gain[:, lanes(q)] = late[q, NS : NS + 1, :]
-        for h in range(HP):
-            here = lane == q * HP + h
-            s = jnp.where(here, late[q, NS + 1 : NS + 2, h * PC : h * PC + 1], s)
-            a = jnp.where(here, late[q, NS + 2 : NS + 3, h * PC : h * PC + 1], a)
+        gain[:, two_lanes(q)] = both(late, q, NS, NS + 1)
+        for h in range(PAIR):
+            r = q * PAIR + h
+            s = jnp.where(lane == r, late[r, NS + 1 : NS + 2, :1], s)
+            a = jnp.where(lane == r, late[r, NS + 2 : NS + 3, :1], a)
     alog[...] = a
     skip[...] = s
     xv = rows_of(xv)

time: 177 us -> 175 us (0.989)
  no operation moved by 1% of the time
where the time goes in v7:
time: 175 us
  blocking collectives  163 us (93%)
  Pallas kernels  10.9 us (6%)
    all_to_all x11, blocking collectives, swap(): return lax.all_to_all(a, axis, 0, 0, tiled=True)  163 us

profile of v7, /device:TPU:1, one launch (start us, length us, event | category | flops | bytes accessed | tf_op | source)
XLA Modules:
  0.0 174.6 jit_solution(6315289359506963499)
XLA Ops:
  0.7 2.8 %shard_map.196 = (f32[8,136,128]{2,1,0:T(8,128)}, f32[48,128]{1,0:T(8,128)}) custom-call(bf16[128,1024]{1,0:T(8,128)(2,1)} %x.5, bf16[128,128]{1,0:T(8,128)(2,1)} %b.5, f32[8,128]{1,0:T(8,128)} %bitcast.11, f32[8]{0:T(128)} %bias_hbm.1, f32[8]{0:T(128)} %alog_hbm.1, f32[8]{0:T(128)} %skip_hbm.1), custom_call_target="tpu_custom_call" | custom-call | tf_op jit(solution)/shard_map/pallas_call | solution.py:508
  3.5 14.3 %all_to_all.55.got.own = f32[8,136,128]{2,1,0:T(8,128)S(1)} all-to-all(f32[8,136,128]{2,1,0:T(8,128)} %get-tuple-element.37.own), channel_id=1, replica_groups=mesh['z'=8,'y'=8,'head'=8] {'y'}, dimensions={0} | all-to-all | bytes 1114112 | tf_op jit(solution)/shard_map/all_to_all | solution.py:487
  17.8 0.1 shard_map.197
  17.8 27.5 %all_to_all.56.got = f32[8,2,1152]{2,1,0:T(2,128)S(1)} all-to-all(f32[8,2,1152]{2,1,0:T(2,128)S(1)} %get-tuple-element.38), channel_id=1, replica_groups=mesh['z'=8,'y'=8,'head'=8] {'z'}, dimensions={0} | all-to-all | bytes 147456 | tf_op jit(solution)/shard_map/all_to_all | solution.py:487
  45.3 0.1 shard_map.198
  45.5 14.6 %all_to_all.57.got = f32[8,2,1024]{2,1,0:T(2,128)S(1)} all-to-all(f32[8,2,1024]{2,1,0:T(2,128)S(1)} %get-tuple-element.39), channel_id=1, replica_groups=mesh['z'=8,'y'=8,'head'=8] {'z'}, dimensions={0} | all-to-all | bytes 131072 | tf_op jit(solution)/shard_map/all_to_all | solution.py:487
  60.1 0.0 copy-start.7
  60.1 0.0 copy-start.8
  60.1 0.1 shard_map.199
  60.2 10.0 %all_to_all.58.enter = f32[8,128,128]{2,1,0:T(8,128)S(1)} all-to-all(f32[8,128,128]{2,1,0:T(8,128)S(1)} %shard_map.199), channel_id=1, replica_groups=mesh['z'=8,'y'=8,'head'=8] {'y'}, dimensions={0} | all-to-all | bytes 1048576 | tf_op jit(solution)/shard_map/all_to_all | solution.py:487
  70.3 1.6 shard_map.200
  71.9 15.2 %all_to_all.59.stats = f32[8,2,128]{2,1,0:T(2,128)S(1)} all-to-all(f32[8,2,128]{2,1,0:T(2,128)S(1)} %get-tuple-element.41), channel_id=1, replica_groups=mesh['z'=8,'y'=8,'head'=8] {'head'}, dimensions={0} | all-to-all | bytes 16384 | tf_op jit(solution)/shard_map/all_to_all | solution.py:487
  87.1 3.3 %shard_map.201 = (bf16[128,1024]{1,0:T(8,128)(2,1)}, f32[128,1024]{1,0:T(8,128)S(1)}, f32[8,264,128]{2,1,0:T(8,128)S(1)}, f32[16,128]{1,0:T(8,128)S(1)}, f32[2,128,128]{2,1,0:T(8,128)S(1)}, /*index=5*/f32[1,128]{1,0:T(1,128)}) custom-call(f32[8,2,128]{2,1,0:T(2,128)S(1)} %all_to_all.59.stats, bf16[128,1024]{1,0:T(8,128)(2,1)S(1)} %copy-done.1, ...), custom_call_target="tpu_custom_call" | custom-call | tf_op jit(solution)/shard_map/pallas_call | solution.py:528
  90.3 17.5 %all_to_all.60.got = f32[8,264,128]{2,1,0:T(8,128)S(1)} all-to-all(f32[8,264,128]{2,1,0:T(8,128)S(1)} %get-tuple-element.47), channel_id=1, replica_groups=mesh['z'=8,'y'=8,'head'=8] {'y'}, dimensions={0} | all-to-all | bytes 2162688 | tf_op jit(solution)/shard_map/all_to_all | solution.py:487
  107.9 0.2 shard_map.202
  108.1 15.3 %all_to_all.61.got = f32[8,2,2176]{2,1,0:T(2,128)S(1)} all-to-all(f32[8,2,2176]{2,1,0:T(2,128)S(1)} %get-tuple-element.48), channel_id=1, replica_groups=mesh['z'=8,'y'=8,'head'=8] {'z'}, dimensions={0} | all-to-all | bytes 278528 | tf_op jit(solution)/shard_map/all_to_all | solution.py:487
  123.5 0.1 shard_map.203
  123.5 15.7 %all_to_all.62.late = f32[8,2,1152]{2,1,0:T(2,128)S(1)} all-to-all(f32[8,2,1152]{2,1,0:T(2,128)S(1)} %get-tuple-element.50), channel_id=1, replica_groups=mesh['z'=8,'y'=8,'head'=8] {'z'}, dimensions={0} | all-to-all | bytes 147456 | tf_op jit(solution)/shard_map/all_to_all | solution.py:487
  139.2 0.2 shard_map.204
  139.4 10.3 %all_to_all.63.late = f32[8,136,128]{2,1,0:T(8,128)S(1)} all-to-all(f32[8,136,128]{2,1,0:T(8,128)S(1)} %shard_map.204), channel_id=1, replica_groups=mesh['z'=8,'y'=8,'head'=8] {'y'}, dimensions={0} | all-to-all | bytes 1114112 | tf_op jit(solution)/shard_map/all_to_all | solution.py:487
  149.7 1.8 %shard_map.205 = (bf16[128,1024]{1,0:T(8,128)(2,1)}, f32[8,128]{1,0:T(8,128)}, f32[1,1024]{1,0:T(1,128)}, f32[1,8]{1,0:T(1,128)}, f32[1,8]{1,0:T(1,128)}, /*index=5*/f32[8,32,128]{2,1,0:T(8,128)S(1)}) custom-call(bf16[128,1024]{1,0:T(8,128)(2,1)S(1)} %copy-done.1, bf16[128,128]{1,0:T(8,128)(2,1)S(1)} %copy-done.4, f32[48,128]{1,0:T(8,128)S(1)} %copy-done.6, ...), custom_call_target="tpu_custom_call" | custom-call | tf_op jit(solution)/shard_map/pallas_call | solution.py:545
  151.5 13.9 %all_to_all.64.got = f32[8,32,128]{2,1,0:T(8,128)S(1)} all-to-all(f32[8,32,128]{2,1,0:T(8,128)S(1)} %get-tuple-element.55), channel_id=1, replica_groups=mesh['z'=8,'y'=8,'head'=8] {'head'}, dimensions={0} | all-to-all | bytes 262144 | tf_op jit(solution)/shard_map/all_to_all | solution.py:487
  165.4 8.5 %all_to_all.65.got = f32[8,32,128]{2,1,0:T(8,128)S(1)} all-to-all(f32[8,32,128]{2,1,0:T(8,128)S(1)} %shard_map.206), channel_id=1, replica_groups=mesh['z'=8,'y'=8,'head'=8] {'head'}, dimensions={0} | all-to-all | bytes 262144 | tf_op jit(solution)/shard_map/all_to_all | solution.py:487
  174.0 0.7 shard_map.207
  (21 shorter events, 0.1 us)
Async XLA Ops:
  0.6 44.7 %copy-start.5 = (f32[8,128,128]{2,1,0:T(8,128)S(1)}, f32[8,128,128]{2,1,0:T(8,128)}, u32[]{:S(2)}) copy-start(f32[8,128,128]{2,1,0:T(8,128)} %state_in.1) | copy-start | bytes 1572868
  60.0 10.1 %copy-start.1 = (bf16[128,1024]{1,0:T(8,128)(2,1)S(1)}, bf16[128,1024]{1,0:T(8,128)(2,1)}, u32[]{:S(2)}) copy-start(bf16[128,1024]{1,0:T(8,128)(2,1)} %x.5) | copy-start | bytes 786436
  60.0 10.1 %copy-start.2 = (bf16[1024,1024]{1,0:T(8,128)(2,1)S(1)}, bf16[1024,1024]{1,0:T(8,128)(2,1)}, u32[]{:S(2)}) copy-start(bf16[1024,1024]{1,0:T(8,128)(2,1)} %grad_full.1) | copy-start | bytes 6291460
  60.0 10.1 %copy-start.3 = (bf16[128,1024]{1,0:T(8,128)(2,1)S(1)}, bf16[128,1024]{1,0:T(8,128)(2,1)}, u32[]{:S(2)}) copy-start(bf16[128,1024]{1,0:T(8,128)(2,1)} %z.3) | copy-start | bytes 786436
  60.0 10.1 %copy-start.4 = (bf16[128,128]{1,0:T(8,128)(2,1)S(1)}, bf16[128,128]{1,0:T(8,128)(2,1)}, u32[]{:S(2)}) copy-start(bf16[128,128]{1,0:T(8,128)(2,1)} %b.5) | copy-start | bytes 98308
  60.1 10.2 %copy-start.6 = (f32[48,128]{1,0:T(8,128)S(1)}, f32[48,128]{1,0:T(8,128)}, u32[]{:S(2)}) copy-start(f32[48,128]{1,0:T(8,128)} %get-tuple-element.36.tok) | copy-start | bytes 73732
  60.1 10.2 %copy-start.7 = (bf16[128,128]{1,0:T(8,128)(2,1)S(1)}, bf16[128,128]{1,0:T(8,128)(2,1)}, u32[]{:S(2)}) copy-start(bf16[128,128]{1,0:T(8,128)(2,1)} %c.3) | copy-start | bytes 98308
  60.1 10.2 %copy-start.8 = (f32[1024]{0:T(1024)S(1)}, f32[1024]{0:T(1024)}, u32[]{:S(2)}) copy-start(f32[1024]{0:T(1024)} %param.24) | copy-start | bytes 12292
  60.1 10.1 %copy-start.9 = (s32[8,16]{1,0:T(8,128)S(1)}, s32[8,16]{1,0:T(8,128)}, u32[]{:S(2)}) copy-start(s32[8,16]{1,0:T(8,128)} %keep.1) | copy-start | bytes 1540
  70.2 16.8 %copy-start = (f32[8,136,128]{2,1,0:T(8,128)S(1)}, f32[8,136,128]{2,1,0:T(8,128)}, u32[]{:S(2)}) copy-start(f32[8,136,128]{2,1,0:T(8,128)} %get-tuple-element.37.own) | copy-start | bytes 1671172
  70.3 16.8 %copy-start.10 = (f32[128]{0:T(128)S(1)}, f32[128]{0:T(128)}, u32[]{:S(2)}) copy-start(f32[128]{0:T(128)} %param.15) | copy-start | bytes 1540

commit v8 on v7

--- a/solution.py
+++ b/solution.py
@@ -149,6 +149,12 @@
 
 def pair_sums(a):
     return [jnp.sum(a[:, h * PC : (h + 1) * PC], axis=1, keepdims=True) for h in range(PAIR)]
+
+
+def token_sums(a, q):
+    shape = (HD, 2 * PAIR * PC)
+    ones = (iota(shape, 0) == q * PAIR + iota(shape, 1) // PC % PAIR).astype(BF16)
+    return mm(ones, stack(split(a), 1), NT)
 
 
 def two_lanes(q):
@@ -281,8 +287,8 @@
     lower = iota((CHUNK, CHUNK), 0) >= iota((CHUNK, CHUNK), 1)
     d = pairs_of(last(table(tok, T_SKIP)))
     scores = mm(c[...], b[...], NT)
-    squares = jnp.zeros((CHUNK, 1), F32)
-    crosses = jnp.zeros((CHUNK, 1), F32)
+    squares = jnp.zeros((CHUNK, PC), F32)
+    crosses = jnp.zeros((CHUNK, PC), F32)
     for q in range(HD // PAIR):
         inner = []
         for h in range(PAIR):
@@ -294,8 +300,12 @@
         y_out[:, two_lanes(q)] = y
         zq = z[:, two_lanes(q)].astype(F32)
         gated = y * zq * sigmoid(zq)
-        squares = squares + jnp.sum(gated * gated, axis=1, keepdims=True)
-        crosses = crosses + jnp.sum(up[:, two_lanes(q)] * gated * gain[:, two_lanes(q)], axis=1, keepdims=True)
+        cross = up[:, two_lanes(q)] * gated * gain[:, two_lanes(q)]
+        square = gated * gated
+        squares = squares + (square[:, :PC] + square[:, PC:])
+        crosses = crosses + (cross[:, :PC] + cross[:, PC:])
+    squares = jnp.sum(squares, axis=1, keepdims=True)
+    crosses = jnp.sum(crosses, axis=1, keepdims=True)
     stats[...] = jnp.broadcast_to(rows_of([squares, crosses])[None], stats.shape)
 
 
@@ -327,7 +337,9 @@
     c_t = c[...].astype(F32).T.astype(BF16)
     dscores = jnp.zeros((CHUNK, CHUNK), F32)
     dc = jnp.zeros((CHUNK, NS), F32)
-    dots, xv, shared, skips = [], [], [], []
+    shared, skips = [], []
+    dots = jnp.zeros((HD, CHUNK), F32)
+    xv = jnp.zeros((HD, CHUNK), F32)
     for q in range(HD // PAIR):
         xb = x[:, two_lanes(q)]
         xq, zq, u, y = xb.astype(F32), z[:, two_lanes(q)].astype(F32), up[:, two_lanes(q)], y_in[:, two_lanes(q)]
@@ -340,7 +352,7 @@
         gy = gg * gate
         shared.append(jnp.sum(scaled * gated, axis=0, keepdims=True))
         skips += whole_sums(gy * xq)
-        dots += pair_sums(gy * (y - d[q] * xq))
+        dots = dots + token_sums(gy * (y - d[q] * xq), q)
         gh, gl = split(gy)
         inner = []
         for h in range(PAIR):
@@ -353,7 +365,7 @@
             inner.append(mm_halves(split(mixed_t), (gh[:, sl], gl[:, sl])))
         v = jnp.concatenate(inner, axis=1)
         gx_out[:, two_lanes(q)] = both_cols(cols, q, 2 * HD) * v + d[q] * gy
-        xv += pair_sums(xq * v)
+        xv = xv + token_sums(xq * v, q)
         eg = both_cols(cols, q, HD) * gy
         dc = dc + mm_both(eg, both(enter, q, 0, NS), NT)
         put(send, q, 0, NS, mm_right(c_t, eg))
@@ -361,9 +373,8 @@
         put(send, q, NS, 2 * NS, near[q] * leaving - mm_right(b_t, xq * both_cols(cols, q, 3 * HD)))
     maps[0] = mm_left(dscores.T, c[...])
     maps[1] = dc + mm_left(dscores, b[...])
-    xv = rows_of(xv)
     after = (iota((CHUNK, CHUNK), 0) >= iota((CHUNK, CHUNK), 1)).astype(F32)
-    dla = jnp.dot(rows_of(dots) - step * xv, after, precision=lax.Precision.HIGHEST, preferred_element_type=F32)
+    dla = jnp.dot(dots - step * xv, after, precision=lax.Precision.HIGHEST, preferred_element_type=F32)
     small[:HD] = dla
     small[HD:] = xv
     alogs = jnp.sum(dla * la, axis=1, keepdims=True)
@@ -422,7 +433,8 @@
     cols = columns(jnp.exp(total - logs), step)
     decay = pairs_of(jnp.exp(total))
     db = maps[0]
-    ends, xv = [], []
+    ends = []
+    xv = jnp.zeros((HD, CHUNK), F32)
     lane = iota((1, HD), 1)
     a = jnp.zeros((1, HD), F32)
     s = jnp.zeros((1, HD), F32)
@@ -434,7 +446,7 @@
         v = tail * mm_right(b[...], grad)
         gx[:, two_lanes(q)] = (gx_in[:, two_lanes(q)] + stepc * v).astype(BF16)
         db = db + mm_both(tail * stepc * xq, grad, NT)
-        xv += pair_sums(xq * v)
+        xv = xv + token_sums(xq * v, q)
         leaving = decay[q] * both(enter, q, 0, NS) + both(own, q, 0, NS)
         ends += whole_sums(grad * leaving)
         gain[:, two_lanes(q)] = both(late, q, NS, NS + 1)
@@ -444,7 +456,6 @@
             a = jnp.where(lane == r, late[r, NS + 2 : NS + 3, :1], a)
     alog[...] = a
     skip[...] = s
-    xv = rows_of(xv)
     after = (iota((CHUNK, CHUNK), 0) >= iota((CHUNK, CHUNK), 1)).astype(F32)
     dla = jnp.dot(-step * xv, after, precision=lax.Precision.HIGHEST, preferred_element_type=F32)
     dla = small[:HD] + dla + jnp.concatenate(ends, axis=0)

time: 175 us -> 175 us (level)
  no operation moved by 1% of the time
where the time goes in v8:
time: 175 us; the launch traced here: 174 us
  blocking collectives  163 us (93%)
  Pallas kernels  10.6 us (6%)
    all_to_all x11, blocking collectives, swap(): return lax.all_to_all(a, axis, 0, 0, tiled=True)  163 us

profile of v8, /device:TPU:1, one launch (start us, length us, event | category | flops | bytes accessed | tf_op | source)
XLA Modules:
  0.0 174.3 jit_solution(16050176668349939644)
XLA Ops:
  0.7 2.8 %shard_map.196 = (f32[8,136,128]{2,1,0:T(8,128)}, f32[48,128]{1,0:T(8,128)}) custom-call(bf16[128,1024]{1,0:T(8,128)(2,1)} %x.5, bf16[128,128]{1,0:T(8,128)(2,1)} %b.5, f32[8,128]{1,0:T(8,128)} %bitcast.11, f32[8]{0:T(128)} %bias_hbm.1, f32[8]{0:T(128)} %alog_hbm.1, f32[8]{0:T(128)} %skip_hbm.1), custom_call_target="tpu_custom_call" | custom-call | tf_op jit(solution)/shard_map/pallas_call | solution.py:519
  3.5 14.3 %all_to_all.55.got.own = f32[8,136,128]{2,1,0:T(8,128)S(1)} all-to-all(f32[8,136,128]{2,1,0:T(8,128)} %get-tuple-element.37.own), channel_id=1, replica_groups=mesh['z'=8,'y'=8,'head'=8] {'y'}, dimensions={0} | all-to-all | bytes 1114112 | tf_op jit(solution)/shard_map/all_to_all | solution.py:498
  17.8 0.1 shard_map.197
  17.8 27.5 %all_to_all.56.got = f32[8,2,1152]{2,1,0:T(2,128)S(1)} all-to-all(f32[8,2,1152]{2,1,0:T(2,128)S(1)} %get-tuple-element.38), channel_id=1, replica_groups=mesh['z'=8,'y'=8,'head'=8] {'z'}, dimensions={0} | all-to-all | bytes 147456 | tf_op jit(solution)/shard_map/all_to_all | solution.py:498
  45.3 0.1 shard_map.198
  45.5 14.6 %all_to_all.57.got = f32[8,2,1024]{2,1,0:T(2,128)S(1)} all-to-all(f32[8,2,1024]{2,1,0:T(2,128)S(1)} %get-tuple-element.39), channel_id=1, replica_groups=mesh['z'=8,'y'=8,'head'=8] {'z'}, dimensions={0} | all-to-all | bytes 131072 | tf_op jit(solution)/shard_map/all_to_all | solution.py:498
  60.1 0.0 copy-start.6
  60.1 0.0 copy-start.9
  60.1 0.1 shard_map.199
  60.2 10.0 %all_to_all.58.enter = f32[8,128,128]{2,1,0:T(8,128)S(1)} all-to-all(f32[8,128,128]{2,1,0:T(8,128)S(1)} %shard_map.199), channel_id=1, replica_groups=mesh['z'=8,'y'=8,'head'=8] {'y'}, dimensions={0} | all-to-all | bytes 1048576 | tf_op jit(solution)/shard_map/all_to_all | solution.py:498
  70.3 1.5 shard_map.200
  71.8 15.2 %all_to_all.59.stats = f32[8,2,128]{2,1,0:T(2,128)S(1)} all-to-all(f32[8,2,128]{2,1,0:T(2,128)S(1)} %get-tuple-element.41), channel_id=1, replica_groups=mesh['z'=8,'y'=8,'head'=8] {'head'}, dimensions={0} | all-to-all | bytes 16384 | tf_op jit(solution)/shard_map/all_to_all | solution.py:498
  87.0 3.1 %shard_map.201 = (bf16[128,1024]{1,0:T(8,128)(2,1)}, f32[128,1024]{1,0:T(8,128)S(1)}, f32[8,264,128]{2,1,0:T(8,128)S(1)}, f32[16,128]{1,0:T(8,128)S(1)}, f32[2,128,128]{2,1,0:T(8,128)S(1)}, /*index=5*/f32[1,128]{1,0:T(1,128)}) custom-call(f32[8,2,128]{2,1,0:T(2,128)S(1)} %all_to_all.59.stats, bf16[128,1024]{1,0:T(8,128)(2,1)S(1)} %copy-done.1, ...), custom_call_target="tpu_custom_call" | custom-call | tf_op jit(solution)/shard_map/pallas_call | solution.py:539
  90.0 17.5 %all_to_all.60.got = f32[8,264,128]{2,1,0:T(8,128)S(1)} all-to-all(f32[8,264,128]{2,1,0:T(8,128)S(1)} %get-tuple-element.47), channel_id=1, replica_groups=mesh['z'=8,'y'=8,'head'=8] {'y'}, dimensions={0} | all-to-all | bytes 2162688 | tf_op jit(solution)/shard_map/all_to_all | solution.py:498
  107.6 0.2 shard_map.202
  107.8 15.3 %all_to_all.61.got = f32[8,2,2176]{2,1,0:T(2,128)S(1)} all-to-all(f32[8,2,2176]{2,1,0:T(2,128)S(1)} %get-tuple-element.48), channel_id=1, replica_groups=mesh['z'=8,'y'=8,'head'=8] {'z'}, dimensions={0} | all-to-all | bytes 278528 | tf_op jit(solution)/shard_map/all_to_all | solution.py:498
  123.1 0.1 shard_map.203
  123.2 15.7 %all_to_all.62.late = f32[8,2,1152]{2,1,0:T(2,128)S(1)} all-to-all(f32[8,2,1152]{2,1,0:T(2,128)S(1)} %get-tuple-element.50), channel_id=1, replica_groups=mesh['z'=8,'y'=8,'head'=8] {'z'}, dimensions={0} | all-to-all | bytes 147456 | tf_op jit(solution)/shard_map/all_to_all | solution.py:498
  138.9 0.2 shard_map.204
  139.1 10.3 %all_to_all.63.late = f32[8,136,128]{2,1,0:T(8,128)S(1)} all-to-all(f32[8,136,128]{2,1,0:T(8,128)S(1)} %shard_map.204), channel_id=1, replica_groups=mesh['z'=8,'y'=8,'head'=8] {'y'}, dimensions={0} | all-to-all | bytes 1114112 | tf_op jit(solution)/shard_map/all_to_all | solution.py:498
  149.4 1.8 %shard_map.205 = (bf16[128,1024]{1,0:T(8,128)(2,1)}, f32[8,128]{1,0:T(8,128)}, f32[1,1024]{1,0:T(1,128)}, f32[1,8]{1,0:T(1,128)}, f32[1,8]{1,0:T(1,128)}, /*index=5*/f32[8,32,128]{2,1,0:T(8,128)S(1)}) custom-call(bf16[128,1024]{1,0:T(8,128)(2,1)S(1)} %copy-done.1, bf16[128,128]{1,0:T(8,128)(2,1)S(1)} %copy-done.4, f32[48,128]{1,0:T(8,128)S(1)} %copy-done.6, ...), custom_call_target="tpu_custom_call" | custom-call | tf_op jit(solution)/shard_map/pallas_call | solution.py:556
  151.2 13.9 %all_to_all.64.got = f32[8,32,128]{2,1,0:T(8,128)S(1)} all-to-all(f32[8,32,128]{2,1,0:T(8,128)S(1)} %get-tuple-element.55), channel_id=1, replica_groups=mesh['z'=8,'y'=8,'head'=8] {'head'}, dimensions={0} | all-to-all | bytes 262144 | tf_op jit(solution)/shard_map/all_to_all | solution.py:498
  165.1 8.5 %all_to_all.65.got = f32[8,32,128]{2,1,0:T(8,128)S(1)} all-to-all(f32[8,32,128]{2,1,0:T(8,128)S(1)} %shard_map.206), channel_id=1, replica_groups=mesh['z'=8,'y'=8,'head'=8] {'head'}, dimensions={0} | all-to-all | bytes 262144 | tf_op jit(solution)/shard_map/all_to_all | solution.py:498
  173.6 0.7 shard_map.207
  (21 shorter events, 0.1 us)
Async XLA Ops:
  0.6 44.7 %copy-start.5 = (f32[8,128,128]{2,1,0:T(8,128)S(1)}, f32[8,128,128]{2,1,0:T(8,128)}, u32[]{:S(2)}) copy-start(f32[8,128,128]{2,1,0:T(8,128)} %state_in.1) | copy-start | bytes 1572868
  60.0 10.1 %copy-start.1 = (bf16[128,1024]{1,0:T(8,128)(2,1)S(1)}, bf16[128,1024]{1,0:T(8,128)(2,1)}, u32[]{:S(2)}) copy-start(bf16[128,1024]{1,0:T(8,128)(2,1)} %x.5) | copy-start | bytes 786436
  60.0 10.1 %copy-start.2 = (bf16[1024,1024]{1,0:T(8,128)(2,1)S(1)}, bf16[1024,1024]{1,0:T(8,128)(2,1)}, u32[]{:S(2)}) copy-start(bf16[1024,1024]{1,0:T(8,128)(2,1)} %grad_full.1) | copy-start | bytes 6291460
  60.0 10.1 %copy-start.3 = (bf16[128,1024]{1,0:T(8,128)(2,1)S(1)}, bf16[128,1024]{1,0:T(8,128)(2,1)}, u32[]{:S(2)}) copy-start(bf16[128,1024]{1,0:T(8,128)(2,1)} %z.3) | copy-start | bytes 786436
  60.0 10.1 %copy-start.4 = (bf16[128,128]{1,0:T(8,128)(2,1)S(1)}, bf16[128,128]{1,0:T(8,128)(2,1)}, u32[]{:S(2)}) copy-start(bf16[128,128]{1,0:T(8,128)(2,1)} %b.5) | copy-start | bytes 98308
  60.1 10.2 %copy-start.6 = (f32[48,128]{1,0:T(8,128)S(1)}, f32[48,128]{1,0:T(8,128)}, u32[]{:S(2)}) copy-start(f32[48,128]{1,0:T(8,128)} %get-tuple-element.36.tok) | copy-start | bytes 73732
  60.1 10.2 %copy-start.7 = (bf16[128,128]{1,0:T(8,128)(2,1)S(1)}, bf16[128,128]{1,0:T(8,128)(2,1)}, u32[]{:S(2)}) copy-start(bf16[128,128]{1,0:T(8,128)(2,1)} %c.3) | copy-start | bytes 98308
  60.1 10.2 %copy-start.8 = (f32[1024]{0:T(1024)S(1)}, f32[1024]{0:T(1024)}, u32[]{:S(2)}) copy-start(f32[1024]{0:T(1024)} %param.24) | copy-start | bytes 12292
  60.1 10.1 %copy-start.9 = (s32[8,16]{1,0:T(8,128)S(1)}, s32[8,16]{1,0:T(8,128)}, u32[]{:S(2)}) copy-start(s32[8,16]{1,0:T(8,128)} %keep.1) | copy-start | bytes 1540
  70.2 16.7 %copy-start = (f32[8,136,128]{2,1,0:T(8,128)S(1)}, f32[8,136,128]{2,1,0:T(8,128)}, u32[]{:S(2)}) copy-start(f32[8,136,128]{2,1,0:T(8,128)} %get-tuple-element.37.own) | copy-start | bytes 1671172
  70.3 16.7 %copy-start.10 = (f32[128]{0:T(128)S(1)}, f32[128]{0:T(128)}, u32[]{:S(2)}) copy-start(f32[128]{0:T(128)} %param.15) | copy-start | bytes 1540
